TPU v7x, 32 devices: a whole 2x2x4 slice. The times are simulated.
32 devices in a mesh: row: 4 (over y, x), col: 8 (over z, core).
Axes of the slice: x: 2, y: 2, z: 4, core: 2. Of those that a mesh axis runs over, the one named last changes fastest.
Arguments:
- features: bfloat16 [16384, 128], P(('col', 'row')), may hold values from -6 to 6
- weight: bfloat16 [128, 256], replicated, may hold values from -0.5 to 0.5
- out_grad: bfloat16 [16384, 256], P(('row', 'col')), may hold values from -0.796875 to 0.796875
- tile_index: int32 [4, 8, 64, 3], P('row', 'col'), may hold values from 0 to 31, as said below
- edge_mask: int32 [4, 8, 64, 128, 128], P('row', 'col'), may hold values 0 or 1
- edge_weight: bfloat16 [4, 8, 64, 128, 128], P('row', 'col'), may hold values from 0 to 1
Outputs:
- edge_grad: bfloat16 [4, 8, 64, 128, 128], P('row', 'col')
- feature_grad: bfloat16 [16384, 128], P(('col', 'row'))
Inputs may be any that keep to these rules, and one draw needn't show every extreme that they name: `tile_index`: within one device the (tile row, tile column) pairs are distinct; tile rows lie below 32, tile columns below 16; live slots come first, a device has between 21 and 64 of them, and some device has all 64 live.
All inputs are finite; a program needn't handle non-finite values. No bound on the sum of `edge_mask` on one device may be relied on, other than what follows from the above.
Results may differ from a plain program's by a relative error of at most 0.0049.
Values may be sent and summed in bfloat16 or wider, within the bound.
No kernel may reach another device: no remote copies, remote signals or barrier semaphores. Data moves between devices by JAX's collectives and lax.ppermute only.
A program may use at most 64 MiB of HBM per device.

v0:
```python
import jax
import jax.numpy as jnp
from jax import lax
from jax.sharding import PartitionSpec as P

BLOCK = 128


def local(features, weight, out_grad, tile_index, edge_mask, edge_weight):
    hidden = weight.shape[1]
    grad_rows = lax.all_gather(out_grad, "col", axis=0, tiled=True)
    proj = jnp.dot(features, weight, preferred_element_type=jnp.float32).astype(jnp.bfloat16)
    proj_cols = lax.all_gather(proj, "row", axis=0, tiled=True)
    table = tile_index[0, 0]
    tile_rows = table[:, 0]
    tile_cols = table[:, 1]
    live = table[:, 2].astype(jnp.float32)
    col_blocks = proj_cols.shape[0] // BLOCK
    grad_tiles = jnp.take(grad_rows.reshape(-1, BLOCK, hidden), tile_rows, axis=0)
    proj_tiles = jnp.take(proj_cols.reshape(col_blocks, BLOCK, hidden), tile_cols, axis=0)
    keep = edge_mask[0, 0].astype(jnp.float32) * live[:, None, None]
    scores = jnp.einsum("tif,tjf->tij", grad_tiles, proj_tiles, preferred_element_type=jnp.float32)
    edge_grad = (keep * scores).astype(jnp.bfloat16)[None, None]
    adjacency = (edge_weight[0, 0].astype(jnp.float32) * keep).astype(jnp.bfloat16)
    contrib = jnp.einsum("tij,tif->tjf", adjacency, grad_tiles, preferred_element_type=jnp.float32)
    selector = (tile_cols[:, None] == jnp.arange(col_blocks, dtype=jnp.int32)[None, :]).astype(
        jnp.float32
    )
    partial_grad = jnp.einsum(
        "tc,tjf->cjf", selector, contrib, precision=lax.Precision.HIGHEST
    ).reshape(col_blocks * BLOCK, hidden)
    wide_weight = weight.astype(jnp.float32)
    proj_grad = lax.psum_scatter(partial_grad, "row", scatter_dimension=0, tiled=True)
    feature_grad = jnp.dot(proj_grad, wide_weight.T, precision=lax.Precision.HIGHEST)
    return (edge_grad, feature_grad.astype(jnp.bfloat16))


def solution(mesh):
    in_specs = (
        P(("col", "row"), None),
        P(),
        P(("row", "col"), None),
        P("row", "col", None, None),
        P("row", "col", None, None, None),
        P("row", "col", None, None, None),
    )
    out_specs = (P("row", "col", None, None, None), P(("col", "row"), None))
    return jax.shard_map(local, mesh=mesh, in_specs=in_specs, out_specs=out_specs, check_vma=False)
```

profile of v0, /device:TPU:0, one launch (start us, length us, event | category | flops | bytes accessed | tf_op | source)
XLA Modules:
  0.0 116.8 jit_solution(1486145231938284226)
XLA Ops:
  7.2 0.0 copy-start
  7.2 0.0 all-gather.3.cloned.1.call-start
  7.2 0.7 all-gather.3.cloned.1.call-update
  7.9 0.0 all-gather.5.cloned.1.call-start
  8.0 0.1 copy-done
  8.1 1.8 %convolution_convert_fusion = bf16[512,256]{1,0:T(8,128)(2,1)} fusion(bf16[512,128]{1,0:T(8,128)(2,1)S(1)} %copy-done, bf16[128,256]{1,0:T(8,128)(2,1)} %param.7), kind=kOutput, calls=%fused_computation.17 | convolution fusion | flops 33685504 | bytes 458752 | tf_op jit(solution)/shard_map/dot_general | solution.py:12
  9.8 0.0 all-gather.5.cloned.1.call-update
  9.9 0.0 reduce-scatter.2.cloned.1.call-start
  9.9 0.7 copy.14
  10.6 30.8 %all-gather.3.cloned.1.call-done = bf16[4096,256]{1,0:T(8,128)(2,1)} async-done(((bf16[512,256]{1,0:T(8,128)(2,1)}), bf16[4096,256]{1,0:T(8,128)(2,1)}) %all-gather.3.cloned.1.call-update) | async-done | bytes 2097168 | tf_op jit(solution)/shard_map/all_gather | solution.py:11
  41.4 0.0 copy-start.1
  41.4 4.5 %gather_fusion = bf16[64,128,256]{2,1,0:T(8,128)(2,1)} fusion(bf16[32,128,256]{2,1,0:T(8,128)(2,1)} %bitcast.43, s32[1024]{0:T(1024)S(1)} %get-tuple-element.9), kind=kCustom, calls=%fused_computation | custom fusion | bytes 8388864 | tf_op jit(solution)/shard_map/jit(_take)/gather | solution.py:19
  46.0 0.0 copy-done.1
  46.0 5.1 %fusion.7 = f32[64,128,256]{2,1,0:T(8,128)S(1)} fusion(s32[1,1,64,128,128]{4,3,2,1,0:T(8,128)} %param.10, bf16[1,1,64,128,128]{4,3,2,1,0:T(8,128)(2,1)S(1)} %copy-done.1, f32[64]{0:T(128)S(1)} %get-tuple-element.5, bf16[64,128,256]{2,1,0:T(8,128)(2,1)} %gather_fusion, pred[64]{0:T(512)(128)(4,1)S(1)} %get-tuple-element.6), kind=kOutput, calls=%fused_computation.13 | convolution fusion | flops 544210944 | bytes 18874688 | tf_op jit(solution)/shard_map/tij,tif->tjf/dot_general | solution.py:25
  51.1 7.5 %fusion = f32[16,128,256]{2,0,1:T(8,128)S(1)} fusion(f32[64,128,256]{2,1,0:T(8,128)S(1)} %fusion.7, s32[64]{0:T(128)S(1)} %get-tuple-element.2), kind=kOutput, calls=%fused_computation.2 | convolution fusion | flops 402654208 | bytes 10486016 | tf_op jit(solution)/shard_map/tc,tjf->cjf/dot_general | solution.py:29
  58.6 2.6 %copy.8 = f32[16,128,256]{2,1,0:T(8,128)} copy(f32[16,128,256]{2,0,1:T(8,128)S(1)} %fusion) | data formatting | bytes 4194304 | tf_op jit(solution)/shard_map/tc,tjf->cjf/dot_general | solution.py:29
  61.2 0.0 reduce-scatter.2.cloned.1.call-update
  61.2 8.8 %all-gather.5.cloned.1.call-done = bf16[2048,256]{1,0:T(8,128)(2,1)} async-done(((bf16[512,256]{1,0:T(8,128)(2,1)}), bf16[2048,256]{1,0:T(8,128)(2,1)}) %all-gather.5.cloned.1.call-update) | async-done | bytes 1048592 | tf_op jit(solution)/shard_map/all_gather | solution.py:13
  70.0 4.0 %gather_fusion.1 = bf16[64,128,256]{2,1,0:T(8,128)(2,1)} fusion(bf16[16,128,256]{2,1,0:T(8,128)(2,1)} %bitcast.42, s32[1024]{0:T(1024)S(1)} %get-tuple-element.8), kind=kCustom, calls=%fused_computation.1 | custom fusion | bytes 8388864 | tf_op jit(solution)/shard_map/jit(_take)/gather | solution.py:20
  74.0 0.0 copy-start.2
  74.0 7.5 %fusion.6 = bf16[1,1,64,128,128]{4,3,2,1,0:T(8,128)(2,1)} fusion(s32[1,1,64,128,128]{4,3,2,1,0:T(8,128)} %param.10, f32[64]{0:T(128)S(1)} %get-tuple-element.5, bf16[64,128,256]{2,1,0:T(8,128)(2,1)} %gather_fusion.1, pred[64]{0:T(512)(128)(4,1)S(1)} %get-tuple-element.7, bf16[64,128,256]{2,1,0:T(8,128)(2,1)} %gather_fusion, ...), kind=kOutput, calls=%fused_computation.12 | convolution fusion | flops 545259520 | bytes 14680448 | tf_op jit(solution)/shard_map/tif,tjf->tij/dot_general | solution.py:22
  81.5 26.7 %reduce-scatter.2.cloned.1.call-done = f32[512,256]{1,0:T(8,128)} async-done(((f32[2048,256]{1,0:T(8,128)}), f32[512,256]{1,0:T(8,128)}) %reduce-scatter.2.cloned.1.call-update) | async-done | bytes 524304 | tf_op jit(solution)/shard_map/reduce_scatter | solution.py:33
  108.2 0.0 copy-done.2
  108.2 2.1 %convolution_convert_fusion.1 = bf16[512,128]{1,0:T(8,128)(2,1)} fusion(f32[512,256]{1,0:T(8,128)} %reduce-scatter.2.cloned.1.call-done, bf16[128,256]{1,0:T(8,128)(2,1)S(1)} %copy-done.2), kind=kOutput, calls=%fused_computation.18 | convolution fusion | flops 201392128 | bytes 720896 | tf_op jit(solution)/shard_map/dot_general | solution.py:34
  (3 shorter events, 0.0 us)
Async XLA Ops:
  7.2 0.9 copy-start
  7.2 34.3 %all-gather.3.cloned.1.call-start = ((), (), s32[]{:S(2)}) async-start(), calls=%async_computation.1 | async-start | bytes 2359296 | tf_op jit(solution)/shard_map/all_gather | solution.py:11
  7.9 62.1 %all-gather.5.cloned.1.call-start = ((), (), s32[]{:S(2)}) async-start(), calls=%async_computation.2 | async-start | bytes 1310720 | tf_op jit(solution)/shard_map/all_gather | solution.py:13
  9.9 98.4 %reduce-scatter.2.cloned.1.call-start = ((), (), s32[]{:S(2)}) async-start(), calls=%async_computation.3 | async-start | bytes 2621440 | tf_op jit(solution)/shard_map/reduce_scatter | solution.py:33
  41.4 4.5 %copy-start.1 = (bf16[1,1,64,128,128]{4,3,2,1,0:T(8,128)(2,1)S(1)}, bf16[1,1,64,128,128]{4,3,2,1,0:T(8,128)(2,1)}, u32[]{:S(2)}) copy-start(bf16[1,1,64,128,128]{4,3,2,1,0:T(8,128)(2,1)} %param.11) | copy-start | bytes 6291460
  74.0 34.2 %copy-start.2 = (bf16[128,256]{1,0:T(8,128)(2,1)S(1)}, bf16[128,256]{1,0:T(8,128)(2,1)}, u32[]{:S(2)}) copy-start(bf16[128,256]{1,0:T(8,128)(2,1)} %param.7) | copy-start | bytes 196612
Sparse Core Ops, SparseCore 0:
  9.6 31.7 all-gather.2
  43.9 26.1 all-gather.4
  73.0 35.1 reduce-scatter.1
where the time goes:
time: 117 us
  waiting for transfers between devices  67 us (57%)
  matrix products  24 us (21%)
  between operations  13.8 us (12%)
  local copies, waits for them, and re-layouts  11.9 us (10%)
    all_gather x1, waiting for transfers between devices, local(): grad_rows = lax.all_gather(out_grad, 'col', axis=0, tiled=True)  30.8 us
    reduce_scatter x1, waiting for transfers between devices, local(): lax.psum_scatter(partial_grad, 'row', scatter_dimension=0, tiled=True)  26.7 us
    all_gather x1, waiting for transfers between devices, local(): proj_cols = lax.all_gather(proj, 'row', axis=0, tiled=True)  8.81 us
    dot_general x1, matrix products, local(): jnp.einsum('tc,tjf->cjf', selector, contrib, precision=lax.Precision.HIGH...  7.52 us
    dot_general x1, matrix products, local(): jnp.einsum('tif,tjf->tij', grad_tiles, proj_tiles, preferred_element_type...  7.51 us
    dot_general x1, matrix products, local(): jnp.einsum('tij,tif->tjf', adjacency, grad_tiles, preferred_element_type=...  5.12 us
    gather x1, local copies, waits for them, and re-layouts, local(): jnp.take(grad_rows.reshape(-1, BLOCK, hidden), tile_rows, axis=0)  4.5 us
    gather x1, local copies, waits for them, and re-layouts, local(): jnp.take(proj_cols.reshape(col_blocks, BLOCK, hidden), tile_cols, axis=0)  4 us
  transfers between devices with their start and end apart: 3, of which 3 were waited for; matrix products, arithmetic and copies ran while one was open for 29% of the time, Pallas kernels for 0%

commit v1 on v0

v1 whole, which is shorter than its diff:
```python
import functools

import jax
import jax.numpy as jnp
from jax import lax
from jax.experimental import pallas as pl
from jax.experimental.pallas import tpu as pltpu
from jax.sharding import PartitionSpec as P

BLOCK = 128
GROUP = 8
VMEM = pltpu.VMEM
SMEM = pltpu.SMEM


def swap(x, axis, size, mask):
    return lax.ppermute(x, axis, [(i, i ^ mask) for i in range(size)])


def prep_kernel(table, mask, weights, keep_out, adj_out):
    step = pl.program_id(0)
    for i in range(GROUP):
        t = step * GROUP + i
        live = table[0, 0, t, 2]
        on = mask[0, 0, i] * live != 0
        adj = jnp.where(on, weights[0, 0, i].astype(jnp.float32), 0.0)
        keep_out[t] = jnp.where(on, 1.0, 0.0).astype(jnp.bfloat16)
        adj_out[t] = adj.T.astype(jnp.bfloat16)


def sums_kernel(n_row, n_col, per, *refs):
    table, adj = refs[:2]
    slots = refs[2 : 2 + n_col]
    panel = refs[2 + n_col]
    outs = refs[3 + n_col : 3 + n_col + n_row]
    total = refs[3 + n_col + n_row]
    me = lax.axis_index("col")
    row = lax.axis_index("row")
    for s in range(n_col):
        for i in range(per):
            panel[s * per + i] = slots[s][i * BLOCK : (i + 1) * BLOCK, :]
    total[...] = jnp.zeros_like(total)

    def group(step, carry):
        found = []
        for i in range(GROUP):
            t = step * GROUP + i
            a = table[0, 0, t, 0]
            place = ((a // per) ^ me) * per + a % per
            found.append(
                jnp.dot(adj[t], panel[place], preferred_element_type=jnp.float32)
            )
        for i in range(GROUP):
            b = table[0, 0, step * GROUP + i, 1]
            total[b] += found[i]
        return carry

    lax.fori_loop(0, adj.shape[0] // GROUP, group, 0)
    for s in range(n_row):
        for i in range(per):
            outs[s][i * BLOCK : (i + 1) * BLOCK, :] = total[(row ^ s) * per + i].astype(outs[s].dtype)


def scores_kernel(n_row, per, *refs):
    table, panel, keep = refs[:3]
    slots = refs[3 : 3 + n_row]
    out = refs[3 + n_row]
    cols = refs[4 + n_row]
    step = pl.program_id(0)
    me = lax.axis_index("col")
    row = lax.axis_index("row")

    @pl.when(step == 0)
    def _():
        for s in range(n_row):
            for i in range(per):
                block = slots[s][i * BLOCK : (i + 1) * BLOCK, :]
                cols[s * per + i] = block.astype(jnp.float32).T.astype(jnp.bfloat16)

    for i in range(GROUP):
        t = step * GROUP + i
        a = table[0, 0, t, 0]
        b = table[0, 0, t, 1]
        left = panel[((a // per) ^ me) * per + a % per]
        right = cols[((b // per) ^ row) * per + b % per]
        found = jnp.dot(left, right, preferred_element_type=jnp.float32)
        out[0, 0, i] = found.astype(jnp.bfloat16) * keep[t]


def local(n_row, n_col, features, weight, out_grad, tile_index, edge_mask, edge_weight):
    tiles = edge_mask.shape[2]
    nodes, fin = features.shape
    per = nodes // BLOCK
    whole = pl.BlockSpec(memory_space=VMEM)
    scalars = pl.BlockSpec(memory_space=SMEM)
    tile_block = pl.BlockSpec((1, 1, GROUP, BLOCK, BLOCK), lambda g: (0, 0, g, 0, 0))
    tile_set = jax.ShapeDtypeStruct((tiles, BLOCK, BLOCK), jnp.bfloat16)

    hidden = lax.dot_general(
        out_grad, weight, (((1,), (1,)), ((), ())), preferred_element_type=jnp.float32
    ).astype(jnp.bfloat16)

    slots = [None] * n_col
    slots[0] = hidden
    for s in range(2, n_col, 2):
        slots[s] = swap(hidden, "col", n_col, s)
    for s in range(0, n_col, 2):
        slots[s + 1] = swap(slots[s], "col", n_col, 1)
    col_slots = [features] + [swap(features, "row", n_row, s) for s in range(1, n_row)]

    keep, adj = pl.pallas_call(
        prep_kernel,
        grid=(tiles // GROUP,),
        in_specs=[scalars, tile_block, tile_block],
        out_specs=[whole, whole],
        out_shape=[tile_set, tile_set],
        cost_estimate=pl.CostEstimate(flops=0, bytes_accessed=edge_mask.size * 6, transcendentals=0),
        name="prep",
    )(tile_index, edge_mask, edge_weight)

    panel_shape = jax.ShapeDtypeStruct((n_col * per, BLOCK, fin), jnp.bfloat16)
    chunk = lambda dtype: jax.ShapeDtypeStruct((nodes, fin), dtype)
    panel, own, *parts = pl.pallas_call(
        functools.partial(sums_kernel, n_row, n_col, per),
        in_specs=[scalars] + [whole] * (1 + n_col),
        out_specs=[whole] * (1 + n_row),
        out_shape=[panel_shape, chunk(jnp.float32)] + [chunk(jnp.bfloat16)] * (n_row - 1),
        scratch_shapes=[VMEM((n_row * per, BLOCK, fin), jnp.float32)],
        cost_estimate=pl.CostEstimate(flops=2 * tiles * BLOCK * BLOCK * fin, bytes_accessed=4 << 20, transcendentals=0),
        name="sums",
    )(tile_index, adj, *slots)

    got = [swap(parts[s - 1], "row", n_row, s) for s in range(1, n_row)]

    edge_grad = pl.pallas_call(
        functools.partial(scores_kernel, n_row, per),
        grid=(tiles // GROUP,),
        in_specs=[scalars] + [whole] * (2 + n_row),
        out_specs=tile_block,
        out_shape=jax.ShapeDtypeStruct(edge_weight.shape, jnp.bfloat16),
        scratch_shapes=[VMEM((n_row * per, fin, BLOCK), jnp.bfloat16)],
        cost_estimate=pl.CostEstimate(flops=2 * tiles * BLOCK * BLOCK * fin, bytes_accessed=8 << 20, transcendentals=0),
        name="scores",
    )(tile_index, panel, keep, *col_slots)

    total = own
    for part in got:
        total = total + part.astype(jnp.float32)
    return edge_grad, total.astype(jnp.bfloat16)


def solution(mesh):
    in_specs = (
        P(("col", "row"), None),
        P(),
        P(("row", "col"), None),
        P("row", "col", None, None),
        P("row", "col", None, None, None),
        P("row", "col", None, None, None),
    )
    out_specs = (P("row", "col", None, None, None), P(("col", "row"), None))
    step = functools.partial(local, mesh.shape["row"], mesh.shape["col"])
    return jax.shard_map(step, mesh=mesh, in_specs=in_specs, out_specs=out_specs, check_vma=False)
```

time: 117 us -> 49.7 us (0.42)
  waiting for transfers between devices: 67 us -> 10.4 us
  matrix products: 24 us -> 1.05 us
  Pallas kernels: 0 us -> 19.4 us
  starting transfers between devices: 0.12 us -> 13.2 us
  between operations: 13.8 us -> 0.78 us
  local copies, waits for them, and re-layouts: 11.9 us -> 3.74 us
    all_gather x2 -> x0, waiting for transfers between devices: 39.6 us -> none  [the longest x1 30.8 us: local(): grad_rows = lax.all_gather(out_grad, 'col', axis=0, tiled=True)]
    reduce_scatter x1 -> x0, waiting for transfers between devices: 26.7 us -> none  [local(): lax.psum_scatter(partial_grad, 'row', scatter_dimension=0, tiled=True)]
    dot_general x5 -> x1, matrix products: 24 us -> 1.05 us  [local(): lax.dot_general(out_grad, weight, (((1,), (1,)), ((), ())), preferred_ele...]
    pallas_call x0 -> x3, Pallas kernels: none -> 19.4 us  [the longest x1 7.75 us: local(): pl.pallas_call(prep_kernel, grid=(tiles // GROUP,), in_specs=[scalars, ti...]
    ppermute x0 -> x13, starting transfers between devices: none -> 13.2 us  [swap(): return lax.ppermute(x, axis, [(i, i ^ mask) for i in range(size)])]
    ppermute x0 -> x13, waiting for transfers between devices: none -> 10.4 us  [swap(): return lax.ppermute(x, axis, [(i, i ^ mask) for i in range(size)])]
    gather x2 -> x0, local copies, waits for them, and re-layouts: 8.5 us -> none  [the longest x1 4.5 us: local(): jnp.take(grad_rows.reshape(-1, BLOCK, hidden), tile_rows, axis=0)]
    unnamed x7 -> x29, local copies, waits for them, and re-layouts: 0.81 us -> 3.74 us
  transfers between devices with their start and end apart: 3 -> 13, of which waited for: 3 -> 2; matrix products, arithmetic and copies ran while one was open for 29% -> 3% of each run, Pallas kernels for 0% -> 39%
where the time goes in v1:
time: 49.7 us; the launch traced here: 49.3 us
  Pallas kernels  19.4 us (39%)
  starting transfers between devices  13.2 us (27%)
  waiting for transfers between devices  10.4 us (21%)
  local copies, waits for them, and re-layouts  3.74 us (8%)
  matrix products  1.05 us (2%)
  between operations  0.78 us (2%)
  other arithmetic  0.72 us (1%)
    ppermute x13, starting transfers between devices, swap(): return lax.ppermute(x, axis, [(i, i ^ mask) for i in range(size)])  13.2 us
    ppermute x13, waiting for transfers between devices, swap(): return lax.ppermute(x, axis, [(i, i ^ mask) for i in range(size)])  10.4 us
    pallas_call x1, Pallas kernels, local(): pl.pallas_call(prep_kernel, grid=(tiles // GROUP,), in_specs=[scalars, ti...  7.75 us
    pallas_call x1, Pallas kernels, local(): pl.pallas_call(functools.partial(scores_kernel, n_row, per), grid=(tiles...  6.6 us
    pallas_call x1, Pallas kernels, local(): pl.pallas_call(functools.partial(sums_kernel, n_row, n_col, per), in_spec...  5.08 us
    unnamed x29, local copies, waits for them, and re-layouts  3.74 us
    dot_general x1, matrix products, local(): lax.dot_general(out_grad, weight, (((1,), (1,)), ((), ())), preferred_ele...  1.05 us
  transfers between devices with their start and end apart: 13, of which 2 were waited for; matrix products, arithmetic and copies ran while one was open for 3% of the time, Pallas kernels for 39%

profile of v1, /device:TPU:0, one launch (start us, length us, event | category | flops | bytes accessed | tf_op | source)
XLA Modules:
  0.0 49.3 jit_solution(10532519039726472871)
XLA Ops:
  0.6 0.0 copy-start
  0.6 0.9 %copy-done = bf16[512,256]{1,0:T(8,128)(2,1)S(1)} copy-done((bf16[512,256]{1,0:T(8,128)(2,1)S(1)}, bf16[512,256]{1,0:T(8,128)(2,1)}, u32[]{:S(2)}) %copy-start) | copy-done | bytes 262168
  1.6 1.1 %convolution_convert_fusion.refs_2_ = bf16[512,128]{1,0:T(8,128)(2,1)S(1)} fusion(bf16[512,256]{1,0:T(8,128)(2,1)S(1)} %copy-done, bf16[128,256]{1,0:T(8,128)(2,1)} %param.7), kind=kOutput, calls=%fused_computation | convolution fusion | flops 33619968 | bytes 458752 | tf_op jit(solution)/shard_map/dot_general | solution.py:99
  2.6 0.0 copy-start.1
  2.7 3.1 %collective-permute-start.1 = (bf16[512,128]{1,0:T(8,128)(2,1)S(1)}, bf16[512,128]{1,0:T(8,128)(2,1)S(1)}, u32[]{:S(2)}, u32[]{:S(2)}) collective-permute-start(bf16[512,128]{1,0:T(8,128)(2,1)S(1)} %convolution_convert_fusion.refs_2_), channel_id=1, source_target_pairs={{0,2},{1,3},{2,0},{3,1},{4,6},{5,7},{6,4},{7,5},{8,10},{9,11},{10,... | collective-permute-start | bytes 393224 | tf_op jit(solution)/shard_map/ppermute | solution.py:17
  5.8 2.6 %collective-permute-start.3 = (bf16[512,128]{1,0:T(8,128)(2,1)S(1)}, bf16[512,128]{1,0:T(8,128)(2,1)S(1)}, u32[]{:S(2)}, u32[]{:S(2)}) collective-permute-start(bf16[512,128]{1,0:T(8,128)(2,1)S(1)} %convolution_convert_fusion.refs_2_), channel_id=1, source_target_pairs={{0,4},{1,5},{2,6},{3,7},{4,0},{5,1},{6,2},{7,3},{8,12},{9,13},{10,... | collective-permute-start | bytes 393224 | tf_op jit(solution)/shard_map/ppermute | solution.py:17
  8.3 0.0 collective-permute-start.5
  8.3 0.0 collective-permute-start
  8.4 2.4 %collective-permute-done.1.refs_4_ = bf16[512,128]{1,0:T(8,128)(2,1)S(1)} collective-permute-done((bf16[512,128]{1,0:T(8,128)(2,1)S(1)}, bf16[512,128]{1,0:T(8,128)(2,1)S(1)}, u32[]{:S(2)}, u32[]{:S(2)}) %collective-permute-start.1) | collective-permute-done | bytes 131104 | tf_op jit(solution)/shard_map/ppermute | solution.py:17
  10.8 0.0 collective-permute-start.2
  10.8 7.9 %collective-permute-done.3.refs_6_ = bf16[512,128]{1,0:T(8,128)(2,1)S(1)} collective-permute-done((bf16[512,128]{1,0:T(8,128)(2,1)S(1)}, bf16[512,128]{1,0:T(8,128)(2,1)S(1)}, u32[]{:S(2)}, u32[]{:S(2)}) %collective-permute-start.3) | collective-permute-done | bytes 131104 | tf_op jit(solution)/shard_map/ppermute | solution.py:17
  18.7 0.0 collective-permute-start.4
  18.7 0.0 collective-permute-done.5.refs_8_
  18.7 0.0 copy-start.6
  18.7 0.5 %collective-permute-start.6 = (bf16[512,128]{1,0:T(8,128)(2,1)S(1)}, bf16[512,128]{1,0:T(8,128)(2,1)S(1)}, u32[]{:S(2)}, u32[]{:S(2)}) collective-permute-start(bf16[512,128]{1,0:T(8,128)(2,1)S(1)} %collective-permute-done.5.refs_8_), channel_id=1, source_target_pairs={{0,1},{1,0},{2,3},{3,2},{4,5},{5,4},{6,7},{7,6},{8,9},{9,8},{10,11... | collective-permute-start | bytes 393224 | tf_op jit(solution)/shard_map/ppermute | solution.py:17
  19.2 1.5 %collective-permute-start.7 = (bf16[512,128]{1,0:T(8,128)(2,1)}, bf16[512,128]{1,0:T(8,128)(2,1)S(1)}, u32[]{:S(2)}, u32[]{:S(2)}) collective-permute-start(bf16[512,128]{1,0:T(8,128)(2,1)} %refs_3_.1), channel_id=1, source_target_pairs={{0,8},{8,0},{16,24},{24,16},{1,9},{9,1},{17,25},{25,17},{2,10},{10... | collective-permute-start | bytes 393224 | tf_op jit(solution)/shard_map/ppermute | solution.py:17
  20.7 1.4 %copy.10.table.refs_0_ = s32[1,1,64,3]{3,2,1,0:T(8,128)} copy(s32[1,1,64,3]{2,1,3,0:T(1,128)} %param.9) | data formatting | bytes 1536 | tf_op args[3]
  22.1 7.8 %prep.1 = (bf16[64,128,128]{2,1,0:T(8,128)(2,1)}, bf16[64,128,128]{2,1,0:T(8,128)(2,1)}) custom-call(s32[1,1,64,3]{3,2,1,0:T(8,128)} %copy.10.table.refs_0_, s32[1,1,64,128,128]{4,3,2,1,0:T(8,128)} %mask.1, bf16[1,1,64,128,128]{4,3,2,1,0:T(8,128)(2,1)} %weights.1), custom_call_target="tpu_custom_call" | custom-call | bytes 6291456 | tf_op jit(solution)/shard_map/prep/pallas_call | solution.py:111
  29.8 0.0 copy-done.1
  29.8 0.0 copy-done.4
  29.8 0.0 copy-done.5
  29.8 0.0 copy-done.6
  29.9 0.0 collective-permute-done.refs_3_
  29.9 0.0 copy-done.3
  29.9 1.6 %collective-permute-start.8 = (bf16[512,128]{1,0:T(8,128)(2,1)S(1)}, bf16[512,128]{1,0:T(8,128)(2,1)S(1)}, u32[]{:S(2)}, u32[]{:S(2)}) collective-permute-start(bf16[512,128]{1,0:T(8,128)(2,1)S(1)} %copy-done.3), channel_id=1, source_target_pairs={{0,16},{8,24},{16,0},{24,8},{1,17},{9,25},{17,1},{25,9},{2,18},{10... | collective-permute-start | bytes 393224 | tf_op jit(solution)/shard_map/ppermute | solution.py:17
  31.5 0.0 collective-permute-done.2.refs_5_
  31.5 0.5 collective-permute-start.9
  32.0 0.0 collective-permute-done.4.refs_7_
  32.0 0.0 collective-permute-done.6.refs_9_
  32.0 0.1 copy-done.10
  32.1 0.5 %copy-done.12 = bf16[512,128]{1,0:T(8,128)(2,1)} copy-done((bf16[512,128]{1,0:T(8,128)(2,1)}, bf16[512,128]{1,0:T(8,128)(2,1)S(1)}, u32[]{:S(2)}) %copy-start.12) | copy-done | bytes 131096
  32.6 0.1 copy-done.13
  32.7 5.1 %sums.1 = (bf16[32,128,128]{2,1,0:T(8,128)(2,1)}, f32[512,128]{1,0:T(8,128)}, bf16[512,128]{1,0:T(8,128)(2,1)}, bf16[512,128]{1,0:T(8,128)(2,1)}, bf16[512,128]{1,0:T(8,128)(2,1)}) custom-call(s32[1,1,64,3]{3,2,1,0:T(8,128)} %copy.10.table.refs_0_, bf16[64,128,128]{2,1,0:T(8,128)(2,1)} %get-tuple-element.9.refs_1_, bf16[512,128]{1,0:T(8,128)(2,1)} %copy-done.1, ...), custom_call_target="tpu_custom_call" | custom-call | flops 268435456 | bytes 4194304 | tf_op jit(solution)/shard_map/sums/pallas_call | solution.py:123
  37.8 1.5 %collective-permute-start.10 = (bf16[512,128]{1,0:T(8,128)(2,1)}, bf16[512,128]{1,0:T(8,128)(2,1)S(1)}, u32[]{:S(2)}, u32[]{:S(2)}) collective-permute-start(bf16[512,128]{1,0:T(8,128)(2,1)} %get-tuple-element.13), channel_id=1, source_target_pairs={{0,8},{8,0},{16,24},{24,16},{1,9},{9,1},{17,25},{25,17},{2,10},{10... | collective-permute-start | bytes 393224 | tf_op jit(solution)/shard_map/ppermute | solution.py:17
  39.3 1.5 %collective-permute-start.11 = (bf16[512,128]{1,0:T(8,128)(2,1)}, bf16[512,128]{1,0:T(8,128)(2,1)S(1)}, u32[]{:S(2)}, u32[]{:S(2)}) collective-permute-start(bf16[512,128]{1,0:T(8,128)(2,1)} %get-tuple-element.14), channel_id=1, source_target_pairs={{0,16},{8,24},{16,0},{24,8},{1,17},{9,25},{17,1},{25,9},{2,18},{10... | collective-permute-start | bytes 393224 | tf_op jit(solution)/shard_map/ppermute | solution.py:17
  40.8 0.0 collective-permute-done.7.refs_4_
  40.8 0.5 collective-permute-start.12
  41.3 0.0 collective-permute-done.8.refs_5_
  41.3 0.0 collective-permute-done.9.refs_6_
  41.3 0.0 copy-start.11
  41.3 0.2 copy-done.7
  41.4 0.5 copy-done.9
  41.9 0.0 copy-done.11
  42.0 6.6 %scores.1 = bf16[1,1,64,128,128]{4,3,2,1,0:T(8,128)(2,1)} custom-call(s32[1,1,64,3]{3,2,1,0:T(8,128)} %copy.10.table.refs_0_, bf16[32,128,128]{2,1,0:T(8,128)(2,1)} %get-tuple-element.10.refs_1_, bf16[64,128,128]{2,1,0:T(8,128)(2,1)} %get-tuple-element.11.refs_2_, bf16[512,128]{1,0:T(8,128)(2,1)} %refs_3_.1, bf16[512,128]{1,0:T(8,128)(2,1)} %copy-done.7, ...), custom_call_target="tpu_custom_call" | custom-call | flops 268435456 | bytes 8388608 | tf_op jit(solution)/shard_map/scores/pallas_call | solution.py:135
  48.6 0.0 collective-permute-done.10
  48.6 0.0 collective-permute-done.11
  48.6 0.0 collective-permute-done.12
  48.6 0.7 %add_convert_fusion = bf16[512,128]{1,0:T(8,128)(2,1)} fusion(bf16[512,128]{1,0:T(8,128)(2,1)S(1)} %collective-permute-done.12, bf16[512,128]{1,0:T(8,128)(2,1)S(1)} %collective-permute-done.11, f32[512,128]{1,0:T(8,128)S(1)} %copy-done.2, bf16[512,128]{1,0:T(8,128)(2,1)S(1)} %collective-permute-done.10), kind=kLoop, calls=%fused_computation.1 | loop fusion | flops 458752 | bytes 786432 | tf_op jit(solution)/shard_map/convert_element_type | solution.py:149
  (12 shorter events, 0.0 us)
Async XLA Ops:
  0.6 1.0 %copy-start = (bf16[512,256]{1,0:T(8,128)(2,1)S(1)}, bf16[512,256]{1,0:T(8,128)(2,1)}, u32[]{:S(2)}) copy-start(bf16[512,256]{1,0:T(8,128)(2,1)} %param.8) | copy-start | bytes 786436
  2.6 27.2 %copy-start.1 = (bf16[512,128]{1,0:T(8,128)(2,1)}, bf16[512,128]{1,0:T(8,128)(2,1)S(1)}, u32[]{:S(2)}) copy-start(bf16[512,128]{1,0:T(8,128)(2,1)S(1)} %convolution_convert_fusion.refs_2_) | copy-start | bytes 393220
  2.7 8.1 %collective-permute-start.1 = (bf16[512,128]{1,0:T(8,128)(2,1)S(1)}, bf16[512,128]{1,0:T(8,128)(2,1)S(1)}, u32[]{:S(2)}, u32[]{:S(2)}) collective-permute-start(bf16[512,128]{1,0:T(8,128)(2,1)S(1)} %convolution_convert_fusion.refs_2_), channel_id=1, source_target_pairs={{0,2},{1,3},{2,0},{3,1},{4,6},{5,7},{6,4},{7,5},{8,10},{9,11},{10,... | collective-permute-start | bytes 393224 | tf_op jit(solution)/shard_map/ppermute | solution.py:17
  5.8 12.9 %collective-permute-start.3 = (bf16[512,128]{1,0:T(8,128)(2,1)S(1)}, bf16[512,128]{1,0:T(8,128)(2,1)S(1)}, u32[]{:S(2)}, u32[]{:S(2)}) collective-permute-start(bf16[512,128]{1,0:T(8,128)(2,1)S(1)} %convolution_convert_fusion.refs_2_), channel_id=1, source_target_pairs={{0,4},{1,5},{2,6},{3,7},{4,0},{5,1},{6,2},{7,3},{8,12},{9,13},{10,... | collective-permute-start | bytes 393224 | tf_op jit(solution)/shard_map/ppermute | solution.py:17
  8.3 10.3 %collective-permute-start.5 = (bf16[512,128]{1,0:T(8,128)(2,1)S(1)}, bf16[512,128]{1,0:T(8,128)(2,1)S(1)}, u32[]{:S(2)}, u32[]{:S(2)}) collective-permute-start(bf16[512,128]{1,0:T(8,128)(2,1)S(1)} %convolution_convert_fusion.refs_2_), channel_id=1, source_target_pairs={{0,6},{1,7},{2,4},{3,5},{4,2},{5,3},{6,0},{7,1},{8,14},{9,15},{10,... | collective-permute-start | bytes 393224 | tf_op jit(solution)/shard_map/ppermute | solution.py:17
  8.3 21.5 %collective-permute-start = (bf16[512,128]{1,0:T(8,128)(2,1)S(1)}, bf16[512,128]{1,0:T(8,128)(2,1)S(1)}, u32[]{:S(2)}, u32[]{:S(2)}) collective-permute-start(bf16[512,128]{1,0:T(8,128)(2,1)S(1)} %convolution_convert_fusion.refs_2_), channel_id=1, source_target_pairs={{0,1},{1,0},{2,3},{3,2},{4,5},{5,4},{6,7},{7,6},{8,9},{9,8},{10,11... | collective-permute-start | bytes 393224 | tf_op jit(solution)/shard_map/ppermute | solution.py:17
  10.8 19.0 %copy-start.4 = (bf16[512,128]{1,0:T(8,128)(2,1)}, bf16[512,128]{1,0:T(8,128)(2,1)S(1)}, u32[]{:S(2)}) copy-start(bf16[512,128]{1,0:T(8,128)(2,1)S(1)} %collective-permute-done.1.refs_4_) | copy-start | bytes 393220
  10.8 20.7 %collective-permute-start.2 = (bf16[512,128]{1,0:T(8,128)(2,1)S(1)}, bf16[512,128]{1,0:T(8,128)(2,1)S(1)}, u32[]{:S(2)}, u32[]{:S(2)}) collective-permute-start(bf16[512,128]{1,0:T(8,128)(2,1)S(1)} %collective-permute-done.1.refs_4_), channel_id=1, source_target_pairs={{0,1},{1,0},{2,3},{3,2},{4,5},{5,4},{6,7},{7,6},{8,9},{9,8},{10,11... | collective-permute-start | bytes 393224 | tf_op jit(solution)/shard_map/ppermute | solution.py:17
  18.7 11.2 %copy-start.5 = (bf16[512,128]{1,0:T(8,128)(2,1)}, bf16[512,128]{1,0:T(8,128)(2,1)S(1)}, u32[]{:S(2)}) copy-start(bf16[512,128]{1,0:T(8,128)(2,1)S(1)} %collective-permute-done.3.refs_6_) | copy-start | bytes 393220
  18.7 13.3 %collective-permute-start.4 = (bf16[512,128]{1,0:T(8,128)(2,1)S(1)}, bf16[512,128]{1,0:T(8,128)(2,1)S(1)}, u32[]{:S(2)}, u32[]{:S(2)}) collective-permute-start(bf16[512,128]{1,0:T(8,128)(2,1)S(1)} %collective-permute-done.3.refs_6_), channel_id=1, source_target_pairs={{0,1},{1,0},{2,3},{3,2},{4,5},{5,4},{6,7},{7,6},{8,9},{9,8},{10,11... | collective-permute-start | bytes 393224 | tf_op jit(solution)/shard_map/ppermute | solution.py:17
  18.7 11.2 %copy-start.6 = (bf16[512,128]{1,0:T(8,128)(2,1)}, bf16[512,128]{1,0:T(8,128)(2,1)S(1)}, u32[]{:S(2)}) copy-start(bf16[512,128]{1,0:T(8,128)(2,1)S(1)} %collective-permute-done.5.refs_8_) | copy-start | bytes 393220
  18.7 13.3 %collective-permute-start.6 = (bf16[512,128]{1,0:T(8,128)(2,1)S(1)}, bf16[512,128]{1,0:T(8,128)(2,1)S(1)}, u32[]{:S(2)}, u32[]{:S(2)}) collective-permute-start(bf16[512,128]{1,0:T(8,128)(2,1)S(1)} %collective-permute-done.5.refs_8_), channel_id=1, source_target_pairs={{0,1},{1,0},{2,3},{3,2},{4,5},{5,4},{6,7},{7,6},{8,9},{9,8},{10,11... | collective-permute-start | bytes 393224 | tf_op jit(solution)/shard_map/ppermute | solution.py:17
  19.2 21.6 %collective-permute-start.7 = (bf16[512,128]{1,0:T(8,128)(2,1)}, bf16[512,128]{1,0:T(8,128)(2,1)S(1)}, u32[]{:S(2)}, u32[]{:S(2)}) collective-permute-start(bf16[512,128]{1,0:T(8,128)(2,1)} %refs_3_.1), channel_id=1, source_target_pairs={{0,8},{8,0},{16,24},{24,16},{1,9},{9,1},{17,25},{25,17},{2,10},{10... | collective-permute-start | bytes 393224 | tf_op jit(solution)/shard_map/ppermute | solution.py:17
  22.1 7.8 %copy-start.3 = (bf16[512,128]{1,0:T(8,128)(2,1)S(1)}, bf16[512,128]{1,0:T(8,128)(2,1)}, u32[]{:S(2)}) copy-start(bf16[512,128]{1,0:T(8,128)(2,1)} %refs_3_.1) | copy-start | bytes 393220
  29.9 2.1 %copy-start.8 = (bf16[512,128]{1,0:T(8,128)(2,1)}, bf16[512,128]{1,0:T(8,128)(2,1)S(1)}, u32[]{:S(2)}) copy-start(bf16[512,128]{1,0:T(8,128)(2,1)S(1)} %collective-permute-done.refs_3_) | copy-start | bytes 393220
  29.9 11.4 %collective-permute-start.8 = (bf16[512,128]{1,0:T(8,128)(2,1)S(1)}, bf16[512,128]{1,0:T(8,128)(2,1)S(1)}, u32[]{:S(2)}, u32[]{:S(2)}) collective-permute-start(bf16[512,128]{1,0:T(8,128)(2,1)S(1)} %copy-done.3), channel_id=1, source_target_pairs={{0,16},{8,24},{16,0},{24,8},{1,17},{9,25},{17,1},{25,9},{2,18},{10... | collective-permute-start | bytes 393224 | tf_op jit(solution)/shard_map/ppermute | solution.py:17
  31.5 0.6 %copy-start.10 = (bf16[512,128]{1,0:T(8,128)(2,1)}, bf16[512,128]{1,0:T(8,128)(2,1)S(1)}, u32[]{:S(2)}) copy-start(bf16[512,128]{1,0:T(8,128)(2,1)S(1)} %collective-permute-done.2.refs_5_) | copy-start | bytes 393220
  31.5 9.8 %collective-permute-start.9 = (bf16[512,128]{1,0:T(8,128)(2,1)S(1)}, bf16[512,128]{1,0:T(8,128)(2,1)S(1)}, u32[]{:S(2)}, u32[]{:S(2)}) collective-permute-start(bf16[512,128]{1,0:T(8,128)(2,1)S(1)} %copy-done.3), channel_id=1, source_target_pairs={{0,24},{8,16},{16,8},{24,0},{1,25},{9,17},{17,9},{25,1},{2,26},{10... | collective-permute-start | bytes 393224 | tf_op jit(solution)/shard_map/ppermute | solution.py:17
  32.0 0.7 %copy-start.12 = (bf16[512,128]{1,0:T(8,128)(2,1)}, bf16[512,128]{1,0:T(8,128)(2,1)S(1)}, u32[]{:S(2)}) copy-start(bf16[512,128]{1,0:T(8,128)(2,1)S(1)} %collective-permute-done.4.refs_7_) | copy-start | bytes 393220
  32.0 0.7 %copy-start.13 = (bf16[512,128]{1,0:T(8,128)(2,1)}, bf16[512,128]{1,0:T(8,128)(2,1)S(1)}, u32[]{:S(2)}) copy-start(bf16[512,128]{1,0:T(8,128)(2,1)S(1)} %collective-permute-done.6.refs_9_) | copy-start | bytes 393220
  37.8 10.8 %collective-permute-start.10 = (bf16[512,128]{1,0:T(8,128)(2,1)}, bf16[512,128]{1,0:T(8,128)(2,1)S(1)}, u32[]{:S(2)}, u32[]{:S(2)}) collective-permute-start(bf16[512,128]{1,0:T(8,128)(2,1)} %get-tuple-element.13), channel_id=1, source_target_pairs={{0,8},{8,0},{16,24},{24,16},{1,9},{9,1},{17,25},{25,17},{2,10},{10... | collective-permute-start | bytes 393224 | tf_op jit(solution)/shard_map/ppermute | solution.py:17
  39.3 9.3 %collective-permute-start.11 = (bf16[512,128]{1,0:T(8,128)(2,1)}, bf16[512,128]{1,0:T(8,128)(2,1)S(1)}, u32[]{:S(2)}, u32[]{:S(2)}) collective-permute-start(bf16[512,128]{1,0:T(8,128)(2,1)} %get-tuple-element.14), channel_id=1, source_target_pairs={{0,16},{8,24},{16,0},{24,8},{1,17},{9,25},{17,1},{25,9},{2,18},{10... | collective-permute-start | bytes 393224 | tf_op jit(solution)/shard_map/ppermute | solution.py:17
  40.8 0.7 %copy-start.7 = (bf16[512,128]{1,0:T(8,128)(2,1)}, bf16[512,128]{1,0:T(8,128)(2,1)S(1)}, u32[]{:S(2)}) copy-start(bf16[512,128]{1,0:T(8,128)(2,1)S(1)} %collective-permute-done.7.refs_4_) | copy-start | bytes 393220
  40.8 7.8 %collective-permute-start.12 = (bf16[512,128]{1,0:T(8,128)(2,1)}, bf16[512,128]{1,0:T(8,128)(2,1)S(1)}, u32[]{:S(2)}, u32[]{:S(2)}) collective-permute-start(bf16[512,128]{1,0:T(8,128)(2,1)} %get-tuple-element.15), channel_id=1, source_target_pairs={{0,24},{8,16},{16,8},{24,0},{1,25},{9,17},{17,9},{25,1},{2,26},{10... | collective-permute-start | bytes 393224 | tf_op jit(solution)/shard_map/ppermute | solution.py:17
  41.3 0.6 %copy-start.9 = (bf16[512,128]{1,0:T(8,128)(2,1)}, bf16[512,128]{1,0:T(8,128)(2,1)S(1)}, u32[]{:S(2)}) copy-start(bf16[512,128]{1,0:T(8,128)(2,1)S(1)} %collective-permute-done.8.refs_5_) | copy-start | bytes 393220
  41.3 0.7 %copy-start.11 = (bf16[512,128]{1,0:T(8,128)(2,1)}, bf16[512,128]{1,0:T(8,128)(2,1)S(1)}, u32[]{:S(2)}) copy-start(bf16[512,128]{1,0:T(8,128)(2,1)S(1)} %collective-permute-done.9.refs_6_) | copy-start | bytes 393220
  42.0 6.6 %copy-start.2 = (f32[512,128]{1,0:T(8,128)S(1)}, f32[512,128]{1,0:T(8,128)}, u32[]{:S(2)}) copy-start(f32[512,128]{1,0:T(8,128)} %get-tuple-element.12) | copy-start | bytes 786436

commit v2 on v1

--- a/solution.py
+++ b/solution.py
@@ -9,12 +9,17 @@
 
 BLOCK = 128
 GROUP = 8
+KERNEL_VMEM = 24 << 20
 VMEM = pltpu.VMEM
 SMEM = pltpu.SMEM
 
 
 def swap(x, axis, size, mask):
     return lax.ppermute(x, axis, [(i, i ^ mask) for i in range(size)])
+
+
+def in_vmem(x):
+    return pltpu.with_memory_space_constraint(x, VMEM)
 
 
 def prep_kernel(table, mask, weights, keep_out, adj_out):
@@ -94,19 +99,15 @@
     whole = pl.BlockSpec(memory_space=VMEM)
     scalars = pl.BlockSpec(memory_space=SMEM)
     tile_block = pl.BlockSpec((1, 1, GROUP, BLOCK, BLOCK), lambda g: (0, 0, g, 0, 0))
-    tile_set = jax.ShapeDtypeStruct((tiles, BLOCK, BLOCK), jnp.bfloat16)
+    tile_set = VMEM((tiles, BLOCK, BLOCK), jnp.bfloat16)
 
     hidden = lax.dot_general(
         out_grad, weight, (((1,), (1,)), ((), ())), preferred_element_type=jnp.float32
     ).astype(jnp.bfloat16)
 
-    slots = [None] * n_col
-    slots[0] = hidden
-    for s in range(2, n_col, 2):
-        slots[s] = swap(hidden, "col", n_col, s)
-    for s in range(0, n_col, 2):
-        slots[s + 1] = swap(slots[s], "col", n_col, 1)
-    col_slots = [features] + [swap(features, "row", n_row, s) for s in range(1, n_row)]
+    near = [swap(hidden, "col", n_col, s) for s in range(2, n_col, 2)]
+    features, hidden = lax.optimization_barrier((features, hidden))
+    cols = [swap(features, "row", n_row, s) for s in range(1, n_row)]
 
     keep, adj = pl.pallas_call(
         prep_kernel,
@@ -115,11 +116,18 @@
         out_specs=[whole, whole],
         out_shape=[tile_set, tile_set],
         cost_estimate=pl.CostEstimate(flops=0, bytes_accessed=edge_mask.size * 6, transcendentals=0),
+        compiler_params=pltpu.CompilerParams(vmem_limit_bytes=KERNEL_VMEM),
         name="prep",
     )(tile_index, edge_mask, edge_weight)
 
-    panel_shape = jax.ShapeDtypeStruct((n_col * per, BLOCK, fin), jnp.bfloat16)
-    chunk = lambda dtype: jax.ShapeDtypeStruct((nodes, fin), dtype)
+    near, cols, keep, adj = lax.optimization_barrier((near, cols, keep, adj))
+    slots = [None] * n_col
+    slots[::2] = [hidden] + near
+    slots[1::2] = [swap(x, "col", n_col, 1) for x in slots[::2]]
+    col_slots = [features] + cols
+
+    panel_shape = VMEM((n_col * per, BLOCK, fin), jnp.bfloat16)
+    chunk = lambda dtype: VMEM((nodes, fin), dtype)
     panel, own, *parts = pl.pallas_call(
         functools.partial(sums_kernel, n_row, n_col, per),
         in_specs=[scalars] + [whole] * (1 + n_col),
@@ -127,8 +135,9 @@
         out_shape=[panel_shape, chunk(jnp.float32)] + [chunk(jnp.bfloat16)] * (n_row - 1),
         scratch_shapes=[VMEM((n_row * per, BLOCK, fin), jnp.float32)],
         cost_estimate=pl.CostEstimate(flops=2 * tiles * BLOCK * BLOCK * fin, bytes_accessed=4 << 20, transcendentals=0),
+        compiler_params=pltpu.CompilerParams(vmem_limit_bytes=KERNEL_VMEM),
         name="sums",
-    )(tile_index, adj, *slots)
+    )(tile_index, *map(in_vmem, (adj, *slots)))
 
     got = [swap(parts[s - 1], "row", n_row, s) for s in range(1, n_row)]
 
@@ -140,8 +149,9 @@
         out_shape=jax.ShapeDtypeStruct(edge_weight.shape, jnp.bfloat16),
         scratch_shapes=[VMEM((n_row * per, fin, BLOCK), jnp.bfloat16)],
         cost_estimate=pl.CostEstimate(flops=2 * tiles * BLOCK * BLOCK * fin, bytes_accessed=8 << 20, transcendentals=0),
+        compiler_params=pltpu.CompilerParams(vmem_limit_bytes=KERNEL_VMEM),
         name="scores",
-    )(tile_index, panel, keep, *col_slots)
+    )(tile_index, *map(in_vmem, (panel, keep, *col_slots)))
 
     total = own
     for part in got:

time: 49.7 us -> 37.2 us (0.75)
  Pallas kernels: 19.4 us -> 11.4 us
  waiting for transfers between devices: 10.4 us -> 3.65 us
  local copies, waits for them, and re-layouts: 3.74 us -> 5.5 us
  starting transfers between devices: 13.2 us -> 13.9 us
    ppermute x13, waiting for transfers between devices: 10.4 us -> 3.65 us  [swap(): return lax.ppermute(x, axis, [(i, i ^ mask) for i in range(size)])]
    pallas_call x1, Pallas kernels: 7.75 us -> 2.59 us  [local(): pl.pallas_call(prep_kernel, grid=(tiles // GROUP,), in_specs=[scalars, ti...]
    pallas_call x1, Pallas kernels: 5.08 us -> 3.15 us  [local(): pl.pallas_call(functools.partial(sums_kernel, n_row, n_col, per), in_spec...]
    unnamed x29 -> x9, local copies, waits for them, and re-layouts: 3.74 us -> 5.5 us
    pallas_call x1, Pallas kernels: 6.6 us -> 5.62 us  [local(): pl.pallas_call(functools.partial(scores_kernel, n_row, per), grid=(tiles...]
    ppermute x13, starting transfers between devices: 13.2 us -> 13.9 us  [swap(): return lax.ppermute(x, axis, [(i, i ^ mask) for i in range(size)])]
  transfers between devices with their start and end apart: 13 -> 13, of which waited for: 2 -> 5; matrix products, arithmetic and copies ran while one was open for 3% -> 2% of each run, Pallas kernels for 39% -> 22%
where the time goes in v2:
time: 37.2 us; the launch traced here: 36.9 us
  starting transfers between devices  13.9 us (37%)
  Pallas kernels  11.4 us (31%)
  local copies, waits for them, and re-layouts  5.5 us (15%)
  waiting for transfers between devices  3.65 us (10%)
  matrix products  1.05 us (3%)
  other arithmetic  0.72 us (2%)
  between operations  0.72 us (2%)
    ppermute x13, starting transfers between devices, swap(): return lax.ppermute(x, axis, [(i, i ^ mask) for i in range(size)])  13.9 us
    pallas_call x1, Pallas kernels, local(): pl.pallas_call(functools.partial(scores_kernel, n_row, per), grid=(tiles...  5.62 us
    unnamed x9, local copies, waits for them, and re-layouts  5.5 us
    ppermute x13, waiting for transfers between devices, swap(): return lax.ppermute(x, axis, [(i, i ^ mask) for i in range(size)])  3.65 us
    pallas_call x1, Pallas kernels, local(): pl.pallas_call(functools.partial(sums_kernel, n_row, n_col, per), in_spec...  3.15 us
    pallas_call x1, Pallas kernels, local(): pl.pallas_call(prep_kernel, grid=(tiles // GROUP,), in_specs=[scalars, ti...  2.59 us
    dot_general x1, matrix products, local(): lax.dot_general(out_grad, weight, (((1,), (1,)), ((), ())), preferred_ele...  1.05 us
  transfers between devices with their start and end apart: 13, of which 5 were waited for; matrix products, arithmetic and copies ran while one was open for 2% of the time, Pallas kernels for 22%

profile of v2, /device:TPU:0, one launch (start us, length us, event | category | flops | bytes accessed | tf_op | source)
XLA Modules:
  0.0 36.9 jit_solution(5814977994738084142)
XLA Ops:
  0.6 0.0 copy-start
  0.6 0.9 %copy-done = bf16[512,256]{1,0:T(8,128)(2,1)S(1)} copy-done((bf16[512,256]{1,0:T(8,128)(2,1)S(1)}, bf16[512,256]{1,0:T(8,128)(2,1)}, u32[]{:S(2)}) %copy-start) | copy-done | bytes 262168
  1.6 1.1 %convolution_convert_fusion.refs_2_ = bf16[512,128]{1,0:T(8,128)(2,1)S(1)} fusion(bf16[512,256]{1,0:T(8,128)(2,1)S(1)} %copy-done, bf16[128,256]{1,0:T(8,128)(2,1)} %param.7), kind=kOutput, calls=%fused_computation | convolution fusion | flops 33619968 | bytes 458752 | tf_op jit(solution)/shard_map/dot_general | solution.py:104
  2.6 4.0 %collective-permute-start.5 = (bf16[512,128]{1,0:T(8,128)(2,1)}, bf16[512,128]{1,0:T(8,128)(2,1)S(1)}, u32[]{:S(2)}, u32[]{:S(2)}) collective-permute-start(bf16[512,128]{1,0:T(8,128)(2,1)} %refs_3_), channel_id=1, source_target_pairs={{0,24},{8,16},{16,8},{24,0},{1,25},{9,17},{17,9},{25,1},{2,26},{10... | collective-permute-start | bytes 393224 | tf_op jit(solution)/shard_map/ppermute | solution.py:18
  6.6 0.5 %collective-permute-start.4 = (bf16[512,128]{1,0:T(8,128)(2,1)}, bf16[512,128]{1,0:T(8,128)(2,1)S(1)}, u32[]{:S(2)}, u32[]{:S(2)}) collective-permute-start(bf16[512,128]{1,0:T(8,128)(2,1)} %refs_3_), channel_id=1, source_target_pairs={{0,16},{8,24},{16,0},{24,8},{1,17},{9,25},{17,1},{25,9},{2,18},{10... | collective-permute-start | bytes 393224 | tf_op jit(solution)/shard_map/ppermute | solution.py:18
  7.1 0.1 collective-permute-start.3
  7.3 4.0 %collective-permute-start.2 = (bf16[512,128]{1,0:T(8,128)(2,1)S(1)}, bf16[512,128]{1,0:T(8,128)(2,1)S(1)}, u32[]{:S(2)}, u32[]{:S(2)}) collective-permute-start(bf16[512,128]{1,0:T(8,128)(2,1)S(1)} %convolution_convert_fusion.refs_2_), channel_id=1, source_target_pairs={{0,6},{1,7},{2,4},{3,5},{4,2},{5,3},{6,0},{7,1},{8,14},{9,15},{10,... | collective-permute-start | bytes 393224 | tf_op jit(solution)/shard_map/ppermute | solution.py:18
  11.3 0.0 collective-permute-start.1
  11.3 0.0 collective-permute-done.5.refs_6_
  11.3 1.1 %collective-permute-start = (bf16[512,128]{1,0:T(8,128)(2,1)S(1)}, bf16[512,128]{1,0:T(8,128)(2,1)S(1)}, u32[]{:S(2)}, u32[]{:S(2)}) collective-permute-start(bf16[512,128]{1,0:T(8,128)(2,1)S(1)} %convolution_convert_fusion.refs_2_), channel_id=1, source_target_pairs={{0,2},{1,3},{2,0},{3,1},{4,6},{5,7},{6,4},{7,5},{8,10},{9,11},{10,... | collective-permute-start | bytes 393224 | tf_op jit(solution)/shard_map/ppermute | solution.py:18
  12.4 0.8 %copy.10.table.refs_0_ = s32[1,1,64,3]{3,2,1,0:T(8,128)S(1)} copy(s32[1,1,64,3]{2,1,3,0:T(1,128)} %param.9) | data formatting | bytes 1536 | tf_op args[3]
  13.2 0.0 copy-start.1
  13.2 2.2 %copy-done.1 = s32[1,1,64,128,128]{4,3,2,1,0:T(8,128)S(1)} copy-done((s32[1,1,64,128,128]{4,3,2,1,0:T(8,128)S(1)}, s32[1,1,64,128,128]{4,3,2,1,0:T(8,128)}, u32[]{:S(2)}) %copy-start.1) | copy-done | bytes 4194328
  15.4 0.0 copy-start.2
  15.4 1.6 %copy-done.2 = bf16[1,1,64,128,128]{4,3,2,1,0:T(8,128)(2,1)S(1)} copy-done((bf16[1,1,64,128,128]{4,3,2,1,0:T(8,128)(2,1)S(1)}, bf16[1,1,64,128,128]{4,3,2,1,0:T(8,128)(2,1)}, u32[]{:S(2)}) %copy-start.2) | copy-done | bytes 2097176
  17.0 2.6 %prep.1 = (bf16[64,128,128]{2,1,0:T(8,128)(2,1)S(1)}, bf16[64,128,128]{2,1,0:T(8,128)(2,1)S(1)}) custom-call(s32[1,1,64,3]{3,2,1,0:T(8,128)S(1)} %copy.10.table.refs_0_, s32[1,1,64,128,128]{4,3,2,1,0:T(8,128)S(1)} %copy-done.1, bf16[1,1,64,128,128]{4,3,2,1,0:T(8,128)(2,1)S(1)} %copy-done.2), custom_call_target="tpu_custom_call" | custom-call | bytes 6291456 | tf_op jit(solution)/shard_map/prep/pallas_call | solution.py:112
  19.6 0.0 copy-start.3
  19.6 0.0 collective-permute-done.4.refs_5_
  19.6 0.1 collective-permute-start.6
  19.7 0.0 collective-permute-done.3.refs_4_
  19.7 0.0 collective-permute-done.2.refs_8_
  19.7 1.8 %collective-permute-done.1.refs_6_ = bf16[512,128]{1,0:T(8,128)(2,1)S(1)} collective-permute-done((bf16[512,128]{1,0:T(8,128)(2,1)S(1)}, bf16[512,128]{1,0:T(8,128)(2,1)S(1)}, u32[]{:S(2)}, u32[]{:S(2)}) %collective-permute-start.1) | collective-permute-done | bytes 131104 | tf_op jit(solution)/shard_map/ppermute | solution.py:18
  21.5 0.0 collective-permute-done.refs_4_
  21.5 0.0 collective-permute-start.7
  21.5 0.5 %collective-permute-start.8 = (bf16[512,128]{1,0:T(8,128)(2,1)S(1)}, bf16[512,128]{1,0:T(8,128)(2,1)S(1)}, u32[]{:S(2)}, u32[]{:S(2)}) collective-permute-start(bf16[512,128]{1,0:T(8,128)(2,1)S(1)} %collective-permute-done.1.refs_6_), channel_id=1, source_target_pairs={{0,1},{1,0},{2,3},{3,2},{4,5},{5,4},{6,7},{7,6},{8,9},{9,8},{10,11... | collective-permute-start | bytes 393224 | tf_op jit(solution)/shard_map/ppermute | solution.py:18
  22.0 0.0 collective-permute-start.9
  22.0 0.0 collective-permute-done.6.refs_3_
  22.0 0.8 %collective-permute-done.7.refs_5_ = bf16[512,128]{1,0:T(8,128)(2,1)S(1)} collective-permute-done((bf16[512,128]{1,0:T(8,128)(2,1)S(1)}, bf16[512,128]{1,0:T(8,128)(2,1)S(1)}, u32[]{:S(2)}, u32[]{:S(2)}) %collective-permute-start.7) | collective-permute-done | bytes 131104 | tf_op jit(solution)/shard_map/ppermute | solution.py:18
  22.8 0.2 collective-permute-done.8.refs_7_
  23.0 0.3 collective-permute-done.9.refs_9_
  23.4 3.2 %sums.1 = (bf16[32,128,128]{2,1,0:T(8,128)(2,1)S(1)}, f32[512,128]{1,0:T(8,128)S(1)}, bf16[512,128]{1,0:T(8,128)(2,1)S(1)}, bf16[512,128]{1,0:T(8,128)(2,1)S(1)}, bf16[512,128]{1,0:T(8,128)(2,1)S(1)}) custom-call(s32[1,1,64,3]{3,2,1,0:T(8,128)S(1)} %copy.10.table.refs_0_, bf16[64,128,128]{2,1,0:T(8,128)(2,1)S(1)} %get-tuple-element.22.refs_1_, ...), custom_call_target="tpu_custom_call" | custom-call | flops 268435456 | bytes 4194304 | tf_op jit(solution)/shard_map/sums/pallas_call | solution.py:131
  26.5 1.6 %collective-permute-start.10 = (bf16[512,128]{1,0:T(8,128)(2,1)S(1)}, bf16[512,128]{1,0:T(8,128)(2,1)S(1)}, u32[]{:S(2)}, u32[]{:S(2)}) collective-permute-start(bf16[512,128]{1,0:T(8,128)(2,1)S(1)} %get-tuple-element.33), channel_id=1, source_target_pairs={{0,8},{8,0},{16,24},{24,16},{1,9},{9,1},{17,25},{25,17},{2,10},{10... | collective-permute-start | bytes 393224 | tf_op jit(solution)/shard_map/ppermute | solution.py:18
  28.1 1.5 %collective-permute-start.11 = (bf16[512,128]{1,0:T(8,128)(2,1)S(1)}, bf16[512,128]{1,0:T(8,128)(2,1)S(1)}, u32[]{:S(2)}, u32[]{:S(2)}) collective-permute-start(bf16[512,128]{1,0:T(8,128)(2,1)S(1)} %get-tuple-element.34), channel_id=1, source_target_pairs={{0,16},{8,24},{16,0},{24,8},{1,17},{9,25},{17,1},{25,9},{2,18},{10... | collective-permute-start | bytes 393224 | tf_op jit(solution)/shard_map/ppermute | solution.py:18
  29.6 0.5 %collective-permute-start.12 = (bf16[512,128]{1,0:T(8,128)(2,1)S(1)}, bf16[512,128]{1,0:T(8,128)(2,1)S(1)}, u32[]{:S(2)}, u32[]{:S(2)}) collective-permute-start(bf16[512,128]{1,0:T(8,128)(2,1)S(1)} %get-tuple-element.35), channel_id=1, source_target_pairs={{0,24},{8,16},{16,8},{24,0},{1,25},{9,17},{17,9},{25,1},{2,26},{10... | collective-permute-start | bytes 393224 | tf_op jit(solution)/shard_map/ppermute | solution.py:18
  30.1 0.0 copy-done.3
  30.1 5.6 %scores.1 = bf16[1,1,64,128,128]{4,3,2,1,0:T(8,128)(2,1)} custom-call(s32[1,1,64,3]{3,2,1,0:T(8,128)S(1)} %copy.10.table.refs_0_, bf16[32,128,128]{2,1,0:T(8,128)(2,1)S(1)} %get-tuple-element.27.refs_1_, bf16[64,128,128]{2,1,0:T(8,128)(2,1)S(1)} %get-tuple-element.28.refs_2_, bf16[512,128]{1,0:T(8,128)(2,1)S(1)} %copy-done.3, ...), custom_call_target="tpu_custom_call" | custom-call | flops 268435456 | bytes 8388608 | tf_op jit(solution)/shard_map/scores/pallas_call | solution.py:144
  35.7 0.0 collective-permute-done.10
  35.7 0.5 %collective-permute-done.11 = bf16[512,128]{1,0:T(8,128)(2,1)S(1)} collective-permute-done((bf16[512,128]{1,0:T(8,128)(2,1)S(1)}, bf16[512,128]{1,0:T(8,128)(2,1)S(1)}, u32[]{:S(2)}, u32[]{:S(2)}) %collective-permute-start.11) | collective-permute-done | bytes 131104 | tf_op jit(solution)/shard_map/ppermute | solution.py:18
  36.2 0.0 collective-permute-done.12
  36.2 0.7 %add_convert_fusion = bf16[512,128]{1,0:T(8,128)(2,1)} fusion(bf16[512,128]{1,0:T(8,128)(2,1)S(1)} %collective-permute-done.12, bf16[512,128]{1,0:T(8,128)(2,1)S(1)} %collective-permute-done.11, f32[512,128]{1,0:T(8,128)S(1)} %get-tuple-element.32, bf16[512,128]{1,0:T(8,128)(2,1)S(1)} %collective-permute-done.10), kind=kLoop, calls=%fused_computation.1 | loop fusion | flops 458752 | bytes 786432 | tf_op jit(solution)/shard_map/convert_element_type | solution.py:159
Async XLA Ops:
  0.6 1.0 %copy-start = (bf16[512,256]{1,0:T(8,128)(2,1)S(1)}, bf16[512,256]{1,0:T(8,128)(2,1)}, u32[]{:S(2)}) copy-start(bf16[512,256]{1,0:T(8,128)(2,1)} %param.8) | copy-start | bytes 786436
  2.6 8.6 %collective-permute-start.5 = (bf16[512,128]{1,0:T(8,128)(2,1)}, bf16[512,128]{1,0:T(8,128)(2,1)S(1)}, u32[]{:S(2)}, u32[]{:S(2)}) collective-permute-start(bf16[512,128]{1,0:T(8,128)(2,1)} %refs_3_), channel_id=1, source_target_pairs={{0,24},{8,16},{16,8},{24,0},{1,25},{9,17},{17,9},{25,1},{2,26},{10... | collective-permute-start | bytes 393224 | tf_op jit(solution)/shard_map/ppermute | solution.py:18
  6.6 13.0 %collective-permute-start.4 = (bf16[512,128]{1,0:T(8,128)(2,1)}, bf16[512,128]{1,0:T(8,128)(2,1)S(1)}, u32[]{:S(2)}, u32[]{:S(2)}) collective-permute-start(bf16[512,128]{1,0:T(8,128)(2,1)} %refs_3_), channel_id=1, source_target_pairs={{0,16},{8,24},{16,0},{24,8},{1,17},{9,25},{17,1},{25,9},{2,18},{10... | collective-permute-start | bytes 393224 | tf_op jit(solution)/shard_map/ppermute | solution.py:18
  7.1 12.6 %collective-permute-start.3 = (bf16[512,128]{1,0:T(8,128)(2,1)}, bf16[512,128]{1,0:T(8,128)(2,1)S(1)}, u32[]{:S(2)}, u32[]{:S(2)}) collective-permute-start(bf16[512,128]{1,0:T(8,128)(2,1)} %refs_3_), channel_id=1, source_target_pairs={{0,8},{8,0},{16,24},{24,16},{1,9},{9,1},{17,25},{25,17},{2,10},{10... | collective-permute-start | bytes 393224 | tf_op jit(solution)/shard_map/ppermute | solution.py:18
  7.3 12.4 %collective-permute-start.2 = (bf16[512,128]{1,0:T(8,128)(2,1)S(1)}, bf16[512,128]{1,0:T(8,128)(2,1)S(1)}, u32[]{:S(2)}, u32[]{:S(2)}) collective-permute-start(bf16[512,128]{1,0:T(8,128)(2,1)S(1)} %convolution_convert_fusion.refs_2_), channel_id=1, source_target_pairs={{0,6},{1,7},{2,4},{3,5},{4,2},{5,3},{6,0},{7,1},{8,14},{9,15},{10,... | collective-permute-start | bytes 393224 | tf_op jit(solution)/shard_map/ppermute | solution.py:18
  11.3 10.2 %collective-permute-start.1 = (bf16[512,128]{1,0:T(8,128)(2,1)S(1)}, bf16[512,128]{1,0:T(8,128)(2,1)S(1)}, u32[]{:S(2)}, u32[]{:S(2)}) collective-permute-start(bf16[512,128]{1,0:T(8,128)(2,1)S(1)} %convolution_convert_fusion.refs_2_), channel_id=1, source_target_pairs={{0,4},{1,5},{2,6},{3,7},{4,0},{5,1},{6,2},{7,3},{8,12},{9,13},{10,... | collective-permute-start | bytes 393224 | tf_op jit(solution)/shard_map/ppermute | solution.py:18
  11.3 10.2 %collective-permute-start = (bf16[512,128]{1,0:T(8,128)(2,1)S(1)}, bf16[512,128]{1,0:T(8,128)(2,1)S(1)}, u32[]{:S(2)}, u32[]{:S(2)}) collective-permute-start(bf16[512,128]{1,0:T(8,128)(2,1)S(1)} %convolution_convert_fusion.refs_2_), channel_id=1, source_target_pairs={{0,2},{1,3},{2,0},{3,1},{4,6},{5,7},{6,4},{7,5},{8,10},{9,11},{10,... | collective-permute-start | bytes 393224 | tf_op jit(solution)/shard_map/ppermute | solution.py:18
  13.2 2.2 %copy-start.1 = (s32[1,1,64,128,128]{4,3,2,1,0:T(8,128)S(1)}, s32[1,1,64,128,128]{4,3,2,1,0:T(8,128)}, u32[]{:S(2)}) copy-start(s32[1,1,64,128,128]{4,3,2,1,0:T(8,128)} %mask.1) | copy-start | bytes 12582916
  15.4 1.6 %copy-start.2 = (bf16[1,1,64,128,128]{4,3,2,1,0:T(8,128)(2,1)S(1)}, bf16[1,1,64,128,128]{4,3,2,1,0:T(8,128)(2,1)}, u32[]{:S(2)}) copy-start(bf16[1,1,64,128,128]{4,3,2,1,0:T(8,128)(2,1)} %weights.1) | copy-start | bytes 6291460
  19.6 10.5 %copy-start.3 = (bf16[512,128]{1,0:T(8,128)(2,1)S(1)}, bf16[512,128]{1,0:T(8,128)(2,1)}, u32[]{:S(2)}) copy-start(bf16[512,128]{1,0:T(8,128)(2,1)} %refs_3_) | copy-start | bytes 393220
  19.6 2.4 %collective-permute-start.6 = (bf16[512,128]{1,0:T(8,128)(2,1)S(1)}, bf16[512,128]{1,0:T(8,128)(2,1)S(1)}, u32[]{:S(2)}, u32[]{:S(2)}) collective-permute-start(bf16[512,128]{1,0:T(8,128)(2,1)S(1)} %convolution_convert_fusion.refs_2_), channel_id=1, source_target_pairs={{0,1},{1,0},{2,3},{3,2},{4,5},{5,4},{6,7},{7,6},{8,9},{9,8},{10,11... | collective-permute-start | bytes 393224 | tf_op jit(solution)/shard_map/ppermute | solution.py:18
  21.5 1.3 %collective-permute-start.7 = (bf16[512,128]{1,0:T(8,128)(2,1)S(1)}, bf16[512,128]{1,0:T(8,128)(2,1)S(1)}, u32[]{:S(2)}, u32[]{:S(2)}) collective-permute-start(bf16[512,128]{1,0:T(8,128)(2,1)S(1)} %collective-permute-done.refs_4_), channel_id=1, source_target_pairs={{0,1},{1,0},{2,3},{3,2},{4,5},{5,4},{6,7},{7,6},{8,9},{9,8},{10,11... | collective-permute-start | bytes 393224 | tf_op jit(solution)/shard_map/ppermute | solution.py:18
  21.5 1.5 %collective-permute-start.8 = (bf16[512,128]{1,0:T(8,128)(2,1)S(1)}, bf16[512,128]{1,0:T(8,128)(2,1)S(1)}, u32[]{:S(2)}, u32[]{:S(2)}) collective-permute-start(bf16[512,128]{1,0:T(8,128)(2,1)S(1)} %collective-permute-done.1.refs_6_), channel_id=1, source_target_pairs={{0,1},{1,0},{2,3},{3,2},{4,5},{5,4},{6,7},{7,6},{8,9},{9,8},{10,11... | collective-permute-start | bytes 393224 | tf_op jit(solution)/shard_map/ppermute | solution.py:18
  22.0 1.3 %collective-permute-start.9 = (bf16[512,128]{1,0:T(8,128)(2,1)S(1)}, bf16[512,128]{1,0:T(8,128)(2,1)S(1)}, u32[]{:S(2)}, u32[]{:S(2)}) collective-permute-start(bf16[512,128]{1,0:T(8,128)(2,1)S(1)} %collective-permute-done.2.refs_8_), channel_id=1, source_target_pairs={{0,1},{1,0},{2,3},{3,2},{4,5},{5,4},{6,7},{7,6},{8,9},{9,8},{10,11... | collective-permute-start | bytes 393224 | tf_op jit(solution)/shard_map/ppermute | solution.py:18
  26.5 9.2 %collective-permute-start.10 = (bf16[512,128]{1,0:T(8,128)(2,1)S(1)}, bf16[512,128]{1,0:T(8,128)(2,1)S(1)}, u32[]{:S(2)}, u32[]{:S(2)}) collective-permute-start(bf16[512,128]{1,0:T(8,128)(2,1)S(1)} %get-tuple-element.33), channel_id=1, source_target_pairs={{0,8},{8,0},{16,24},{24,16},{1,9},{9,1},{17,25},{25,17},{2,10},{10... | collective-permute-start | bytes 393224 | tf_op jit(solution)/shard_map/ppermute | solution.py:18
  28.1 8.1 %collective-permute-start.11 = (bf16[512,128]{1,0:T(8,128)(2,1)S(1)}, bf16[512,128]{1,0:T(8,128)(2,1)S(1)}, u32[]{:S(2)}, u32[]{:S(2)}) collective-permute-start(bf16[512,128]{1,0:T(8,128)(2,1)S(1)} %get-tuple-element.34), channel_id=1, source_target_pairs={{0,16},{8,24},{16,0},{24,8},{1,17},{9,25},{17,1},{25,9},{2,18},{10... | collective-permute-start | bytes 393224 | tf_op jit(solution)/shard_map/ppermute | solution.py:18
  29.6 6.6 %collective-permute-start.12 = (bf16[512,128]{1,0:T(8,128)(2,1)S(1)}, bf16[512,128]{1,0:T(8,128)(2,1)S(1)}, u32[]{:S(2)}, u32[]{:S(2)}) collective-permute-start(bf16[512,128]{1,0:T(8,128)(2,1)S(1)} %get-tuple-element.35), channel_id=1, source_target_pairs={{0,24},{8,16},{16,8},{24,0},{1,25},{9,17},{17,9},{25,1},{2,26},{10... | collective-permute-start | bytes 393224 | tf_op jit(solution)/shard_map/ppermute | solution.py:18

commit v3 on v2

v3 whole, which is shorter than its diff:
```python
import functools

import jax
import jax.numpy as jnp
from jax import lax
from jax.experimental import pallas as pl
from jax.experimental.pallas import tpu as pltpu
from jax.sharding import PartitionSpec as P

BLOCK = 128
GROUP = 8
KERNEL_VMEM = 24 << 20
VMEM = pltpu.VMEM
SMEM = pltpu.SMEM


def in_vmem(x):
    return pltpu.with_memory_space_constraint(x, VMEM)


def in_hbm(x):
    return pltpu.with_memory_space_constraint(x, pltpu.HBM)


def swap(x, axis, size, mask):
    return lax.ppermute(x, axis, [(i, i ^ mask) for i in range(size)])


def prep_kernel(n_row, n_col, per, index, mask, weights, keep_out, adj_out, places, table, mask_buf, weight_buf, sems, table_sem):
    tiles = mask_buf.shape[0]
    groups = tiles // GROUP
    me = lax.axis_index("col")
    row = lax.axis_index("row")

    def fetch(g):
        span = pl.ds(pl.multiple_of(g * GROUP, GROUP), GROUP)
        return (
            pltpu.make_async_copy(mask.at[0, 0, span], mask_buf.at[span], sems.at[0, g]),
            pltpu.make_async_copy(weights.at[0, 0, span], weight_buf.at[span], sems.at[1, g]),
        )

    table_copy = pltpu.make_async_copy(index, table, table_sem)
    table_copy.start()
    for g in range(groups):
        for copy in fetch(g):
            copy.start()
    table_copy.wait()

    def body(g, carry):
        for i in range(GROUP):
            t = g * GROUP + i
            a = table[0, 0, 0, t]
            b = table[0, 1, 0, t]
            places[t] = ((a // per) ^ me) * per + a % per
            places[tiles + t] = ((b // per) ^ row) * per + b % per
        for copy in fetch(g):
            copy.wait()
        for i in range(GROUP):
            t = g * GROUP + i
            keep = (mask_buf[t] * table[0, 2, 0, t]).astype(jnp.float32).astype(jnp.bfloat16)
            keep_out[t] = keep
            adj_out[t] = (weight_buf[t] * keep).T
        return carry

    lax.fori_loop(0, groups, body, 0)


def sums_kernel(n_row, n_col, per, *refs):
    places, adj = refs[:2]
    slots = refs[2 : 2 + n_col]
    panel = refs[2 + n_col]
    outs = refs[3 + n_col : 3 + n_col + n_row]
    total = refs[3 + n_col + n_row]
    tiles = adj.shape[0]
    for s in range(n_col):
        for i in range(per):
            panel[s * per + i] = slots[s][i * BLOCK : (i + 1) * BLOCK, :]
    total[...] = jnp.zeros_like(total)
    for t in range(tiles):
        total[places[tiles + t]] += jnp.dot(adj[t], panel[places[t]], preferred_element_type=jnp.float32)
    for s in range(n_row):
        for i in range(per):
            outs[s][i * BLOCK : (i + 1) * BLOCK, :] = total[s * per + i].astype(outs[s].dtype)


def scores_kernel(n_row, per, *refs):
    places, panel, keep = refs[:3]
    slots = refs[3 : 3 + n_row]
    out, cols, stage, sems = refs[3 + n_row :]
    tiles = keep.shape[0]
    for s in range(n_row):
        for i in range(per):
            cols[s * per + i] = slots[s][i * BLOCK : (i + 1) * BLOCK, :].T
    copies = []
    for g in range(tiles // GROUP):
        for t in range(g * GROUP, (g + 1) * GROUP):
            found = jnp.dot(panel[places[t]], cols[places[tiles + t]], preferred_element_type=jnp.float32)
            stage[t] = found.astype(jnp.bfloat16) * keep[t]
        span = pl.ds(g * GROUP, GROUP)
        copies.append(pltpu.make_async_copy(stage.at[span], out.at[0, 0, span], sems.at[g]))
        copies[-1].start()
    for copy in copies:
        copy.wait()


def local(n_row, n_col, features, weight, out_grad, tile_index, edge_mask, edge_weight):
    tiles = edge_mask.shape[2]
    nodes, fin = features.shape
    per = nodes // BLOCK
    whole = pl.BlockSpec(memory_space=VMEM)
    far = pl.BlockSpec(memory_space=pl.ANY)
    scalars = pl.BlockSpec(memory_space=SMEM)
    params = pltpu.CompilerParams(vmem_limit_bytes=KERNEL_VMEM)
    tile_set = VMEM((tiles, BLOCK, BLOCK), jnp.bfloat16)
    product_flops = 2 * tiles * BLOCK * BLOCK * fin

    hidden = lax.dot_general(
        out_grad, weight, (((1,), (1,)), ((), ())), preferred_element_type=jnp.float32
    ).astype(jnp.bfloat16)

    near = [swap(hidden, "col", n_col, s) for s in range(2, n_col, 2)]
    beside = swap(hidden, "col", n_col, 1)
    features, hidden = lax.optimization_barrier((features, hidden))
    cols = [swap(features, "row", n_row, s) for s in range(1, n_row)]

    index = jnp.transpose(tile_index, (0, 3, 1, 2))
    index, beside = lax.optimization_barrier((index, beside))
    keep, adj, places = pl.pallas_call(
        functools.partial(prep_kernel, n_row, n_col, per),
        in_specs=[far, far, far],
        out_specs=[whole, whole, scalars],
        out_shape=[tile_set, tile_set, SMEM((2 * tiles,), jnp.int32)],
        scratch_shapes=[
            SMEM(index.shape, jnp.int32),
            VMEM((tiles, BLOCK, BLOCK), jnp.int32),
            VMEM((tiles, BLOCK, BLOCK), jnp.bfloat16),
            pltpu.SemaphoreType.DMA((2, tiles // GROUP)),
            pltpu.SemaphoreType.DMA,
        ],
        cost_estimate=pl.CostEstimate(flops=0, bytes_accessed=6 * tiles * BLOCK * BLOCK, transcendentals=0),
        compiler_params=params,
        name="prep",
    )(index, in_hbm(edge_mask), in_hbm(edge_weight))
    places = pltpu.with_memory_space_constraint(places, SMEM)

    near, keep, adj = lax.optimization_barrier((near, keep, adj))
    slots = [None] * n_col
    slots[::2] = [hidden] + near
    slots[1::2] = [beside] + [swap(x, "col", n_col, 1) for x in near]
    slots, cols = lax.optimization_barrier((slots, cols))
    cols = [features] + cols

    panel, own, *parts = pl.pallas_call(
        functools.partial(sums_kernel, n_row, n_col, per),
        in_specs=[scalars] + [whole] * (1 + n_col),
        out_specs=[whole] * (1 + n_row),
        out_shape=[VMEM((n_col * per, BLOCK, fin), jnp.bfloat16), VMEM((nodes, fin), jnp.float32)]
        + [VMEM((nodes, fin), jnp.bfloat16)] * (n_row - 1),
        scratch_shapes=[VMEM((n_row * per, BLOCK, fin), jnp.float32)],
        cost_estimate=pl.CostEstimate(flops=product_flops, bytes_accessed=4 << 20, transcendentals=0),
        compiler_params=params,
        name="sums",
    )(places, *map(in_vmem, (adj, *slots)))

    got = [swap(part, "row", n_row, s + 1) for s, part in enumerate(parts)]

    edge_grad = pl.pallas_call(
        functools.partial(scores_kernel, n_row, per),
        in_specs=[scalars] + [whole] * (2 + n_row),
        out_specs=far,
        out_shape=jax.ShapeDtypeStruct(edge_weight.shape, jnp.bfloat16),
        scratch_shapes=[
            VMEM((n_row * per, fin, BLOCK), jnp.bfloat16),
            VMEM((tiles, BLOCK, BLOCK), jnp.bfloat16),
            pltpu.SemaphoreType.DMA((tiles // GROUP,)),
        ],
        cost_estimate=pl.CostEstimate(flops=product_flops, bytes_accessed=4 << 20, transcendentals=0),
        compiler_params=params,
        name="scores",
    )(places, *map(in_vmem, (panel, keep, *cols)))

    total = own
    for part in got:
        total = total + part.astype(jnp.float32)
    return edge_grad, total.astype(jnp.bfloat16)


def solution(mesh):
    in_specs = (
        P(("col", "row"), None),
        P(),
        P(("row", "col"), None),
        P("row", "col", None, None),
        P("row", "col", None, None, None),
        P("row", "col", None, None, None),
    )
    out_specs = (P("row", "col", None, None, None), P(("col", "row"), None))
    step = functools.partial(local, mesh.shape["row"], mesh.shape["col"])
    return jax.shard_map(step, mesh=mesh, in_specs=in_specs, out_specs=out_specs, check_vma=False)
```

time: 37.2 us -> 33 us (0.89)
  waiting for transfers between devices: 3.65 us -> 9.01 us
  Pallas kernels: 11.4 us -> 6.17 us
  local copies, waits for them, and re-layouts: 5.5 us -> 1.63 us
  starting transfers between devices: 13.9 us -> 13.5 us
    ppermute x13, waiting for transfers between devices: 3.65 us -> 9.01 us  [swap(): return lax.ppermute(x, axis, [(i, i ^ mask) for i in range(size)])]
    unnamed x9 -> x6, local copies, waits for them, and re-layouts: 5.5 us -> 1.63 us
    pallas_call x2, Pallas kernels: 8.21 us -> 5.22 us  [the longest x1 3.36 us: local(): pl.pallas_call(functools.partial(prep_kernel, n_row, n_col, per), in_spec...]
    pallas_call x1, Pallas kernels: 3.15 us -> 0.95 us  [local(): pl.pallas_call(functools.partial(sums_kernel, n_row, n_col, per), in_spec...]
    ppermute x13, starting transfers between devices: 13.9 us -> 13.5 us  [swap(): return lax.ppermute(x, axis, [(i, i ^ mask) for i in range(size)])]
  transfers between devices with their start and end apart: 13 -> 13, of which waited for: 5 -> 7; matrix products, arithmetic and copies ran while one was open for 2% -> 0% of each run, Pallas kernels for 22% -> 16%
where the time goes in v3:
time: 33 us; the launch traced here: 32.7 us
  starting transfers between devices  13.5 us (41%)
  waiting for transfers between devices  9.01 us (27%)
  Pallas kernels  6.17 us (19%)
  local copies, waits for them, and re-layouts  1.63 us (5%)
  matrix products  1.05 us (3%)
  other arithmetic  0.72 us (2%)
  between operations  0.7 us (2%)
    ppermute x13, starting transfers between devices, swap(): return lax.ppermute(x, axis, [(i, i ^ mask) for i in range(size)])  13.5 us
    ppermute x13, waiting for transfers between devices, swap(): return lax.ppermute(x, axis, [(i, i ^ mask) for i in range(size)])  9.01 us
    pallas_call x1, Pallas kernels, local(): pl.pallas_call(functools.partial(prep_kernel, n_row, n_col, per), in_spec...  3.36 us
    pallas_call x1, Pallas kernels, local(): pl.pallas_call(functools.partial(scores_kernel, n_row, per), in_specs=[sc...  1.86 us
    unnamed x6, local copies, waits for them, and re-layouts  1.63 us
    dot_general x1, matrix products, local(): lax.dot_general(out_grad, weight, (((1,), (1,)), ((), ())), preferred_ele...  1.05 us
    pallas_call x1, Pallas kernels, local(): pl.pallas_call(functools.partial(sums_kernel, n_row, n_col, per), in_spec...  0.95 us
    convert_element_type x1, other arithmetic, local(): return (edge_grad, total.astype(jnp.bfloat16))  0.72 us
  transfers between devices with their start and end apart: 13, of which 7 were waited for; matrix products, arithmetic and copies ran while one was open for 0% of the time, Pallas kernels for 16%

profile of v3, /device:TPU:0, one launch (start us, length us, event | category | flops | bytes accessed | tf_op | source)
XLA Modules:
  0.0 32.7 jit_solution(2072881145386750193)
XLA Ops:
  0.6 0.0 copy-start
  0.6 0.9 %copy-done = bf16[512,256]{1,0:T(8,128)(2,1)S(1)} copy-done((bf16[512,256]{1,0:T(8,128)(2,1)S(1)}, bf16[512,256]{1,0:T(8,128)(2,1)}, u32[]{:S(2)}) %copy-start) | copy-done | bytes 262168
  1.6 1.1 %convolution_convert_fusion.refs_2_ = bf16[512,128]{1,0:T(8,128)(2,1)S(1)} fusion(bf16[512,256]{1,0:T(8,128)(2,1)S(1)} %copy-done, bf16[128,256]{1,0:T(8,128)(2,1)} %param.7), kind=kOutput, calls=%fused_computation | convolution fusion | flops 33619968 | bytes 458752 | tf_op jit(solution)/shard_map/dot_general | solution.py:117
  2.6 0.5 %collective-permute-start = (bf16[512,128]{1,0:T(8,128)(2,1)S(1)}, bf16[512,128]{1,0:T(8,128)(2,1)S(1)}, u32[]{:S(2)}, u32[]{:S(2)}) collective-permute-start(bf16[512,128]{1,0:T(8,128)(2,1)S(1)} %convolution_convert_fusion.refs_2_), channel_id=1, source_target_pairs={{0,1},{1,0},{2,3},{3,2},{4,5},{5,4},{6,7},{7,6},{8,9},{9,8},{10,11... | collective-permute-start | bytes 393224 | tf_op jit(solution)/shard_map/ppermute | solution.py:26
  3.2 4.7 %collective-permute-start.3 = (bf16[512,128]{1,0:T(8,128)(2,1)S(1)}, bf16[512,128]{1,0:T(8,128)(2,1)S(1)}, u32[]{:S(2)}, u32[]{:S(2)}) collective-permute-start(bf16[512,128]{1,0:T(8,128)(2,1)S(1)} %convolution_convert_fusion.refs_2_), channel_id=1, source_target_pairs={{0,6},{1,7},{2,4},{3,5},{4,2},{5,3},{6,0},{7,1},{8,14},{9,15},{10,... | collective-permute-start | bytes 393224 | tf_op jit(solution)/shard_map/ppermute | solution.py:26
  7.8 0.0 collective-permute-start.2
  7.9 0.6 %collective-permute-start.1 = (bf16[512,128]{1,0:T(8,128)(2,1)S(1)}, bf16[512,128]{1,0:T(8,128)(2,1)S(1)}, u32[]{:S(2)}, u32[]{:S(2)}) collective-permute-start(bf16[512,128]{1,0:T(8,128)(2,1)S(1)} %convolution_convert_fusion.refs_2_), channel_id=1, source_target_pairs={{0,2},{1,3},{2,0},{3,1},{4,6},{5,7},{6,4},{7,5},{8,10},{9,11},{10,... | collective-permute-start | bytes 393224 | tf_op jit(solution)/shard_map/ppermute | solution.py:26
  8.5 2.6 %collective-permute-start.9 = (bf16[512,128]{1,0:T(8,128)(2,1)}, bf16[512,128]{1,0:T(8,128)(2,1)S(1)}, u32[]{:S(2)}, u32[]{:S(2)}) collective-permute-start(bf16[512,128]{1,0:T(8,128)(2,1)} %refs_3_), channel_id=1, source_target_pairs={{0,24},{8,16},{16,8},{24,0},{1,25},{9,17},{17,9},{25,1},{2,26},{10... | collective-permute-start | bytes 393224 | tf_op jit(solution)/shard_map/ppermute | solution.py:26
  11.1 0.0 collective-permute-done.refs_3_
  11.1 0.5 %collective-permute-start.8 = (bf16[512,128]{1,0:T(8,128)(2,1)}, bf16[512,128]{1,0:T(8,128)(2,1)S(1)}, u32[]{:S(2)}, u32[]{:S(2)}) collective-permute-start(bf16[512,128]{1,0:T(8,128)(2,1)} %refs_3_), channel_id=1, source_target_pairs={{0,16},{8,24},{16,0},{24,8},{1,17},{9,25},{17,1},{25,9},{2,18},{10... | collective-permute-start | bytes 393224 | tf_op jit(solution)/shard_map/ppermute | solution.py:26
  11.6 0.0 copy-start.2
  11.6 0.7 %copy-done.2 = s32[1,1,64,3]{2,1,3,0:T(1,128)S(1)} copy-done((s32[1,1,64,3]{2,1,3,0:T(1,128)S(1)}, s32[1,1,64,3]{2,1,3,0:T(1,128)}, u32[]{:S(2)}) %copy-start.2) | copy-done | bytes 792
  12.3 0.0 copy-start.1
  12.3 3.4 %prep.1 = (bf16[64,128,128]{2,1,0:T(8,128)(2,1)S(1)}, bf16[64,128,128]{2,1,0:T(8,128)(2,1)S(1)}, s32[128]{0:T(128)S(4)}) custom-call(s32[1,3,1,64]{3,2,1,0:T(1,128)S(1)} %bitcast.3, s32[1,1,64,128,128]{4,3,2,1,0:T(8,128)} %mask.1, bf16[1,1,64,128,128]{4,3,2,1,0:T(8,128)(2,1)} %weights.1), custom_call_target="tpu_custom_call" | custom-call | bytes 6291456 | tf_op jit(solution)/shard_map/prep/pallas_call | solution.py:128
  15.6 0.0 collective-permute-done.3.refs_8_
  15.6 0.0 copy-done.1
  15.7 0.5 %collective-permute-start.7 = (bf16[512,128]{1,0:T(8,128)(2,1)S(1)}, bf16[512,128]{1,0:T(8,128)(2,1)S(1)}, u32[]{:S(2)}, u32[]{:S(2)}) collective-permute-start(bf16[512,128]{1,0:T(8,128)(2,1)S(1)} %copy-done.1), channel_id=1, source_target_pairs={{0,8},{8,0},{16,24},{24,16},{1,9},{9,1},{17,25},{25,17},{2,10},{10... | collective-permute-start | bytes 393224 | tf_op jit(solution)/shard_map/ppermute | solution.py:26
  16.1 3.4 %collective-permute-done.2.refs_6_ = bf16[512,128]{1,0:T(8,128)(2,1)S(1)} collective-permute-done((bf16[512,128]{1,0:T(8,128)(2,1)S(1)}, bf16[512,128]{1,0:T(8,128)(2,1)S(1)}, u32[]{:S(2)}, u32[]{:S(2)}) %collective-permute-start.2) | collective-permute-done | bytes 131104 | tf_op jit(solution)/shard_map/ppermute | solution.py:26
  19.5 0.0 collective-permute-done.1.refs_4_
  19.5 0.0 collective-permute-start.4
  19.5 0.5 %collective-permute-start.5 = (bf16[512,128]{1,0:T(8,128)(2,1)S(1)}, bf16[512,128]{1,0:T(8,128)(2,1)S(1)}, u32[]{:S(2)}, u32[]{:S(2)}) collective-permute-start(bf16[512,128]{1,0:T(8,128)(2,1)S(1)} %collective-permute-done.2.refs_6_), channel_id=1, source_target_pairs={{0,1},{1,0},{2,3},{3,2},{4,5},{5,4},{6,7},{7,6},{8,9},{9,8},{10,11... | collective-permute-start | bytes 393224 | tf_op jit(solution)/shard_map/ppermute | solution.py:26
  20.0 0.0 collective-permute-done.9.refs_6_
  20.1 0.0 collective-permute-start.6
  20.1 0.0 collective-permute-done.8.refs_5_
  20.1 0.6 %collective-permute-done.7.refs_4_ = bf16[512,128]{1,0:T(8,128)(2,1)S(1)} collective-permute-done((bf16[512,128]{1,0:T(8,128)(2,1)S(1)}, bf16[512,128]{1,0:T(8,128)(2,1)S(1)}, u32[]{:S(2)}, u32[]{:S(2)}) %collective-permute-start.7) | collective-permute-done | bytes 131104 | tf_op jit(solution)/shard_map/ppermute | solution.py:26
  20.7 0.2 collective-permute-done.4.refs_5_
  20.9 0.2 collective-permute-done.5.refs_7_
  21.1 0.3 collective-permute-done.6.refs_9_
  21.4 1.0 %sums.1 = (bf16[32,128,128]{2,1,0:T(8,128)(2,1)S(1)}, f32[512,128]{1,0:T(8,128)S(1)}, bf16[512,128]{1,0:T(8,128)(2,1)S(1)}, bf16[512,128]{1,0:T(8,128)(2,1)S(1)}, bf16[512,128]{1,0:T(8,128)(2,1)S(1)}) custom-call(s32[128]{0:T(128)S(4)} %get-tuple-element.31.refs_0_, bf16[64,128,128]{2,1,0:T(8,128)(2,1)S(1)} %get-tuple-element.34.refs_1_, ...), custom_call_target="tpu_custom_call" | custom-call | flops 268435456 | bytes 4194304 | tf_op jit(solution)/shard_map/sums/pallas_call | solution.py:153
  22.4 1.6 %collective-permute-start.10 = (bf16[512,128]{1,0:T(8,128)(2,1)S(1)}, bf16[512,128]{1,0:T(8,128)(2,1)S(1)}, u32[]{:S(2)}, u32[]{:S(2)}) collective-permute-start(bf16[512,128]{1,0:T(8,128)(2,1)S(1)} %get-tuple-element.55), channel_id=1, source_target_pairs={{0,8},{8,0},{16,24},{24,16},{1,9},{9,1},{17,25},{25,17},{2,10},{10... | collective-permute-start | bytes 393224 | tf_op jit(solution)/shard_map/ppermute | solution.py:26
  23.9 1.5 %collective-permute-start.11 = (bf16[512,128]{1,0:T(8,128)(2,1)S(1)}, bf16[512,128]{1,0:T(8,128)(2,1)S(1)}, u32[]{:S(2)}, u32[]{:S(2)}) collective-permute-start(bf16[512,128]{1,0:T(8,128)(2,1)S(1)} %get-tuple-element.56), channel_id=1, source_target_pairs={{0,16},{8,24},{16,0},{24,8},{1,17},{9,25},{17,1},{25,9},{2,18},{10... | collective-permute-start | bytes 393224 | tf_op jit(solution)/shard_map/ppermute | solution.py:26
  25.4 0.5 %collective-permute-start.12 = (bf16[512,128]{1,0:T(8,128)(2,1)S(1)}, bf16[512,128]{1,0:T(8,128)(2,1)S(1)}, u32[]{:S(2)}, u32[]{:S(2)}) collective-permute-start(bf16[512,128]{1,0:T(8,128)(2,1)S(1)} %get-tuple-element.57), channel_id=1, source_target_pairs={{0,24},{8,16},{16,8},{24,0},{1,25},{9,17},{17,9},{25,1},{2,26},{10... | collective-permute-start | bytes 393224 | tf_op jit(solution)/shard_map/ppermute | solution.py:26
  25.9 1.9 %scores.1 = bf16[1,1,64,128,128]{4,3,2,1,0:T(8,128)(2,1)} custom-call(s32[128]{0:T(128)S(4)} %get-tuple-element.31.refs_0_, bf16[32,128,128]{2,1,0:T(8,128)(2,1)S(1)} %get-tuple-element.49.refs_1_, bf16[64,128,128]{2,1,0:T(8,128)(2,1)S(1)} %get-tuple-element.50.refs_2_, bf16[512,128]{1,0:T(8,128)(2,1)S(1)} %copy-done.1, ...), custom_call_target="tpu_custom_call" | custom-call | flops 268435456 | bytes 4194304 | tf_op jit(solution)/shard_map/scores/pallas_call | solution.py:167
  27.8 0.6 %collective-permute-done.10 = bf16[512,128]{1,0:T(8,128)(2,1)S(1)} collective-permute-done((bf16[512,128]{1,0:T(8,128)(2,1)S(1)}, bf16[512,128]{1,0:T(8,128)(2,1)S(1)}, u32[]{:S(2)}, u32[]{:S(2)}) %collective-permute-start.10) | collective-permute-done | bytes 131104 | tf_op jit(solution)/shard_map/ppermute | solution.py:26
  28.4 3.6 %collective-permute-done.11 = bf16[512,128]{1,0:T(8,128)(2,1)S(1)} collective-permute-done((bf16[512,128]{1,0:T(8,128)(2,1)S(1)}, bf16[512,128]{1,0:T(8,128)(2,1)S(1)}, u32[]{:S(2)}, u32[]{:S(2)}) %collective-permute-start.11) | collective-permute-done | bytes 131104 | tf_op jit(solution)/shard_map/ppermute | solution.py:26
  32.0 0.0 collective-permute-done.12
  32.0 0.7 %add_convert_fusion = bf16[512,128]{1,0:T(8,128)(2,1)} fusion(bf16[512,128]{1,0:T(8,128)(2,1)S(1)} %collective-permute-done.12, bf16[512,128]{1,0:T(8,128)(2,1)S(1)} %collective-permute-done.11, f32[512,128]{1,0:T(8,128)S(1)} %get-tuple-element.54, bf16[512,128]{1,0:T(8,128)(2,1)S(1)} %collective-permute-done.10), kind=kLoop, calls=%fused_computation.1 | loop fusion | flops 458752 | bytes 786432 | tf_op jit(solution)/shard_map/convert_element_type | solution.py:185
Async XLA Ops:
  0.6 1.0 %copy-start = (bf16[512,256]{1,0:T(8,128)(2,1)S(1)}, bf16[512,256]{1,0:T(8,128)(2,1)}, u32[]{:S(2)}) copy-start(bf16[512,256]{1,0:T(8,128)(2,1)} %param.8) | copy-start | bytes 786436
  2.6 8.4 %collective-permute-start = (bf16[512,128]{1,0:T(8,128)(2,1)S(1)}, bf16[512,128]{1,0:T(8,128)(2,1)S(1)}, u32[]{:S(2)}, u32[]{:S(2)}) collective-permute-start(bf16[512,128]{1,0:T(8,128)(2,1)S(1)} %convolution_convert_fusion.refs_2_), channel_id=1, source_target_pairs={{0,1},{1,0},{2,3},{3,2},{4,5},{5,4},{6,7},{7,6},{8,9},{9,8},{10,11... | collective-permute-start | bytes 393224 | tf_op jit(solution)/shard_map/ppermute | solution.py:26
  3.2 12.5 %collective-permute-start.3 = (bf16[512,128]{1,0:T(8,128)(2,1)S(1)}, bf16[512,128]{1,0:T(8,128)(2,1)S(1)}, u32[]{:S(2)}, u32[]{:S(2)}) collective-permute-start(bf16[512,128]{1,0:T(8,128)(2,1)S(1)} %convolution_convert_fusion.refs_2_), channel_id=1, source_target_pairs={{0,6},{1,7},{2,4},{3,5},{4,2},{5,3},{6,0},{7,1},{8,14},{9,15},{10,... | collective-permute-start | bytes 393224 | tf_op jit(solution)/shard_map/ppermute | solution.py:26
  7.8 11.7 %collective-permute-start.2 = (bf16[512,128]{1,0:T(8,128)(2,1)S(1)}, bf16[512,128]{1,0:T(8,128)(2,1)S(1)}, u32[]{:S(2)}, u32[]{:S(2)}) collective-permute-start(bf16[512,128]{1,0:T(8,128)(2,1)S(1)} %convolution_convert_fusion.refs_2_), channel_id=1, source_target_pairs={{0,4},{1,5},{2,6},{3,7},{4,0},{5,1},{6,2},{7,3},{8,12},{9,13},{10,... | collective-permute-start | bytes 393224 | tf_op jit(solution)/shard_map/ppermute | solution.py:26
  7.9 11.7 %collective-permute-start.1 = (bf16[512,128]{1,0:T(8,128)(2,1)S(1)}, bf16[512,128]{1,0:T(8,128)(2,1)S(1)}, u32[]{:S(2)}, u32[]{:S(2)}) collective-permute-start(bf16[512,128]{1,0:T(8,128)(2,1)S(1)} %convolution_convert_fusion.refs_2_), channel_id=1, source_target_pairs={{0,2},{1,3},{2,0},{3,1},{4,6},{5,7},{6,4},{7,5},{8,10},{9,11},{10,... | collective-permute-start | bytes 393224 | tf_op jit(solution)/shard_map/ppermute | solution.py:26
  8.5 11.6 %collective-permute-start.9 = (bf16[512,128]{1,0:T(8,128)(2,1)}, bf16[512,128]{1,0:T(8,128)(2,1)S(1)}, u32[]{:S(2)}, u32[]{:S(2)}) collective-permute-start(bf16[512,128]{1,0:T(8,128)(2,1)} %refs_3_), channel_id=1, source_target_pairs={{0,24},{8,16},{16,8},{24,0},{1,25},{9,17},{17,9},{25,1},{2,26},{10... | collective-permute-start | bytes 393224 | tf_op jit(solution)/shard_map/ppermute | solution.py:26
  11.1 9.0 %collective-permute-start.8 = (bf16[512,128]{1,0:T(8,128)(2,1)}, bf16[512,128]{1,0:T(8,128)(2,1)S(1)}, u32[]{:S(2)}, u32[]{:S(2)}) collective-permute-start(bf16[512,128]{1,0:T(8,128)(2,1)} %refs_3_), channel_id=1, source_target_pairs={{0,16},{8,24},{16,0},{24,8},{1,17},{9,25},{17,1},{25,9},{2,18},{10... | collective-permute-start | bytes 393224 | tf_op jit(solution)/shard_map/ppermute | solution.py:26
  11.6 0.7 %copy-start.2 = (s32[1,1,64,3]{2,1,3,0:T(1,128)S(1)}, s32[1,1,64,3]{2,1,3,0:T(1,128)}, u32[]{:S(2)}) copy-start(s32[1,1,64,3]{2,1,3,0:T(1,128)} %param.9) | copy-start | bytes 2308
  12.3 3.4 %copy-start.1 = (bf16[512,128]{1,0:T(8,128)(2,1)S(1)}, bf16[512,128]{1,0:T(8,128)(2,1)}, u32[]{:S(2)}) copy-start(bf16[512,128]{1,0:T(8,128)(2,1)} %refs_3_) | copy-start | bytes 393220
  15.7 5.0 %collective-permute-start.7 = (bf16[512,128]{1,0:T(8,128)(2,1)S(1)}, bf16[512,128]{1,0:T(8,128)(2,1)S(1)}, u32[]{:S(2)}, u32[]{:S(2)}) collective-permute-start(bf16[512,128]{1,0:T(8,128)(2,1)S(1)} %copy-done.1), channel_id=1, source_target_pairs={{0,8},{8,0},{16,24},{24,16},{1,9},{9,1},{17,25},{25,17},{2,10},{10... | collective-permute-start | bytes 393224 | tf_op jit(solution)/shard_map/ppermute | solution.py:26
  19.5 1.3 %collective-permute-start.4 = (bf16[512,128]{1,0:T(8,128)(2,1)S(1)}, bf16[512,128]{1,0:T(8,128)(2,1)S(1)}, u32[]{:S(2)}, u32[]{:S(2)}) collective-permute-start(bf16[512,128]{1,0:T(8,128)(2,1)S(1)} %collective-permute-done.1.refs_4_), channel_id=1, source_target_pairs={{0,1},{1,0},{2,3},{3,2},{4,5},{5,4},{6,7},{7,6},{8,9},{9,8},{10,11... | collective-permute-start | bytes 393224 | tf_op jit(solution)/shard_map/ppermute | solution.py:26
  19.5 1.5 %collective-permute-start.5 = (bf16[512,128]{1,0:T(8,128)(2,1)S(1)}, bf16[512,128]{1,0:T(8,128)(2,1)S(1)}, u32[]{:S(2)}, u32[]{:S(2)}) collective-permute-start(bf16[512,128]{1,0:T(8,128)(2,1)S(1)} %collective-permute-done.2.refs_6_), channel_id=1, source_target_pairs={{0,1},{1,0},{2,3},{3,2},{4,5},{5,4},{6,7},{7,6},{8,9},{9,8},{10,11... | collective-permute-start | bytes 393224 | tf_op jit(solution)/shard_map/ppermute | solution.py:26
  20.1 1.3 %collective-permute-start.6 = (bf16[512,128]{1,0:T(8,128)(2,1)S(1)}, bf16[512,128]{1,0:T(8,128)(2,1)S(1)}, u32[]{:S(2)}, u32[]{:S(2)}) collective-permute-start(bf16[512,128]{1,0:T(8,128)(2,1)S(1)} %collective-permute-done.3.refs_8_), channel_id=1, source_target_pairs={{0,1},{1,0},{2,3},{3,2},{4,5},{5,4},{6,7},{7,6},{8,9},{9,8},{10,11... | collective-permute-start | bytes 393224 | tf_op jit(solution)/shard_map/ppermute | solution.py:26
  22.4 6.0 %collective-permute-start.10 = (bf16[512,128]{1,0:T(8,128)(2,1)S(1)}, bf16[512,128]{1,0:T(8,128)(2,1)S(1)}, u32[]{:S(2)}, u32[]{:S(2)}) collective-permute-start(bf16[512,128]{1,0:T(8,128)(2,1)S(1)} %get-tuple-element.55), channel_id=1, source_target_pairs={{0,8},{8,0},{16,24},{24,16},{1,9},{9,1},{17,25},{25,17},{2,10},{10... | collective-permute-start | bytes 393224 | tf_op jit(solution)/shard_map/ppermute | solution.py:26
  23.9 8.1 %collective-permute-start.11 = (bf16[512,128]{1,0:T(8,128)(2,1)S(1)}, bf16[512,128]{1,0:T(8,128)(2,1)S(1)}, u32[]{:S(2)}, u32[]{:S(2)}) collective-permute-start(bf16[512,128]{1,0:T(8,128)(2,1)S(1)} %get-tuple-element.56), channel_id=1, source_target_pairs={{0,16},{8,24},{16,0},{24,8},{1,17},{9,25},{17,1},{25,9},{2,18},{10... | collective-permute-start | bytes 393224 | tf_op jit(solution)/shard_map/ppermute | solution.py:26
  25.4 6.6 %collective-permute-start.12 = (bf16[512,128]{1,0:T(8,128)(2,1)S(1)}, bf16[512,128]{1,0:T(8,128)(2,1)S(1)}, u32[]{:S(2)}, u32[]{:S(2)}) collective-permute-start(bf16[512,128]{1,0:T(8,128)(2,1)S(1)} %get-tuple-element.57), channel_id=1, source_target_pairs={{0,24},{8,16},{16,8},{24,0},{1,25},{9,17},{17,9},{25,1},{2,26},{10... | collective-permute-start | bytes 393224 | tf_op jit(solution)/shard_map/ppermute | solution.py:26

commit v4 on v3

--- a/solution.py
+++ b/solution.py
@@ -26,11 +26,33 @@
     return lax.ppermute(x, axis, [(i, i ^ mask) for i in range(size)])
 
 
+def swap_rows(x, n_row, n_col, even, odd):
+    places = [(r, c) for r in range(n_row) for c in range(n_col)]
+    pairs = [(r * n_col + c, (r ^ (odd if c % 2 else even)) * n_col + c) for r, c in places]
+    return lax.ppermute(x, ("row", "col"), pairs)
+
+
+def hidden_kernel(grads, weight, out, grad_buf, weight_buf, sems):
+    copies = [
+        pltpu.make_async_copy(grads, grad_buf, sems.at[0]),
+        pltpu.make_async_copy(weight, weight_buf, sems.at[1]),
+    ]
+    for copy in copies:
+        copy.start()
+    for copy in copies:
+        copy.wait()
+    out[...] = lax.dot_general(
+        grad_buf[...], weight_buf[...], (((1,), (1,)), ((), ())), preferred_element_type=jnp.float32
+    ).astype(out.dtype)
+
+
 def prep_kernel(n_row, n_col, per, index, mask, weights, keep_out, adj_out, places, table, mask_buf, weight_buf, sems, table_sem):
     tiles = mask_buf.shape[0]
     groups = tiles // GROUP
     me = lax.axis_index("col")
     row = lax.axis_index("row")
+    core = me % 2
+    bits = n_row.bit_length() - 1
 
     def fetch(g):
         span = pl.ds(pl.multiple_of(g * GROUP, GROUP), GROUP)
@@ -52,7 +74,10 @@
             a = table[0, 0, 0, t]
             b = table[0, 1, 0, t]
             places[t] = ((a // per) ^ me) * per + a % per
-            places[tiles + t] = ((b // per) ^ row) * per + b % per
+            off = (b // per) ^ row
+            back = sum(((off >> i) & 1) << (bits - 1 - i) for i in range(bits))
+            places[tiles + t] = off * per + b % per
+            places[2 * tiles + t] = (off + core * (back - off)) * per + b % per
         for copy in fetch(g):
             copy.wait()
         for i in range(GROUP):
@@ -83,18 +108,14 @@
             outs[s][i * BLOCK : (i + 1) * BLOCK, :] = total[s * per + i].astype(outs[s].dtype)
 
 
-def scores_kernel(n_row, per, *refs):
-    places, panel, keep = refs[:3]
-    slots = refs[3 : 3 + n_row]
-    out, cols, stage, sems = refs[3 + n_row :]
+def scores_kernel(places, panel, keep, features, out, cols, stage, sems):
     tiles = keep.shape[0]
-    for s in range(n_row):
-        for i in range(per):
-            cols[s * per + i] = slots[s][i * BLOCK : (i + 1) * BLOCK, :].T
+    for i in range(cols.shape[0]):
+        cols[i] = features[i * BLOCK : (i + 1) * BLOCK, :].T
     copies = []
     for g in range(tiles // GROUP):
         for t in range(g * GROUP, (g + 1) * GROUP):
-            found = jnp.dot(panel[places[t]], cols[places[tiles + t]], preferred_element_type=jnp.float32)
+            found = jnp.dot(panel[places[t]], cols[places[2 * tiles + t]], preferred_element_type=jnp.float32)
             stage[t] = found.astype(jnp.bfloat16) * keep[t]
         span = pl.ds(g * GROUP, GROUP)
         copies.append(pltpu.make_async_copy(stage.at[span], out.at[0, 0, span], sems.at[g]))
@@ -114,22 +135,35 @@
     tile_set = VMEM((tiles, BLOCK, BLOCK), jnp.bfloat16)
     product_flops = 2 * tiles * BLOCK * BLOCK * fin
 
-    hidden = lax.dot_general(
-        out_grad, weight, (((1,), (1,)), ((), ())), preferred_element_type=jnp.float32
-    ).astype(jnp.bfloat16)
-
-    near = [swap(hidden, "col", n_col, s) for s in range(2, n_col, 2)]
-    beside = swap(hidden, "col", n_col, 1)
+    hidden = pl.pallas_call(
+        hidden_kernel,
+        in_specs=[far, far],
+        out_specs=whole,
+        out_shape=VMEM((nodes, fin), jnp.bfloat16),
+        scratch_shapes=[
+            VMEM(out_grad.shape, out_grad.dtype),
+            VMEM(weight.shape, weight.dtype),
+            pltpu.SemaphoreType.DMA((2,)),
+        ],
+        compiler_params=params,
+        name="hidden",
+    )(in_hbm(out_grad), in_hbm(weight))
+
+    masks = [1 << i for i in reversed(range(1, n_col.bit_length() - 1))]
+    shards = {0: hidden}
+    for mask in masks:
+        shards[mask] = swap(hidden, "col", n_col, mask)
     features, hidden = lax.optimization_barrier((features, hidden))
-    cols = [swap(features, "row", n_row, s) for s in range(1, n_row)]
+    bits = [1 << i for i in range(n_row.bit_length() - 1)]
+    stages = list(zip(bits, reversed(bits), strict=True))
+    cols = [features, swap_rows(features, n_row, n_col, *stages[0])]
 
     index = jnp.transpose(tile_index, (0, 3, 1, 2))
-    index, beside = lax.optimization_barrier((index, beside))
     keep, adj, places = pl.pallas_call(
         functools.partial(prep_kernel, n_row, n_col, per),
         in_specs=[far, far, far],
         out_specs=[whole, whole, scalars],
-        out_shape=[tile_set, tile_set, SMEM((2 * tiles,), jnp.int32)],
+        out_shape=[tile_set, tile_set, SMEM((3 * tiles,), jnp.int32)],
         scratch_shapes=[
             SMEM(index.shape, jnp.int32),
             VMEM((tiles, BLOCK, BLOCK), jnp.int32),
@@ -137,18 +171,22 @@
             pltpu.SemaphoreType.DMA((2, tiles // GROUP)),
             pltpu.SemaphoreType.DMA,
         ],
-        cost_estimate=pl.CostEstimate(flops=0, bytes_accessed=6 * tiles * BLOCK * BLOCK, transcendentals=0),
+        cost_estimate=pl.CostEstimate(flops=0, bytes_accessed=4096, transcendentals=0),
         compiler_params=params,
         name="prep",
-    )(index, in_hbm(edge_mask), in_hbm(edge_weight))
+    )(in_hbm(index), in_hbm(edge_mask), in_hbm(edge_weight))
     places = pltpu.with_memory_space_constraint(places, SMEM)
 
-    near, keep, adj = lax.optimization_barrier((near, keep, adj))
-    slots = [None] * n_col
-    slots[::2] = [hidden] + near
-    slots[1::2] = [beside] + [swap(x, "col", n_col, 1) for x in near]
-    slots, cols = lax.optimization_barrier((slots, cols))
-    cols = [features] + cols
+    shards[masks[0]], hidden, keep, adj = lax.optimization_barrier((shards[masks[0]], hidden, keep, adj))
+    shards[0] = hidden
+    for i, mask in enumerate(masks[1:], 1):
+        for s in range(masks[i - 1], n_col, masks[i - 1]):
+            shards[s ^ mask] = swap(shards[s], "col", n_col, mask)
+    cols = jnp.concatenate(cols)
+    for stage in stages[1:]:
+        cols = jnp.concatenate([cols, swap_rows(cols, n_row, n_col, *stage)])
+    slots = [shards[s] for s in range(0, n_col, 2)]
+    slots = [x for shard in slots for x in (shard, swap(shard, "col", n_col, 1))]
 
     panel, own, *parts = pl.pallas_call(
         functools.partial(sums_kernel, n_row, n_col, per),
@@ -157,16 +195,17 @@
         out_shape=[VMEM((n_col * per, BLOCK, fin), jnp.bfloat16), VMEM((nodes, fin), jnp.float32)]
         + [VMEM((nodes, fin), jnp.bfloat16)] * (n_row - 1),
         scratch_shapes=[VMEM((n_row * per, BLOCK, fin), jnp.float32)],
-        cost_estimate=pl.CostEstimate(flops=product_flops, bytes_accessed=4 << 20, transcendentals=0),
+        cost_estimate=pl.CostEstimate(flops=0, bytes_accessed=4096, transcendentals=0),
         compiler_params=params,
         name="sums",
     )(places, *map(in_vmem, (adj, *slots)))
 
-    got = [swap(part, "row", n_row, s + 1) for s, part in enumerate(parts)]
+    order = sorted(range(1, n_row), key=lambda s: -s.bit_count())
+    got = [swap(parts[s - 1], "row", n_row, s) for s in order]
 
     edge_grad = pl.pallas_call(
-        functools.partial(scores_kernel, n_row, per),
-        in_specs=[scalars] + [whole] * (2 + n_row),
+        scores_kernel,
+        in_specs=[scalars] + [whole] * 3,
         out_specs=far,
         out_shape=jax.ShapeDtypeStruct(edge_weight.shape, jnp.bfloat16),
         scratch_shapes=[
@@ -177,7 +216,7 @@
         cost_estimate=pl.CostEstimate(flops=product_flops, bytes_accessed=4 << 20, transcendentals=0),
         compiler_params=params,
         name="scores",
-    )(places, *map(in_vmem, (panel, keep, *cols)))
+    )(places, *map(in_vmem, (panel, keep, cols)))
 
     total = own
     for part in got:

time: 33 us -> 30.2 us (0.915)
  local copies, waits for them, and re-layouts: 1.63 us -> 0.01 us
  Pallas kernels: 6.17 us -> 7.56 us
  waiting for transfers between devices: 9.01 us -> 7.66 us
  matrix products: 1.05 us -> 0 us
    ppermute x13 -> x10, starting transfers between devices: 13.5 us -> 10.3 us  [swap(): return lax.ppermute(x, axis, [(i, i ^ mask) for i in range(size)])]
    ppermute x0 -> x2, starting transfers between devices: none -> 3.07 us  [swap_rows(): return lax.ppermute(x, ('row', 'col'), pairs)]
    unnamed x6 -> x2, local copies, waits for them, and re-layouts: 1.63 us -> 0.01 us
    ppermute x13 -> x10, waiting for transfers between devices: 9.01 us -> 7.66 us  [swap(): return lax.ppermute(x, axis, [(i, i ^ mask) for i in range(size)])]
    pallas_call x1 -> x2, Pallas kernels: 1.86 us -> 3.06 us  [the longest x1 1.86 us: local(): pl.pallas_call(scores_kernel, in_specs=[scalars] + [whole] * 3, out_specs...]
    dot_general x1 -> x0, matrix products: 1.05 us -> none  [local(): lax.dot_general(out_grad, weight, (((1,), (1,)), ((), ())), preferred_ele...]
  transfers between devices with their start and end apart: 13 -> 12, of which waited for: 7 -> 5; matrix products, arithmetic and copies ran while one was open for 0% -> 0% of each run, Pallas kernels for 16% -> 21%
where the time goes in v4:
time: 30.2 us; the launch traced here: 30 us
  starting transfers between devices  13.3 us (44%)
  waiting for transfers between devices  7.66 us (25%)
  Pallas kernels  7.56 us (25%)
  other arithmetic  0.77 us (3%)
  between operations  0.7 us (2%)
    ppermute x10, starting transfers between devices, swap(): return lax.ppermute(x, axis, [(i, i ^ mask) for i in range(size)])  10.3 us
    ppermute x10, waiting for transfers between devices, swap(): return lax.ppermute(x, axis, [(i, i ^ mask) for i in range(size)])  7.66 us
    pallas_call x1, Pallas kernels, local(): pl.pallas_call(functools.partial(prep_kernel, n_row, n_col, per), in_spec...  3.55 us
    ppermute x2, starting transfers between devices, swap_rows(): return lax.ppermute(x, ('row', 'col'), pairs)  3.07 us
    pallas_call x1, Pallas kernels, local(): pl.pallas_call(scores_kernel, in_specs=[scalars] + [whole] * 3, out_specs...  1.86 us
    pallas_call x1, Pallas kernels, local(): pl.pallas_call(hidden_kernel, in_specs=[far, far], out_specs=whole, out_s...  1.19 us
    pallas_call x1, Pallas kernels, local(): pl.pallas_call(functools.partial(sums_kernel, n_row, n_col, per), in_spec...  0.95 us
    convert_element_type x1, other arithmetic, local(): return (edge_grad, total.astype(jnp.bfloat16))  0.72 us
  transfers between devices with their start and end apart: 12, of which 5 were waited for; matrix products, arithmetic and copies ran while one was open for 0% of the time, Pallas kernels for 21%

profile of v4, /device:TPU:0, one launch (start us, length us, event | category | flops | bytes accessed | tf_op | source)
XLA Modules:
  0.0 30.0 jit_solution(13848573035837389410)
XLA Ops:
  0.6 1.2 %hidden.1.refs_2_ = bf16[512,128]{1,0:T(8,128)(2,1)S(1)} custom-call(bf16[512,256]{1,0:T(8,128)(2,1)} %grads.1, bf16[128,256]{1,0:T(8,128)(2,1)} %weight.1), custom_call_target="tpu_custom_call" | custom-call | tf_op jit(solution)/shard_map/hidden/pallas_call | solution.py:138
  1.8 4.1 %collective-permute-start = (bf16[512,128]{1,0:T(8,128)(2,1)S(1)}, bf16[512,128]{1,0:T(8,128)(2,1)S(1)}, u32[]{:S(2)}, u32[]{:S(2)}) collective-permute-start(bf16[512,128]{1,0:T(8,128)(2,1)S(1)} %hidden.1.refs_2_), channel_id=1, source_target_pairs={{0,4},{1,5},{2,6},{3,7},{4,0},{5,1},{6,2},{7,3},{8,12},{9,13},{10,... | collective-permute-start | bytes 393224 | tf_op jit(solution)/shard_map/ppermute | solution.py:26
  5.9 1.5 %collective-permute-start.7 = (bf16[512,128]{1,0:T(8,128)(2,1)}, bf16[512,128]{1,0:T(8,128)(2,1)S(1)}, u32[]{:S(2)}, u32[]{:S(2)}) collective-permute-start(bf16[512,128]{1,0:T(8,128)(2,1)} %param.6), channel_id=1, source_target_pairs={{0,8},{1,17},{2,10},{3,19},{4,12},{5,21},{6,14},{7,23},{8,0},{9,25... | collective-permute-start | bytes 393224 | tf_op jit(solution)/shard_map/ppermute | solution.py:32
  7.4 1.6 %collective-permute-start.2 = (bf16[512,128]{1,0:T(8,128)(2,1)S(1)}, bf16[512,128]{1,0:T(8,128)(2,1)S(1)}, u32[]{:S(2)}, u32[]{:S(2)}) collective-permute-start(bf16[512,128]{1,0:T(8,128)(2,1)S(1)} %hidden.1.refs_2_), channel_id=1, source_target_pairs={{0,2},{1,3},{2,0},{3,1},{4,6},{5,7},{6,4},{7,5},{8,10},{9,11},{10,... | collective-permute-start | bytes 393224 | tf_op jit(solution)/shard_map/ppermute | solution.py:26
  9.0 0.0 copy-start
  9.0 3.6 %prep.1 = (bf16[64,128,128]{2,1,0:T(8,128)(2,1)S(1)}, bf16[64,128,128]{2,1,0:T(8,128)(2,1)S(1)}, s32[192]{0:T(256)S(4)}) custom-call(s32[1,3,1,64]{3,2,1,0:T(1,128)} %bitcast.1, s32[1,1,64,128,128]{4,3,2,1,0:T(8,128)} %mask.1, bf16[1,1,64,128,128]{4,3,2,1,0:T(8,128)(2,1)} %weights.1), custom_call_target="tpu_custom_call" | custom-call | bytes 4096 | tf_op jit(solution)/shard_map/prep/pallas_call | solution.py:162
  12.6 0.0 collective-permute-done.refs_6_
  12.6 0.5 %collective-permute-start.5 = (bf16[512,128]{1,0:T(8,128)(2,1)S(1)}, bf16[512,128]{1,0:T(8,128)(2,1)S(1)}, u32[]{:S(2)}, u32[]{:S(2)}) collective-permute-start(bf16[512,128]{1,0:T(8,128)(2,1)S(1)} %collective-permute-done.refs_6_), channel_id=1, source_target_pairs={{0,2},{1,3},{2,0},{3,1},{4,6},{5,7},{6,4},{7,5},{8,10},{9,11},{10,... | collective-permute-start | bytes 393224 | tf_op jit(solution)/shard_map/ppermute | solution.py:26
  13.1 0.0 collective-permute-done.7
  13.1 0.0 copy-done
  13.1 1.6 %collective-permute-start.8 = (bf16[1024,128]{1,0:T(8,128)(2,1)S(1)}, bf16[1024,128]{1,0:T(8,128)(2,1)S(1)}, u32[]{:S(2)}, u32[]{:S(2)}) collective-permute-start(bf16[1024,128]{1,0:T(8,128)(2,1)S(1)} %pad_maximum_fusion.1), channel_id=1, source_target_pairs={{0,16},{1,9},{2,18},{3,11},{4,20},{5,13},{6,22},{7,15},{8,24},{9,1... | collective-permute-start | bytes 786440 | tf_op jit(solution)/shard_map/ppermute | solution.py:32
  14.7 0.0 collective-permute-start.4
  14.7 0.5 %collective-permute-start.1 = (bf16[512,128]{1,0:T(8,128)(2,1)S(1)}, bf16[512,128]{1,0:T(8,128)(2,1)S(1)}, u32[]{:S(2)}, u32[]{:S(2)}) collective-permute-start(bf16[512,128]{1,0:T(8,128)(2,1)S(1)} %hidden.1.refs_2_), channel_id=1, source_target_pairs={{0,1},{1,0},{2,3},{3,2},{4,5},{5,4},{6,7},{7,6},{8,9},{9,8},{10,11... | collective-permute-start | bytes 393224 | tf_op jit(solution)/shard_map/ppermute | solution.py:26
  15.2 0.0 collective-permute-done.2.refs_4_
  15.2 0.0 collective-permute-start.3
  15.2 2.4 %collective-permute-done.5.refs_8_ = bf16[512,128]{1,0:T(8,128)(2,1)S(1)} collective-permute-done((bf16[512,128]{1,0:T(8,128)(2,1)S(1)}, bf16[512,128]{1,0:T(8,128)(2,1)S(1)}, u32[]{:S(2)}, u32[]{:S(2)}) %collective-permute-start.5) | collective-permute-done | bytes 131104 | tf_op jit(solution)/shard_map/ppermute | solution.py:26
  17.6 0.0 collective-permute-start.6
  17.6 0.0 collective-permute-done.4.refs_7_
  17.6 0.0 collective-permute-done.1.refs_3_
  17.6 0.0 collective-permute-done.3.refs_5_
  17.6 1.3 %collective-permute-done.6.refs_9_ = bf16[512,128]{1,0:T(8,128)(2,1)S(1)} collective-permute-done((bf16[512,128]{1,0:T(8,128)(2,1)S(1)}, bf16[512,128]{1,0:T(8,128)(2,1)S(1)}, u32[]{:S(2)}, u32[]{:S(2)}) %collective-permute-start.6) | collective-permute-done | bytes 131104 | tf_op jit(solution)/shard_map/ppermute | solution.py:26
  19.0 1.0 %sums.1 = (bf16[32,128,128]{2,1,0:T(8,128)(2,1)S(1)}, f32[512,128]{1,0:T(8,128)S(1)}, bf16[512,128]{1,0:T(8,128)(2,1)S(1)}, bf16[512,128]{1,0:T(8,128)(2,1)S(1)}, bf16[512,128]{1,0:T(8,128)(2,1)S(1)}) custom-call(s32[192]{0:T(256)S(4)} %get-tuple-element.16.refs_0_.places, bf16[64,128,128]{2,1,0:T(8,128)(2,1)S(1)} %get-tuple-element.20.refs_1_, ...), custom_call_target="tpu_custom_call" | custom-call | bytes 4096 | tf_op jit(solution)/shard_map/sums/pallas_call | solution.py:191
  19.9 1.3 %collective-permute-start.10 = (bf16[512,128]{1,0:T(8,128)(2,1)S(1)}, bf16[512,128]{1,0:T(8,128)(2,1)S(1)}, u32[]{:S(2)}, u32[]{:S(2)}) collective-permute-start(bf16[512,128]{1,0:T(8,128)(2,1)S(1)} %get-tuple-element.28), channel_id=1, source_target_pairs={{0,8},{8,0},{16,24},{24,16},{1,9},{9,1},{17,25},{25,17},{2,10},{10... | collective-permute-start | bytes 393224 | tf_op jit(solution)/shard_map/ppermute | solution.py:26
  21.2 1.5 %collective-permute-start.11 = (bf16[512,128]{1,0:T(8,128)(2,1)S(1)}, bf16[512,128]{1,0:T(8,128)(2,1)S(1)}, u32[]{:S(2)}, u32[]{:S(2)}) collective-permute-start(bf16[512,128]{1,0:T(8,128)(2,1)S(1)} %get-tuple-element.29), channel_id=1, source_target_pairs={{0,16},{8,24},{16,0},{24,8},{1,17},{9,25},{17,1},{25,9},{2,18},{10... | collective-permute-start | bytes 393224 | tf_op jit(solution)/shard_map/ppermute | solution.py:26
  22.7 0.7 %collective-permute-start.9 = (bf16[512,128]{1,0:T(8,128)(2,1)S(1)}, bf16[512,128]{1,0:T(8,128)(2,1)S(1)}, u32[]{:S(2)}, u32[]{:S(2)}) collective-permute-start(bf16[512,128]{1,0:T(8,128)(2,1)S(1)} %get-tuple-element.27), channel_id=1, source_target_pairs={{0,24},{8,16},{16,8},{24,0},{1,25},{9,17},{17,9},{25,1},{2,26},{10... | collective-permute-start | bytes 393224 | tf_op jit(solution)/shard_map/ppermute | solution.py:26
  23.5 0.0 collective-permute-done.8
  23.5 1.9 %scores.1 = bf16[1,1,64,128,128]{4,3,2,1,0:T(8,128)(2,1)} custom-call(s32[192]{0:T(256)S(4)} %get-tuple-element.16.refs_0_.places, bf16[32,128,128]{2,1,0:T(8,128)(2,1)S(1)} %get-tuple-element.23.panel, bf16[64,128,128]{2,1,0:T(8,128)(2,1)S(1)} %get-tuple-element.24.keep, bf16[2048,128]{1,0:T(8,128)(2,1)S(1)} %pad_maximum_fusion.features), custom_call_target="tpu_custom_call" | custom-call | flops 268435456 | bytes 4194304 | tf_op jit(solution)/shard_map/scores/pallas_call | solution.py:206
  25.4 0.8 %collective-permute-done.10 = bf16[512,128]{1,0:T(8,128)(2,1)S(1)} collective-permute-done((bf16[512,128]{1,0:T(8,128)(2,1)S(1)}, bf16[512,128]{1,0:T(8,128)(2,1)S(1)}, u32[]{:S(2)}, u32[]{:S(2)}) %collective-permute-start.10) | collective-permute-done | bytes 131104 | tf_op jit(solution)/shard_map/ppermute | solution.py:26
  26.2 2.2 %collective-permute-done.11 = bf16[512,128]{1,0:T(8,128)(2,1)S(1)} collective-permute-done((bf16[512,128]{1,0:T(8,128)(2,1)S(1)}, bf16[512,128]{1,0:T(8,128)(2,1)S(1)}, u32[]{:S(2)}, u32[]{:S(2)}) %collective-permute-start.11) | collective-permute-done | bytes 131104 | tf_op jit(solution)/shard_map/ppermute | solution.py:26
  28.3 1.0 %collective-permute-done.9 = bf16[512,128]{1,0:T(8,128)(2,1)S(1)} collective-permute-done((bf16[512,128]{1,0:T(8,128)(2,1)S(1)}, bf16[512,128]{1,0:T(8,128)(2,1)S(1)}, u32[]{:S(2)}, u32[]{:S(2)}) %collective-permute-start.9) | collective-permute-done | bytes 131104 | tf_op jit(solution)/shard_map/ppermute | solution.py:26
  29.3 0.7 %add_convert_fusion = bf16[512,128]{1,0:T(8,128)(2,1)} fusion(bf16[512,128]{1,0:T(8,128)(2,1)S(1)} %collective-permute-done.11, bf16[512,128]{1,0:T(8,128)(2,1)S(1)} %collective-permute-done.10, f32[512,128]{1,0:T(8,128)S(1)} %get-tuple-element.26, bf16[512,128]{1,0:T(8,128)(2,1)S(1)} %collective-permute-done.9), kind=kLoop, calls=%fused_computation.2 | loop fusion | flops 458752 | bytes 786432 | tf_op jit(solution)/shard_map/convert_element_type | solution.py:224
  (2 shorter events, 0.1 us)
Async XLA Ops:
  1.8 10.7 %collective-permute-start = (bf16[512,128]{1,0:T(8,128)(2,1)S(1)}, bf16[512,128]{1,0:T(8,128)(2,1)S(1)}, u32[]{:S(2)}, u32[]{:S(2)}) collective-permute-start(bf16[512,128]{1,0:T(8,128)(2,1)S(1)} %hidden.1.refs_2_), channel_id=1, source_target_pairs={{0,4},{1,5},{2,6},{3,7},{4,0},{5,1},{6,2},{7,3},{8,12},{9,13},{10,... | collective-permute-start | bytes 393224 | tf_op jit(solution)/shard_map/ppermute | solution.py:26
  5.9 7.2 %collective-permute-start.7 = (bf16[512,128]{1,0:T(8,128)(2,1)}, bf16[512,128]{1,0:T(8,128)(2,1)S(1)}, u32[]{:S(2)}, u32[]{:S(2)}) collective-permute-start(bf16[512,128]{1,0:T(8,128)(2,1)} %param.6), channel_id=1, source_target_pairs={{0,8},{1,17},{2,10},{3,19},{4,12},{5,21},{6,14},{7,23},{8,0},{9,25... | collective-permute-start | bytes 393224 | tf_op jit(solution)/shard_map/ppermute | solution.py:32
  7.4 7.8 %collective-permute-start.2 = (bf16[512,128]{1,0:T(8,128)(2,1)S(1)}, bf16[512,128]{1,0:T(8,128)(2,1)S(1)}, u32[]{:S(2)}, u32[]{:S(2)}) collective-permute-start(bf16[512,128]{1,0:T(8,128)(2,1)S(1)} %hidden.1.refs_2_), channel_id=1, source_target_pairs={{0,2},{1,3},{2,0},{3,1},{4,6},{5,7},{6,4},{7,5},{8,10},{9,11},{10,... | collective-permute-start | bytes 393224 | tf_op jit(solution)/shard_map/ppermute | solution.py:26
  9.0 4.1 %copy-start = (bf16[512,128]{1,0:T(8,128)(2,1)S(1)}, bf16[512,128]{1,0:T(8,128)(2,1)}, u32[]{:S(2)}) copy-start(bf16[512,128]{1,0:T(8,128)(2,1)} %param.6) | copy-start | bytes 393220
  12.6 5.0 %collective-permute-start.5 = (bf16[512,128]{1,0:T(8,128)(2,1)S(1)}, bf16[512,128]{1,0:T(8,128)(2,1)S(1)}, u32[]{:S(2)}, u32[]{:S(2)}) collective-permute-start(bf16[512,128]{1,0:T(8,128)(2,1)S(1)} %collective-permute-done.refs_6_), channel_id=1, source_target_pairs={{0,2},{1,3},{2,0},{3,1},{4,6},{5,7},{6,4},{7,5},{8,10},{9,11},{10,... | collective-permute-start | bytes 393224 | tf_op jit(solution)/shard_map/ppermute | solution.py:26
  13.1 10.4 %collective-permute-start.8 = (bf16[1024,128]{1,0:T(8,128)(2,1)S(1)}, bf16[1024,128]{1,0:T(8,128)(2,1)S(1)}, u32[]{:S(2)}, u32[]{:S(2)}) collective-permute-start(bf16[1024,128]{1,0:T(8,128)(2,1)S(1)} %pad_maximum_fusion.1), channel_id=1, source_target_pairs={{0,16},{1,9},{2,18},{3,11},{4,20},{5,13},{6,22},{7,15},{8,24},{9,1... | collective-permute-start | bytes 786440 | tf_op jit(solution)/shard_map/ppermute | solution.py:32
  14.7 2.9 %collective-permute-start.4 = (bf16[512,128]{1,0:T(8,128)(2,1)S(1)}, bf16[512,128]{1,0:T(8,128)(2,1)S(1)}, u32[]{:S(2)}, u32[]{:S(2)}) collective-permute-start(bf16[512,128]{1,0:T(8,128)(2,1)S(1)} %collective-permute-done.refs_6_), channel_id=1, source_target_pairs={{0,1},{1,0},{2,3},{3,2},{4,5},{5,4},{6,7},{7,6},{8,9},{9,8},{10,11... | collective-permute-start | bytes 393224 | tf_op jit(solution)/shard_map/ppermute | solution.py:26
  14.7 2.9 %collective-permute-start.1 = (bf16[512,128]{1,0:T(8,128)(2,1)S(1)}, bf16[512,128]{1,0:T(8,128)(2,1)S(1)}, u32[]{:S(2)}, u32[]{:S(2)}) collective-permute-start(bf16[512,128]{1,0:T(8,128)(2,1)S(1)} %hidden.1.refs_2_), channel_id=1, source_target_pairs={{0,1},{1,0},{2,3},{3,2},{4,5},{5,4},{6,7},{7,6},{8,9},{9,8},{10,11... | collective-permute-start | bytes 393224 | tf_op jit(solution)/shard_map/ppermute | solution.py:26
  15.2 2.4 %collective-permute-start.3 = (bf16[512,128]{1,0:T(8,128)(2,1)S(1)}, bf16[512,128]{1,0:T(8,128)(2,1)S(1)}, u32[]{:S(2)}, u32[]{:S(2)}) collective-permute-start(bf16[512,128]{1,0:T(8,128)(2,1)S(1)} %collective-permute-done.2.refs_4_), channel_id=1, source_target_pairs={{0,1},{1,0},{2,3},{3,2},{4,5},{5,4},{6,7},{7,6},{8,9},{9,8},{10,11... | collective-permute-start | bytes 393224 | tf_op jit(solution)/shard_map/ppermute | solution.py:26
  17.6 1.3 %collective-permute-start.6 = (bf16[512,128]{1,0:T(8,128)(2,1)S(1)}, bf16[512,128]{1,0:T(8,128)(2,1)S(1)}, u32[]{:S(2)}, u32[]{:S(2)}) collective-permute-start(bf16[512,128]{1,0:T(8,128)(2,1)S(1)} %collective-permute-done.5.refs_8_), channel_id=1, source_target_pairs={{0,1},{1,0},{2,3},{3,2},{4,5},{5,4},{6,7},{7,6},{8,9},{9,8},{10,11... | collective-permute-start | bytes 393224 | tf_op jit(solution)/shard_map/ppermute | solution.py:26
  19.9 6.2 %collective-permute-start.10 = (bf16[512,128]{1,0:T(8,128)(2,1)S(1)}, bf16[512,128]{1,0:T(8,128)(2,1)S(1)}, u32[]{:S(2)}, u32[]{:S(2)}) collective-permute-start(bf16[512,128]{1,0:T(8,128)(2,1)S(1)} %get-tuple-element.28), channel_id=1, source_target_pairs={{0,8},{8,0},{16,24},{24,16},{1,9},{9,1},{17,25},{25,17},{2,10},{10... | collective-permute-start | bytes 393224 | tf_op jit(solution)/shard_map/ppermute | solution.py:26
  21.2 7.1 %collective-permute-start.11 = (bf16[512,128]{1,0:T(8,128)(2,1)S(1)}, bf16[512,128]{1,0:T(8,128)(2,1)S(1)}, u32[]{:S(2)}, u32[]{:S(2)}) collective-permute-start(bf16[512,128]{1,0:T(8,128)(2,1)S(1)} %get-tuple-element.29), channel_id=1, source_target_pairs={{0,16},{8,24},{16,0},{24,8},{1,17},{9,25},{17,1},{25,9},{2,18},{10... | collective-permute-start | bytes 393224 | tf_op jit(solution)/shard_map/ppermute | solution.py:26
  22.7 6.6 %collective-permute-start.9 = (bf16[512,128]{1,0:T(8,128)(2,1)S(1)}, bf16[512,128]{1,0:T(8,128)(2,1)S(1)}, u32[]{:S(2)}, u32[]{:S(2)}) collective-permute-start(bf16[512,128]{1,0:T(8,128)(2,1)S(1)} %get-tuple-element.27), channel_id=1, source_target_pairs={{0,24},{8,16},{16,8},{24,0},{1,25},{9,17},{17,9},{25,1},{2,26},{10... | collective-permute-start | bytes 393224 | tf_op jit(solution)/shard_map/ppermute | solution.py:26

commit v5 on v4

--- a/solution.py
+++ b/solution.py
@@ -68,16 +68,22 @@
             copy.start()
     table_copy.wait()
 
-    def body(g, carry):
+    def body(g, late):
         for i in range(GROUP):
             t = g * GROUP + i
             a = table[0, 0, 0, t]
             b = table[0, 1, 0, t]
-            places[t] = ((a // per) ^ me) * per + a % per
+            slot = (a // per) ^ me
             off = (b // per) ^ row
-            back = sum(((off >> i) & 1) << (bits - 1 - i) for i in range(bits))
-            places[tiles + t] = off * per + b % per
-            places[2 * tiles + t] = (off + core * (back - off)) * per + b % per
+            back = sum(((off >> j) & 1) << (bits - 1 - j) for j in range(bits))
+            places[t] = slot * per + a % per
+            places[tiles + t] = (off + core * (back - off)) * per + b % per
+            last = (slot == n_col - 1).astype(jnp.int32)
+            at = (1 - last) * (t - late) + last * (tiles - 1 - late)
+            late = late + last
+            places[2 * tiles + at] = t
+            places[3 * tiles + at] = off * per + b % per
+            places[4 * tiles + at] = (1 - last) * per + last * (a % per)
         for copy in fetch(g):
             copy.wait()
         for i in range(GROUP):
@@ -85,37 +91,61 @@
             keep = (mask_buf[t] * table[0, 2, 0, t]).astype(jnp.float32).astype(jnp.bfloat16)
             keep_out[t] = keep
             adj_out[t] = (weight_buf[t] * keep).T
+        return late
+
+    late = lax.fori_loop(0, groups, body, jnp.int32(0))
+    places[5 * tiles] = (tiles - late) // GROUP
+
+
+def sums_kernel(per, *refs):
+    places, adj, *slots, panel, total = refs
+    tiles = adj.shape[0]
+    for s, slot in enumerate(slots):
+        for i in range(per):
+            panel[s * per + i] = slot[i * BLOCK : (i + 1) * BLOCK, :]
+    for i in range(len(slots) * per, panel.shape[0]):
+        panel[i] = jnp.zeros_like(panel[i])
+    total[...] = jnp.zeros_like(total)
+    for p in range(tiles):
+        t = places[2 * tiles + p]
+        total[places[3 * tiles + p]] += jnp.dot(adj[t], panel[places[t]], preferred_element_type=jnp.float32)
+
+
+def rest_kernel(per, places, adj, total, last, *refs):
+    *outs, blocks, extra = refs
+    tiles = adj.shape[0]
+    for i in range(per):
+        blocks[i] = last[i * BLOCK : (i + 1) * BLOCK, :]
+    blocks[per] = jnp.zeros_like(blocks[per])
+    extra[...] = jnp.zeros_like(extra)
+
+    def body(g, carry):
+        for i in range(GROUP):
+            p = g * GROUP + i
+            extra[places[3 * tiles + p]] += jnp.dot(
+                adj[places[2 * tiles + p]], blocks[places[4 * tiles + p]], preferred_element_type=jnp.float32
+            )
         return carry
 
-    lax.fori_loop(0, groups, body, 0)
-
-
-def sums_kernel(n_row, n_col, per, *refs):
-    places, adj = refs[:2]
-    slots = refs[2 : 2 + n_col]
-    panel = refs[2 + n_col]
-    outs = refs[3 + n_col : 3 + n_col + n_row]
-    total = refs[3 + n_col + n_row]
-    tiles = adj.shape[0]
-    for s in range(n_col):
+    lax.fori_loop(places[5 * tiles], tiles // GROUP, body, 0)
+    for s, out in enumerate(outs):
         for i in range(per):
-            panel[s * per + i] = slots[s][i * BLOCK : (i + 1) * BLOCK, :]
-    total[...] = jnp.zeros_like(total)
-    for t in range(tiles):
-        total[places[tiles + t]] += jnp.dot(adj[t], panel[places[t]], preferred_element_type=jnp.float32)
-    for s in range(n_row):
-        for i in range(per):
-            outs[s][i * BLOCK : (i + 1) * BLOCK, :] = total[s * per + i].astype(outs[s].dtype)
-
-
-def scores_kernel(places, panel, keep, features, out, cols, stage, sems):
+            found = total[s * per + i] + extra[s * per + i]
+            out[i * BLOCK : (i + 1) * BLOCK, :] = found.astype(out.dtype)
+
+
+def scores_kernel(per, places, panel, last, keep, features, out, rows, cols, stage, sems):
     tiles = keep.shape[0]
+    head = rows.shape[0] - per
+    rows[:head] = panel[:head]
+    for i in range(per):
+        rows[head + i] = last[i * BLOCK : (i + 1) * BLOCK, :]
     for i in range(cols.shape[0]):
         cols[i] = features[i * BLOCK : (i + 1) * BLOCK, :].T
     copies = []
     for g in range(tiles // GROUP):
         for t in range(g * GROUP, (g + 1) * GROUP):
-            found = jnp.dot(panel[places[t]], cols[places[2 * tiles + t]], preferred_element_type=jnp.float32)
+            found = jnp.dot(rows[places[t]], cols[places[tiles + t]], preferred_element_type=jnp.float32)
             stage[t] = found.astype(jnp.bfloat16) * keep[t]
         span = pl.ds(g * GROUP, GROUP)
         copies.append(pltpu.make_async_copy(stage.at[span], out.at[0, 0, span], sems.at[g]))
@@ -163,7 +193,7 @@
         functools.partial(prep_kernel, n_row, n_col, per),
         in_specs=[far, far, far],
         out_specs=[whole, whole, scalars],
-        out_shape=[tile_set, tile_set, SMEM((3 * tiles,), jnp.int32)],
+        out_shape=[tile_set, tile_set, SMEM((5 * tiles + 1,), jnp.int32)],
         scratch_shapes=[
             SMEM(index.shape, jnp.int32),
             VMEM((tiles, BLOCK, BLOCK), jnp.int32),
@@ -179,6 +209,7 @@
 
     shards[masks[0]], hidden, keep, adj = lax.optimization_barrier((shards[masks[0]], hidden, keep, adj))
     shards[0] = hidden
+    cols, keep = lax.optimization_barrier((cols, keep))
     for i, mask in enumerate(masks[1:], 1):
         for s in range(masks[i - 1], n_col, masks[i - 1]):
             shards[s ^ mask] = swap(shards[s], "col", n_col, mask)
@@ -188,27 +219,39 @@
     slots = [shards[s] for s in range(0, n_col, 2)]
     slots = [x for shard in slots for x in (shard, swap(shard, "col", n_col, 1))]
 
-    panel, own, *parts = pl.pallas_call(
-        functools.partial(sums_kernel, n_row, n_col, per),
-        in_specs=[scalars] + [whole] * (1 + n_col),
-        out_specs=[whole] * (1 + n_row),
-        out_shape=[VMEM((n_col * per, BLOCK, fin), jnp.bfloat16), VMEM((nodes, fin), jnp.float32)]
-        + [VMEM((nodes, fin), jnp.bfloat16)] * (n_row - 1),
-        scratch_shapes=[VMEM((n_row * per, BLOCK, fin), jnp.float32)],
-        cost_estimate=pl.CostEstimate(flops=0, bytes_accessed=4096, transcendentals=0),
+    *slots, last = slots
+    total_shape = (n_row * per, BLOCK, fin)
+    panel, total = pl.pallas_call(
+        functools.partial(sums_kernel, per),
+        in_specs=[scalars] + [whole] * n_col,
+        out_specs=[whole] * 2,
+        out_shape=[VMEM((n_col * per, BLOCK, fin), jnp.bfloat16), VMEM(total_shape, jnp.float32)],
+        cost_estimate=pl.CostEstimate(flops=product_flops, bytes_accessed=1 << 20, transcendentals=0),
         compiler_params=params,
         name="sums",
     )(places, *map(in_vmem, (adj, *slots)))
+    own, *parts = pl.pallas_call(
+        functools.partial(rest_kernel, per),
+        in_specs=[scalars] + [whole] * 3,
+        out_specs=[whole] * n_row,
+        out_shape=[VMEM((nodes, fin), jnp.float32)] + [VMEM((nodes, fin), jnp.bfloat16)] * (n_row - 1),
+        scratch_shapes=[VMEM((per + 1, BLOCK, fin), jnp.bfloat16), VMEM(total_shape, jnp.float32)],
+        cost_estimate=pl.CostEstimate(flops=0, bytes_accessed=4096, transcendentals=0),
+        compiler_params=params,
+        name="rest",
+    )(places, *map(in_vmem, (adj, total, last)))
 
     order = sorted(range(1, n_row), key=lambda s: -s.bit_count())
+    order = order[-1:] + order[:-1]
     got = [swap(parts[s - 1], "row", n_row, s) for s in order]
 
     edge_grad = pl.pallas_call(
-        scores_kernel,
-        in_specs=[scalars] + [whole] * 3,
+        functools.partial(scores_kernel, per),
+        in_specs=[scalars] + [whole] * 4,
         out_specs=far,
         out_shape=jax.ShapeDtypeStruct(edge_weight.shape, jnp.bfloat16),
         scratch_shapes=[
+            VMEM((n_col * per, BLOCK, fin), jnp.bfloat16),
             VMEM((n_row * per, fin, BLOCK), jnp.bfloat16),
             VMEM((tiles, BLOCK, BLOCK), jnp.bfloat16),
             pltpu.SemaphoreType.DMA((tiles // GROUP,)),
@@ -216,12 +259,11 @@
         cost_estimate=pl.CostEstimate(flops=product_flops, bytes_accessed=4 << 20, transcendentals=0),
         compiler_params=params,
         name="scores",
-    )(places, *map(in_vmem, (panel, keep, cols)))
-
-    total = own
+    )(places, *map(in_vmem, (panel, last, keep, cols)))
+
     for part in got:
-        total = total + part.astype(jnp.float32)
-    return edge_grad, total.astype(jnp.bfloat16)
+        own = own + part.astype(jnp.float32)
+    return edge_grad, own.astype(jnp.bfloat16)
 
 
 def solution(mesh):

time: 30.2 us -> 30 us (level)
  waiting for transfers between devices: 7.66 us -> 6.88 us
  Pallas kernels: 7.56 us -> 8.27 us
    ppermute x10, waiting for transfers between devices: 7.66 us -> 6.87 us  [swap(): return lax.ppermute(x, axis, [(i, i ^ mask) for i in range(size)])]
    pallas_call x2 -> x3, Pallas kernels: 2.82 us -> 3.24 us  [the longest x1 1.92 us: local(): pl.pallas_call(functools.partial(scores_kernel, per), in_specs=[scalars]...]
  transfers between devices with their start and end apart: 12 -> 12, of which waited for: 5 -> 4; matrix products, arithmetic and copies ran while one was open for 0% -> 0% of each run, Pallas kernels for 21% -> 24%
where the time goes in v5:
time: 30 us
  starting transfers between devices  13.4 us (45%)
  Pallas kernels  8.27 us (28%)
  waiting for transfers between devices  6.88 us (23%)
  other arithmetic  0.77 us (3%)
  between operations  0.71 us (2%)
    ppermute x10, starting transfers between devices, swap(): return lax.ppermute(x, axis, [(i, i ^ mask) for i in range(size)])  10.3 us
    ppermute x10, waiting for transfers between devices, swap(): return lax.ppermute(x, axis, [(i, i ^ mask) for i in range(size)])  6.87 us
    pallas_call x1, Pallas kernels, local(): pl.pallas_call(functools.partial(prep_kernel, n_row, n_col, per), in_spec...  3.83 us
    ppermute x2, starting transfers between devices, swap_rows(): return lax.ppermute(x, ('row', 'col'), pairs)  3.07 us
    pallas_call x1, Pallas kernels, local(): pl.pallas_call(functools.partial(scores_kernel, per), in_specs=[scalars]...  1.92 us
    pallas_call x1, Pallas kernels, local(): pl.pallas_call(hidden_kernel, in_specs=[far, far], out_specs=whole, out_s...  1.19 us
    pallas_call x1, Pallas kernels, local(): pl.pallas_call(functools.partial(sums_kernel, per), in_specs=[scalars] +...  0.91 us
    convert_element_type x1, other arithmetic, local(): return (edge_grad, own.astype(jnp.bfloat16))  0.72 us
  transfers between devices with their start and end apart: 12, of which 4 were waited for; matrix products, arithmetic and copies ran while one was open for 0% of the time, Pallas kernels for 24%

profile of v5, /device:TPU:0, one launch (start us, length us, event | category | flops | bytes accessed | tf_op | source)
XLA Modules:
  0.0 30.0 jit_solution(9033487746465909336)
XLA Ops:
  0.6 1.2 %hidden.1.refs_2_ = bf16[512,128]{1,0:T(8,128)(2,1)S(1)} custom-call(bf16[512,256]{1,0:T(8,128)(2,1)} %grads.1, bf16[128,256]{1,0:T(8,128)(2,1)} %weight.1), custom_call_target="tpu_custom_call" | custom-call | tf_op jit(solution)/shard_map/hidden/pallas_call | solution.py:168
  1.8 4.1 %collective-permute-start = (bf16[512,128]{1,0:T(8,128)(2,1)S(1)}, bf16[512,128]{1,0:T(8,128)(2,1)S(1)}, u32[]{:S(2)}, u32[]{:S(2)}) collective-permute-start(bf16[512,128]{1,0:T(8,128)(2,1)S(1)} %hidden.1.refs_2_), channel_id=1, source_target_pairs={{0,4},{1,5},{2,6},{3,7},{4,0},{5,1},{6,2},{7,3},{8,12},{9,13},{10,... | collective-permute-start | bytes 393224 | tf_op jit(solution)/shard_map/ppermute | solution.py:26
  5.9 1.5 %collective-permute-start.7 = (bf16[512,128]{1,0:T(8,128)(2,1)}, bf16[512,128]{1,0:T(8,128)(2,1)S(1)}, u32[]{:S(2)}, u32[]{:S(2)}) collective-permute-start(bf16[512,128]{1,0:T(8,128)(2,1)} %param.6), channel_id=1, source_target_pairs={{0,8},{1,17},{2,10},{3,19},{4,12},{5,21},{6,14},{7,23},{8,0},{9,25... | collective-permute-start | bytes 393224 | tf_op jit(solution)/shard_map/ppermute | solution.py:32
  7.4 1.6 %collective-permute-start.2 = (bf16[512,128]{1,0:T(8,128)(2,1)S(1)}, bf16[512,128]{1,0:T(8,128)(2,1)S(1)}, u32[]{:S(2)}, u32[]{:S(2)}) collective-permute-start(bf16[512,128]{1,0:T(8,128)(2,1)S(1)} %hidden.1.refs_2_), channel_id=1, source_target_pairs={{0,2},{1,3},{2,0},{3,1},{4,6},{5,7},{6,4},{7,5},{8,10},{9,11},{10,... | collective-permute-start | bytes 393224 | tf_op jit(solution)/shard_map/ppermute | solution.py:26
  9.0 0.0 copy-start
  9.0 3.8 %prep.1 = (bf16[64,128,128]{2,1,0:T(8,128)(2,1)S(1)}, bf16[64,128,128]{2,1,0:T(8,128)(2,1)S(1)}, s32[321]{0:T(512)S(4)}) custom-call(s32[1,3,1,64]{3,2,1,0:T(1,128)} %bitcast.1, s32[1,1,64,128,128]{4,3,2,1,0:T(8,128)} %mask.1, bf16[1,1,64,128,128]{4,3,2,1,0:T(8,128)(2,1)} %weights.1), custom_call_target="tpu_custom_call" | custom-call | bytes 4096 | tf_op jit(solution)/shard_map/prep/pallas_call | solution.py:192
  12.9 0.0 collective-permute-done.refs_6_
  12.9 0.5 %collective-permute-start.5 = (bf16[512,128]{1,0:T(8,128)(2,1)S(1)}, bf16[512,128]{1,0:T(8,128)(2,1)S(1)}, u32[]{:S(2)}, u32[]{:S(2)}) collective-permute-start(bf16[512,128]{1,0:T(8,128)(2,1)S(1)} %collective-permute-done.refs_6_), channel_id=1, source_target_pairs={{0,2},{1,3},{2,0},{3,1},{4,6},{5,7},{6,4},{7,5},{8,10},{9,11},{10,... | collective-permute-start | bytes 393224 | tf_op jit(solution)/shard_map/ppermute | solution.py:26
  13.4 0.0 collective-permute-done.7
  13.4 0.0 copy-done
  13.4 1.6 %collective-permute-start.8 = (bf16[1024,128]{1,0:T(8,128)(2,1)S(1)}, bf16[1024,128]{1,0:T(8,128)(2,1)S(1)}, u32[]{:S(2)}, u32[]{:S(2)}) collective-permute-start(bf16[1024,128]{1,0:T(8,128)(2,1)S(1)} %pad_maximum_fusion.1), channel_id=1, source_target_pairs={{0,16},{1,9},{2,18},{3,11},{4,20},{5,13},{6,22},{7,15},{8,24},{9,1... | collective-permute-start | bytes 786440 | tf_op jit(solution)/shard_map/ppermute | solution.py:32
  15.0 0.0 collective-permute-start.4
  15.0 0.5 %collective-permute-start.1 = (bf16[512,128]{1,0:T(8,128)(2,1)S(1)}, bf16[512,128]{1,0:T(8,128)(2,1)S(1)}, u32[]{:S(2)}, u32[]{:S(2)}) collective-permute-start(bf16[512,128]{1,0:T(8,128)(2,1)S(1)} %hidden.1.refs_2_), channel_id=1, source_target_pairs={{0,1},{1,0},{2,3},{3,2},{4,5},{5,4},{6,7},{7,6},{8,9},{9,8},{10,11... | collective-permute-start | bytes 393224 | tf_op jit(solution)/shard_map/ppermute | solution.py:26
  15.5 0.0 collective-permute-done.2.refs_4_
  15.5 0.0 collective-permute-start.3
  15.5 2.4 %collective-permute-done.5.refs_8_ = bf16[512,128]{1,0:T(8,128)(2,1)S(1)} collective-permute-done((bf16[512,128]{1,0:T(8,128)(2,1)S(1)}, bf16[512,128]{1,0:T(8,128)(2,1)S(1)}, u32[]{:S(2)}, u32[]{:S(2)}) %collective-permute-start.5) | collective-permute-done | bytes 131104 | tf_op jit(solution)/shard_map/ppermute | solution.py:26
  17.9 0.0 collective-permute-start.6
  17.9 0.0 collective-permute-done.4.refs_7_
  17.9 0.0 collective-permute-done.1.refs_3_
  17.9 0.0 collective-permute-done.3.refs_5_
  17.9 0.9 %sums.1 = (bf16[32,128,128]{2,1,0:T(8,128)(2,1)S(1)}, f32[16,128,128]{2,1,0:T(8,128)S(1)}) custom-call(s32[321]{0:T(512)S(4)} %get-tuple-element.20.refs_0_.places, bf16[64,128,128]{2,1,0:T(8,128)(2,1)S(1)} %get-tuple-element.24.refs_1_.adj, bf16[512,128]{1,0:T(8,128)(2,1)S(1)} %hidden.1.refs_2_, bf16[512,128]{1,0:T(8,128)(2,1)S(1)} %collective-permute-done.1.refs_3_, ...), custom_call_target="tpu_custom_call" | custom-call | flops 268435456 | bytes 1048576 | tf_op jit(solution)/shard_map/sums/pallas_call | solution.py:224
  18.8 0.4 %collective-permute-done.6.last = bf16[512,128]{1,0:T(8,128)(2,1)S(1)} collective-permute-done((bf16[512,128]{1,0:T(8,128)(2,1)S(1)}, bf16[512,128]{1,0:T(8,128)(2,1)S(1)}, u32[]{:S(2)}, u32[]{:S(2)}) %collective-permute-start.6) | collective-permute-done | bytes 131104 | tf_op jit(solution)/shard_map/ppermute | solution.py:26
  19.2 0.4 %rest.1 = (f32[512,128]{1,0:T(8,128)S(1)}, bf16[512,128]{1,0:T(8,128)(2,1)S(1)}, bf16[512,128]{1,0:T(8,128)(2,1)S(1)}, bf16[512,128]{1,0:T(8,128)(2,1)S(1)}) custom-call(s32[321]{0:T(512)S(4)} %get-tuple-element.20.refs_0_.places, bf16[64,128,128]{2,1,0:T(8,128)(2,1)S(1)} %get-tuple-element.24.refs_1_.adj, f32[16,128,128]{2,1,0:T(8,128)S(1)} %get-tuple-element.33.total, ...), custom_call_target="tpu_custom_call" | custom-call | bytes 4096 | tf_op jit(solution)/shard_map/rest/pallas_call | solution.py:233
  19.7 2.0 %collective-permute-start.10 = (bf16[512,128]{1,0:T(8,128)(2,1)S(1)}, bf16[512,128]{1,0:T(8,128)(2,1)S(1)}, u32[]{:S(2)}, u32[]{:S(2)}) collective-permute-start(bf16[512,128]{1,0:T(8,128)(2,1)S(1)} %get-tuple-element.36), channel_id=1, source_target_pairs={{0,24},{8,16},{16,8},{24,0},{1,25},{9,17},{17,9},{25,1},{2,26},{10... | collective-permute-start | bytes 393224 | tf_op jit(solution)/shard_map/ppermute | solution.py:26
  21.7 1.3 %collective-permute-start.11 = (bf16[512,128]{1,0:T(8,128)(2,1)S(1)}, bf16[512,128]{1,0:T(8,128)(2,1)S(1)}, u32[]{:S(2)}, u32[]{:S(2)}) collective-permute-start(bf16[512,128]{1,0:T(8,128)(2,1)S(1)} %get-tuple-element.37), channel_id=1, source_target_pairs={{0,8},{8,0},{16,24},{24,16},{1,9},{9,1},{17,25},{25,17},{2,10},{10... | collective-permute-start | bytes 393224 | tf_op jit(solution)/shard_map/ppermute | solution.py:26
  22.9 0.3 %collective-permute-start.9 = (bf16[512,128]{1,0:T(8,128)(2,1)S(1)}, bf16[512,128]{1,0:T(8,128)(2,1)S(1)}, u32[]{:S(2)}, u32[]{:S(2)}) collective-permute-start(bf16[512,128]{1,0:T(8,128)(2,1)S(1)} %get-tuple-element.35), channel_id=1, source_target_pairs={{0,16},{8,24},{16,0},{24,8},{1,17},{9,25},{17,1},{25,9},{2,18},{10... | collective-permute-start | bytes 393224 | tf_op jit(solution)/shard_map/ppermute | solution.py:26
  23.2 0.0 collective-permute-done.8
  23.3 1.9 %scores.1 = bf16[1,1,64,128,128]{4,3,2,1,0:T(8,128)(2,1)} custom-call(s32[321]{0:T(512)S(4)} %get-tuple-element.20.refs_0_.places, bf16[32,128,128]{2,1,0:T(8,128)(2,1)S(1)} %get-tuple-element.27.panel, bf16[512,128]{1,0:T(8,128)(2,1)S(1)} %collective-permute-done.6.last, bf16[64,128,128]{2,1,0:T(8,128)(2,1)S(1)} %get-tuple-element.30.keep, ...), custom_call_target="tpu_custom_call" | custom-call | flops 268435456 | bytes 4194304 | tf_op jit(solution)/shard_map/scores/pallas_call | solution.py:248
  25.2 1.7 %collective-permute-done.10 = bf16[512,128]{1,0:T(8,128)(2,1)S(1)} collective-permute-done((bf16[512,128]{1,0:T(8,128)(2,1)S(1)}, bf16[512,128]{1,0:T(8,128)(2,1)S(1)}, u32[]{:S(2)}, u32[]{:S(2)}) %collective-permute-start.10) | collective-permute-done | bytes 131104 | tf_op jit(solution)/shard_map/ppermute | solution.py:26
  27.0 2.3 %collective-permute-done.11 = bf16[512,128]{1,0:T(8,128)(2,1)S(1)} collective-permute-done((bf16[512,128]{1,0:T(8,128)(2,1)S(1)}, bf16[512,128]{1,0:T(8,128)(2,1)S(1)}, u32[]{:S(2)}, u32[]{:S(2)}) %collective-permute-start.11) | collective-permute-done | bytes 131104 | tf_op jit(solution)/shard_map/ppermute | solution.py:26
  29.3 0.0 collective-permute-done.9
  29.3 0.7 %add_convert_fusion = bf16[512,128]{1,0:T(8,128)(2,1)} fusion(bf16[512,128]{1,0:T(8,128)(2,1)S(1)} %collective-permute-done.11, bf16[512,128]{1,0:T(8,128)(2,1)S(1)} %collective-permute-done.10, f32[512,128]{1,0:T(8,128)S(1)} %get-tuple-element.34, bf16[512,128]{1,0:T(8,128)(2,1)S(1)} %collective-permute-done.9), kind=kLoop, calls=%fused_computation.2 | loop fusion | flops 458752 | bytes 786432 | tf_op jit(solution)/shard_map/convert_element_type | solution.py:266
  (2 shorter events, 0.1 us)
Async XLA Ops:
  1.8 11.0 %collective-permute-start = (bf16[512,128]{1,0:T(8,128)(2,1)S(1)}, bf16[512,128]{1,0:T(8,128)(2,1)S(1)}, u32[]{:S(2)}, u32[]{:S(2)}) collective-permute-start(bf16[512,128]{1,0:T(8,128)(2,1)S(1)} %hidden.1.refs_2_), channel_id=1, source_target_pairs={{0,4},{1,5},{2,6},{3,7},{4,0},{5,1},{6,2},{7,3},{8,12},{9,13},{10,... | collective-permute-start | bytes 393224 | tf_op jit(solution)/shard_map/ppermute | solution.py:26
  5.9 7.4 %collective-permute-start.7 = (bf16[512,128]{1,0:T(8,128)(2,1)}, bf16[512,128]{1,0:T(8,128)(2,1)S(1)}, u32[]{:S(2)}, u32[]{:S(2)}) collective-permute-start(bf16[512,128]{1,0:T(8,128)(2,1)} %param.6), channel_id=1, source_target_pairs={{0,8},{1,17},{2,10},{3,19},{4,12},{5,21},{6,14},{7,23},{8,0},{9,25... | collective-permute-start | bytes 393224 | tf_op jit(solution)/shard_map/ppermute | solution.py:32
  7.4 8.1 %collective-permute-start.2 = (bf16[512,128]{1,0:T(8,128)(2,1)S(1)}, bf16[512,128]{1,0:T(8,128)(2,1)S(1)}, u32[]{:S(2)}, u32[]{:S(2)}) collective-permute-start(bf16[512,128]{1,0:T(8,128)(2,1)S(1)} %hidden.1.refs_2_), channel_id=1, source_target_pairs={{0,2},{1,3},{2,0},{3,1},{4,6},{5,7},{6,4},{7,5},{8,10},{9,11},{10,... | collective-permute-start | bytes 393224 | tf_op jit(solution)/shard_map/ppermute | solution.py:26
  9.0 4.4 %copy-start = (bf16[512,128]{1,0:T(8,128)(2,1)S(1)}, bf16[512,128]{1,0:T(8,128)(2,1)}, u32[]{:S(2)}) copy-start(bf16[512,128]{1,0:T(8,128)(2,1)} %param.6) | copy-start | bytes 393220
  12.9 5.0 %collective-permute-start.5 = (bf16[512,128]{1,0:T(8,128)(2,1)S(1)}, bf16[512,128]{1,0:T(8,128)(2,1)S(1)}, u32[]{:S(2)}, u32[]{:S(2)}) collective-permute-start(bf16[512,128]{1,0:T(8,128)(2,1)S(1)} %collective-permute-done.refs_6_), channel_id=1, source_target_pairs={{0,2},{1,3},{2,0},{3,1},{4,6},{5,7},{6,4},{7,5},{8,10},{9,11},{10,... | collective-permute-start | bytes 393224 | tf_op jit(solution)/shard_map/ppermute | solution.py:26
  13.4 9.8 %collective-permute-start.8 = (bf16[1024,128]{1,0:T(8,128)(2,1)S(1)}, bf16[1024,128]{1,0:T(8,128)(2,1)S(1)}, u32[]{:S(2)}, u32[]{:S(2)}) collective-permute-start(bf16[1024,128]{1,0:T(8,128)(2,1)S(1)} %pad_maximum_fusion.1), channel_id=1, source_target_pairs={{0,16},{1,9},{2,18},{3,11},{4,20},{5,13},{6,22},{7,15},{8,24},{9,1... | collective-permute-start | bytes 786440 | tf_op jit(solution)/shard_map/ppermute | solution.py:32
  15.0 2.9 %collective-permute-start.4 = (bf16[512,128]{1,0:T(8,128)(2,1)S(1)}, bf16[512,128]{1,0:T(8,128)(2,1)S(1)}, u32[]{:S(2)}, u32[]{:S(2)}) collective-permute-start(bf16[512,128]{1,0:T(8,128)(2,1)S(1)} %collective-permute-done.refs_6_), channel_id=1, source_target_pairs={{0,1},{1,0},{2,3},{3,2},{4,5},{5,4},{6,7},{7,6},{8,9},{9,8},{10,11... | collective-permute-start | bytes 393224 | tf_op jit(solution)/shard_map/ppermute | solution.py:26
  15.0 2.9 %collective-permute-start.1 = (bf16[512,128]{1,0:T(8,128)(2,1)S(1)}, bf16[512,128]{1,0:T(8,128)(2,1)S(1)}, u32[]{:S(2)}, u32[]{:S(2)}) collective-permute-start(bf16[512,128]{1,0:T(8,128)(2,1)S(1)} %hidden.1.refs_2_), channel_id=1, source_target_pairs={{0,1},{1,0},{2,3},{3,2},{4,5},{5,4},{6,7},{7,6},{8,9},{9,8},{10,11... | collective-permute-start | bytes 393224 | tf_op jit(solution)/shard_map/ppermute | solution.py:26
  15.5 2.4 %collective-permute-start.3 = (bf16[512,128]{1,0:T(8,128)(2,1)S(1)}, bf16[512,128]{1,0:T(8,128)(2,1)S(1)}, u32[]{:S(2)}, u32[]{:S(2)}) collective-permute-start(bf16[512,128]{1,0:T(8,128)(2,1)S(1)} %collective-permute-done.2.refs_4_), channel_id=1, source_target_pairs={{0,1},{1,0},{2,3},{3,2},{4,5},{5,4},{6,7},{7,6},{8,9},{9,8},{10,11... | collective-permute-start | bytes 393224 | tf_op jit(solution)/shard_map/ppermute | solution.py:26
  17.9 1.3 %collective-permute-start.6 = (bf16[512,128]{1,0:T(8,128)(2,1)S(1)}, bf16[512,128]{1,0:T(8,128)(2,1)S(1)}, u32[]{:S(2)}, u32[]{:S(2)}) collective-permute-start(bf16[512,128]{1,0:T(8,128)(2,1)S(1)} %collective-permute-done.5.refs_8_), channel_id=1, source_target_pairs={{0,1},{1,0},{2,3},{3,2},{4,5},{5,4},{6,7},{7,6},{8,9},{9,8},{10,11... | collective-permute-start | bytes 393224 | tf_op jit(solution)/shard_map/ppermute | solution.py:26
  19.7 7.3 %collective-permute-start.10 = (bf16[512,128]{1,0:T(8,128)(2,1)S(1)}, bf16[512,128]{1,0:T(8,128)(2,1)S(1)}, u32[]{:S(2)}, u32[]{:S(2)}) collective-permute-start(bf16[512,128]{1,0:T(8,128)(2,1)S(1)} %get-tuple-element.36), channel_id=1, source_target_pairs={{0,24},{8,16},{16,8},{24,0},{1,25},{9,17},{17,9},{25,1},{2,26},{10... | collective-permute-start | bytes 393224 | tf_op jit(solution)/shard_map/ppermute | solution.py:26
  21.7 7.6 %collective-permute-start.11 = (bf16[512,128]{1,0:T(8,128)(2,1)S(1)}, bf16[512,128]{1,0:T(8,128)(2,1)S(1)}, u32[]{:S(2)}, u32[]{:S(2)}) collective-permute-start(bf16[512,128]{1,0:T(8,128)(2,1)S(1)} %get-tuple-element.37), channel_id=1, source_target_pairs={{0,8},{8,0},{16,24},{24,16},{1,9},{9,1},{17,25},{25,17},{2,10},{10... | collective-permute-start | bytes 393224 | tf_op jit(solution)/shard_map/ppermute | solution.py:26
  22.9 6.3 %collective-permute-start.9 = (bf16[512,128]{1,0:T(8,128)(2,1)S(1)}, bf16[512,128]{1,0:T(8,128)(2,1)S(1)}, u32[]{:S(2)}, u32[]{:S(2)}) collective-permute-start(bf16[512,128]{1,0:T(8,128)(2,1)S(1)} %get-tuple-element.35), channel_id=1, source_target_pairs={{0,16},{8,24},{16,0},{24,8},{1,17},{9,25},{17,1},{25,9},{2,18},{10... | collective-permute-start | bytes 393224 | tf_op jit(solution)/shard_map/ppermute | solution.py:26

commit v6 on v5

--- a/solution.py
+++ b/solution.py
@@ -46,13 +46,9 @@
     ).astype(out.dtype)
 
 
-def prep_kernel(n_row, n_col, per, index, mask, weights, keep_out, adj_out, places, table, mask_buf, weight_buf, sems, table_sem):
+def prep_kernel(index, mask, weights, keep_out, adj_out, table, mask_buf, weight_buf, sems, table_sem):
     tiles = mask_buf.shape[0]
     groups = tiles // GROUP
-    me = lax.axis_index("col")
-    row = lax.axis_index("row")
-    core = me % 2
-    bits = n_row.bit_length() - 1
 
     def fetch(g):
         span = pl.ds(pl.multiple_of(g * GROUP, GROUP), GROUP)
@@ -67,6 +63,26 @@
         for copy in fetch(g):
             copy.start()
     table_copy.wait()
+
+    def body(g, carry):
+        for copy in fetch(g):
+            copy.wait()
+        for i in range(GROUP):
+            t = g * GROUP + i
+            keep = (mask_buf[t] * table[0, 2, 0, t]).astype(jnp.float32).astype(jnp.bfloat16)
+            keep_out[t] = keep
+            adj_out[t] = (weight_buf[t] * keep).T
+        return carry
+
+    lax.fori_loop(0, groups, body, 0)
+
+
+def places_kernel(n_row, n_col, per, table, places):
+    tiles = table.shape[3]
+    me = lax.axis_index("col")
+    row = lax.axis_index("row")
+    core = me % 2
+    bits = n_row.bit_length() - 1
 
     def body(g, late):
         for i in range(GROUP):
@@ -84,16 +100,9 @@
             places[2 * tiles + at] = t
             places[3 * tiles + at] = off * per + b % per
             places[4 * tiles + at] = (1 - last) * per + last * (a % per)
-        for copy in fetch(g):
-            copy.wait()
-        for i in range(GROUP):
-            t = g * GROUP + i
-            keep = (mask_buf[t] * table[0, 2, 0, t]).astype(jnp.float32).astype(jnp.bfloat16)
-            keep_out[t] = keep
-            adj_out[t] = (weight_buf[t] * keep).T
         return late
 
-    late = lax.fori_loop(0, groups, body, jnp.int32(0))
+    late = lax.fori_loop(0, tiles // GROUP, body, jnp.int32(0))
     places[5 * tiles] = (tiles - late) // GROUP
 
 
@@ -189,13 +198,12 @@
     cols = [features, swap_rows(features, n_row, n_col, *stages[0])]
 
     index = jnp.transpose(tile_index, (0, 3, 1, 2))
-    keep, adj, places = pl.pallas_call(
-        functools.partial(prep_kernel, n_row, n_col, per),
+    keep, adj, table = pl.pallas_call(
+        prep_kernel,
         in_specs=[far, far, far],
         out_specs=[whole, whole, scalars],
-        out_shape=[tile_set, tile_set, SMEM((5 * tiles + 1,), jnp.int32)],
+        out_shape=[tile_set, tile_set, SMEM(index.shape, jnp.int32)],
         scratch_shapes=[
-            SMEM(index.shape, jnp.int32),
             VMEM((tiles, BLOCK, BLOCK), jnp.int32),
             VMEM((tiles, BLOCK, BLOCK), jnp.bfloat16),
             pltpu.SemaphoreType.DMA((2, tiles // GROUP)),
@@ -205,6 +213,15 @@
         compiler_params=params,
         name="prep",
     )(in_hbm(index), in_hbm(edge_mask), in_hbm(edge_weight))
+    places = pl.pallas_call(
+        functools.partial(places_kernel, n_row, n_col, per),
+        in_specs=[scalars],
+        out_specs=scalars,
+        out_shape=SMEM((5 * tiles + 1,), jnp.int32),
+        cost_estimate=pl.CostEstimate(flops=0, bytes_accessed=4096, transcendentals=0),
+        compiler_params=params,
+        name="places",
+    )(pltpu.with_memory_space_constraint(table, SMEM))
     places = pltpu.with_memory_space_constraint(places, SMEM)
 
     shards[masks[0]], hidden, keep, adj = lax.optimization_barrier((shards[masks[0]], hidden, keep, adj))

time: 30 us -> 29.6 us (0.987)
  Pallas kernels: 8.27 us -> 7.52 us
    pallas_call x1 -> x2, Pallas kernels: 3.83 us -> 3.09 us  [the longest x1 3.09 us: local(): pl.pallas_call(prep_kernel, in_specs=[far, far, far], out_specs=[whole, w...]
  transfers between devices with their start and end apart: 12 -> 12, of which waited for: 4 -> 5; matrix products, arithmetic and copies ran while one was open for 0% -> 0% of each run, Pallas kernels for 24% -> 21%
where the time goes in v6:
time: 29.6 us; the launch traced here: 29.5 us
  starting transfers between devices  13.5 us (46%)
  Pallas kernels  7.52 us (25%)
  waiting for transfers between devices  7 us (24%)
  other arithmetic  0.77 us (3%)
  between operations  0.7 us (2%)
    ppermute x10, starting transfers between devices, swap(): return lax.ppermute(x, axis, [(i, i ^ mask) for i in range(size)])  10.4 us
    ppermute x10, waiting for transfers between devices, swap(): return lax.ppermute(x, axis, [(i, i ^ mask) for i in range(size)])  6.99 us
    pallas_call x1, Pallas kernels, local(): pl.pallas_call(prep_kernel, in_specs=[far, far, far], out_specs=[whole, w...  3.09 us
    ppermute x2, starting transfers between devices, swap_rows(): return lax.ppermute(x, ('row', 'col'), pairs)  3.07 us
    pallas_call x1, Pallas kernels, local(): pl.pallas_call(functools.partial(scores_kernel, per), in_specs=[scalars]...  1.92 us
    pallas_call x1, Pallas kernels, local(): pl.pallas_call(hidden_kernel, in_specs=[far, far], out_specs=whole, out_s...  1.19 us
    pallas_call x1, Pallas kernels, local(): pl.pallas_call(functools.partial(sums_kernel, per), in_specs=[scalars] +...  0.92 us
    convert_element_type x1, other arithmetic, local(): return (edge_grad, own.astype(jnp.bfloat16))  0.72 us
  transfers between devices with their start and end apart: 12, of which 5 were waited for; matrix products, arithmetic and copies ran while one was open for 0% of the time, Pallas kernels for 21%

profile of v6, /device:TPU:0, one launch (start us, length us, event | category | flops | bytes accessed | tf_op | source)
XLA Modules:
  0.0 29.5 jit_solution(5743791006203156458)
XLA Ops:
  0.6 1.2 %hidden.1.refs_2_ = bf16[512,128]{1,0:T(8,128)(2,1)S(1)} custom-call(bf16[512,256]{1,0:T(8,128)(2,1)} %grads.1, bf16[128,256]{1,0:T(8,128)(2,1)} %weight.1), custom_call_target="tpu_custom_call" | custom-call | tf_op jit(solution)/shard_map/hidden/pallas_call | solution.py:177
  1.8 4.1 %collective-permute-start = (bf16[512,128]{1,0:T(8,128)(2,1)S(1)}, bf16[512,128]{1,0:T(8,128)(2,1)S(1)}, u32[]{:S(2)}, u32[]{:S(2)}) collective-permute-start(bf16[512,128]{1,0:T(8,128)(2,1)S(1)} %hidden.1.refs_2_), channel_id=1, source_target_pairs={{0,4},{1,5},{2,6},{3,7},{4,0},{5,1},{6,2},{7,3},{8,12},{9,13},{10,... | collective-permute-start | bytes 393224 | tf_op jit(solution)/shard_map/ppermute | solution.py:26
  5.9 1.5 %collective-permute-start.7 = (bf16[512,128]{1,0:T(8,128)(2,1)}, bf16[512,128]{1,0:T(8,128)(2,1)S(1)}, u32[]{:S(2)}, u32[]{:S(2)}) collective-permute-start(bf16[512,128]{1,0:T(8,128)(2,1)} %param.6), channel_id=1, source_target_pairs={{0,8},{1,17},{2,10},{3,19},{4,12},{5,21},{6,14},{7,23},{8,0},{9,25... | collective-permute-start | bytes 393224 | tf_op jit(solution)/shard_map/ppermute | solution.py:32
  7.4 1.6 %collective-permute-start.2 = (bf16[512,128]{1,0:T(8,128)(2,1)S(1)}, bf16[512,128]{1,0:T(8,128)(2,1)S(1)}, u32[]{:S(2)}, u32[]{:S(2)}) collective-permute-start(bf16[512,128]{1,0:T(8,128)(2,1)S(1)} %hidden.1.refs_2_), channel_id=1, source_target_pairs={{0,2},{1,3},{2,0},{3,1},{4,6},{5,7},{6,4},{7,5},{8,10},{9,11},{10,... | collective-permute-start | bytes 393224 | tf_op jit(solution)/shard_map/ppermute | solution.py:26
  9.0 0.0 copy-start
  9.0 3.1 %prep.1 = (bf16[64,128,128]{2,1,0:T(8,128)(2,1)S(1)}, bf16[64,128,128]{2,1,0:T(8,128)(2,1)S(1)}, s32[1,3,1,64]{3,2,1,0:T(1,128)S(4)}) custom-call(s32[1,3,1,64]{3,2,1,0:T(1,128)} %bitcast.1, s32[1,1,64,128,128]{4,3,2,1,0:T(8,128)} %mask.1, bf16[1,1,64,128,128]{4,3,2,1,0:T(8,128)(2,1)} %weights.1), custom_call_target="tpu_custom_call" | custom-call | bytes 4096 | tf_op jit(solution)/shard_map/prep/pallas_call | solution.py:201
  12.1 0.2 collective-permute-done.refs_6_
  12.3 0.7 %collective-permute-start.5 = (bf16[512,128]{1,0:T(8,128)(2,1)S(1)}, bf16[512,128]{1,0:T(8,128)(2,1)S(1)}, u32[]{:S(2)}, u32[]{:S(2)}) collective-permute-start(bf16[512,128]{1,0:T(8,128)(2,1)S(1)} %collective-permute-done.refs_6_), channel_id=1, source_target_pairs={{0,2},{1,3},{2,0},{3,1},{4,6},{5,7},{6,4},{7,5},{8,10},{9,11},{10,... | collective-permute-start | bytes 393224 | tf_op jit(solution)/shard_map/ppermute | solution.py:26
  13.0 0.0 collective-permute-done.7
  13.0 0.0 copy-done
  13.0 1.6 %collective-permute-start.8 = (bf16[1024,128]{1,0:T(8,128)(2,1)S(1)}, bf16[1024,128]{1,0:T(8,128)(2,1)S(1)}, u32[]{:S(2)}, u32[]{:S(2)}) collective-permute-start(bf16[1024,128]{1,0:T(8,128)(2,1)S(1)} %pad_maximum_fusion.1), channel_id=1, source_target_pairs={{0,16},{1,9},{2,18},{3,11},{4,20},{5,13},{6,22},{7,15},{8,24},{9,1... | collective-permute-start | bytes 786440 | tf_op jit(solution)/shard_map/ppermute | solution.py:32
  14.6 0.0 collective-permute-start.4
  14.6 0.5 %collective-permute-start.1 = (bf16[512,128]{1,0:T(8,128)(2,1)S(1)}, bf16[512,128]{1,0:T(8,128)(2,1)S(1)}, u32[]{:S(2)}, u32[]{:S(2)}) collective-permute-start(bf16[512,128]{1,0:T(8,128)(2,1)S(1)} %hidden.1.refs_2_), channel_id=1, source_target_pairs={{0,1},{1,0},{2,3},{3,2},{4,5},{5,4},{6,7},{7,6},{8,9},{9,8},{10,11... | collective-permute-start | bytes 393224 | tf_op jit(solution)/shard_map/ppermute | solution.py:26
  15.1 0.0 collective-permute-done.2.refs_4_
  15.1 0.0 collective-permute-start.3
  15.1 2.2 %collective-permute-done.5.refs_8_ = bf16[512,128]{1,0:T(8,128)(2,1)S(1)} collective-permute-done((bf16[512,128]{1,0:T(8,128)(2,1)S(1)}, bf16[512,128]{1,0:T(8,128)(2,1)S(1)}, u32[]{:S(2)}, u32[]{:S(2)}) %collective-permute-start.5) | collective-permute-done | bytes 131104 | tf_op jit(solution)/shard_map/ppermute | solution.py:26
  17.3 0.0 collective-permute-start.6
  17.3 0.0 collective-permute-done.4.refs_7_
  17.3 0.0 collective-permute-done.1.refs_3_
  17.3 0.0 collective-permute-done.3.refs_5_
  17.3 0.9 %sums.1 = (bf16[32,128,128]{2,1,0:T(8,128)(2,1)S(1)}, f32[16,128,128]{2,1,0:T(8,128)S(1)}) custom-call(s32[321]{0:T(512)S(4)} %places.1.refs_0_, bf16[64,128,128]{2,1,0:T(8,128)(2,1)S(1)} %get-tuple-element.24.refs_1_.adj, bf16[512,128]{1,0:T(8,128)(2,1)S(1)} %hidden.1.refs_2_, bf16[512,128]{1,0:T(8,128)(2,1)S(1)} %collective-permute-done.1.refs_3_, ...), custom_call_target="tpu_custom_call" | custom-call | flops 268435456 | bytes 1048576 | tf_op jit(solution)/shard_map/sums/pallas_call | solution.py:241
  18.3 0.4 %collective-permute-done.6.last = bf16[512,128]{1,0:T(8,128)(2,1)S(1)} collective-permute-done((bf16[512,128]{1,0:T(8,128)(2,1)S(1)}, bf16[512,128]{1,0:T(8,128)(2,1)S(1)}, u32[]{:S(2)}, u32[]{:S(2)}) %collective-permute-start.6) | collective-permute-done | bytes 131104 | tf_op jit(solution)/shard_map/ppermute | solution.py:26
  18.7 0.4 %rest.1 = (f32[512,128]{1,0:T(8,128)S(1)}, bf16[512,128]{1,0:T(8,128)(2,1)S(1)}, bf16[512,128]{1,0:T(8,128)(2,1)S(1)}, bf16[512,128]{1,0:T(8,128)(2,1)S(1)}) custom-call(s32[321]{0:T(512)S(4)} %places.1.refs_0_, bf16[64,128,128]{2,1,0:T(8,128)(2,1)S(1)} %get-tuple-element.24.refs_1_.adj, f32[16,128,128]{2,1,0:T(8,128)S(1)} %get-tuple-element.33.total, ...), custom_call_target="tpu_custom_call" | custom-call | bytes 4096 | tf_op jit(solution)/shard_map/rest/pallas_call | solution.py:250
  19.1 2.8 %collective-permute-start.10 = (bf16[512,128]{1,0:T(8,128)(2,1)S(1)}, bf16[512,128]{1,0:T(8,128)(2,1)S(1)}, u32[]{:S(2)}, u32[]{:S(2)}) collective-permute-start(bf16[512,128]{1,0:T(8,128)(2,1)S(1)} %get-tuple-element.36), channel_id=1, source_target_pairs={{0,24},{8,16},{16,8},{24,0},{1,25},{9,17},{17,9},{25,1},{2,26},{10... | collective-permute-start | bytes 393224 | tf_op jit(solution)/shard_map/ppermute | solution.py:26
  21.9 0.3 %collective-permute-start.11 = (bf16[512,128]{1,0:T(8,128)(2,1)S(1)}, bf16[512,128]{1,0:T(8,128)(2,1)S(1)}, u32[]{:S(2)}, u32[]{:S(2)}) collective-permute-start(bf16[512,128]{1,0:T(8,128)(2,1)S(1)} %get-tuple-element.37), channel_id=1, source_target_pairs={{0,8},{8,0},{16,24},{24,16},{1,9},{9,1},{17,25},{25,17},{2,10},{10... | collective-permute-start | bytes 393224 | tf_op jit(solution)/shard_map/ppermute | solution.py:26
  22.2 0.4 %collective-permute-start.9 = (bf16[512,128]{1,0:T(8,128)(2,1)S(1)}, bf16[512,128]{1,0:T(8,128)(2,1)S(1)}, u32[]{:S(2)}, u32[]{:S(2)}) collective-permute-start(bf16[512,128]{1,0:T(8,128)(2,1)S(1)} %get-tuple-element.35), channel_id=1, source_target_pairs={{0,16},{8,24},{16,0},{24,8},{1,17},{9,25},{17,1},{25,9},{2,18},{10... | collective-permute-start | bytes 393224 | tf_op jit(solution)/shard_map/ppermute | solution.py:26
  22.7 0.0 collective-permute-done.8
  22.7 1.9 %scores.1 = bf16[1,1,64,128,128]{4,3,2,1,0:T(8,128)(2,1)} custom-call(s32[321]{0:T(512)S(4)} %places.1.refs_0_, bf16[32,128,128]{2,1,0:T(8,128)(2,1)S(1)} %get-tuple-element.27.panel, bf16[512,128]{1,0:T(8,128)(2,1)S(1)} %collective-permute-done.6.last, bf16[64,128,128]{2,1,0:T(8,128)(2,1)S(1)} %get-tuple-element.30.keep, ...), custom_call_target="tpu_custom_call" | custom-call | flops 268435456 | bytes 4194304 | tf_op jit(solution)/shard_map/scores/pallas_call | solution.py:265
  24.6 1.8 %collective-permute-done.10 = bf16[512,128]{1,0:T(8,128)(2,1)S(1)} collective-permute-done((bf16[512,128]{1,0:T(8,128)(2,1)S(1)}, bf16[512,128]{1,0:T(8,128)(2,1)S(1)}, u32[]{:S(2)}, u32[]{:S(2)}) %collective-permute-start.10) | collective-permute-done | bytes 131104 | tf_op jit(solution)/shard_map/ppermute | solution.py:26
  26.4 2.4 %collective-permute-done.11 = bf16[512,128]{1,0:T(8,128)(2,1)S(1)} collective-permute-done((bf16[512,128]{1,0:T(8,128)(2,1)S(1)}, bf16[512,128]{1,0:T(8,128)(2,1)S(1)}, u32[]{:S(2)}, u32[]{:S(2)}) %collective-permute-start.11) | collective-permute-done | bytes 131104 | tf_op jit(solution)/shard_map/ppermute | solution.py:26
  28.8 0.0 collective-permute-done.9
  28.8 0.7 %add_convert_fusion = bf16[512,128]{1,0:T(8,128)(2,1)} fusion(bf16[512,128]{1,0:T(8,128)(2,1)S(1)} %collective-permute-done.11, bf16[512,128]{1,0:T(8,128)(2,1)S(1)} %collective-permute-done.10, f32[512,128]{1,0:T(8,128)S(1)} %get-tuple-element.34, bf16[512,128]{1,0:T(8,128)(2,1)S(1)} %collective-permute-done.9), kind=kLoop, calls=%fused_computation.2 | loop fusion | flops 458752 | bytes 786432 | tf_op jit(solution)/shard_map/convert_element_type | solution.py:283
  (3 shorter events, 0.1 us)
Async XLA Ops:
  1.8 10.5 %collective-permute-start = (bf16[512,128]{1,0:T(8,128)(2,1)S(1)}, bf16[512,128]{1,0:T(8,128)(2,1)S(1)}, u32[]{:S(2)}, u32[]{:S(2)}) collective-permute-start(bf16[512,128]{1,0:T(8,128)(2,1)S(1)} %hidden.1.refs_2_), channel_id=1, source_target_pairs={{0,4},{1,5},{2,6},{3,7},{4,0},{5,1},{6,2},{7,3},{8,12},{9,13},{10,... | collective-permute-start | bytes 393224 | tf_op jit(solution)/shard_map/ppermute | solution.py:26
  5.9 7.1 %collective-permute-start.7 = (bf16[512,128]{1,0:T(8,128)(2,1)}, bf16[512,128]{1,0:T(8,128)(2,1)S(1)}, u32[]{:S(2)}, u32[]{:S(2)}) collective-permute-start(bf16[512,128]{1,0:T(8,128)(2,1)} %param.6), channel_id=1, source_target_pairs={{0,8},{1,17},{2,10},{3,19},{4,12},{5,21},{6,14},{7,23},{8,0},{9,25... | collective-permute-start | bytes 393224 | tf_op jit(solution)/shard_map/ppermute | solution.py:32
  7.4 7.7 %collective-permute-start.2 = (bf16[512,128]{1,0:T(8,128)(2,1)S(1)}, bf16[512,128]{1,0:T(8,128)(2,1)S(1)}, u32[]{:S(2)}, u32[]{:S(2)}) collective-permute-start(bf16[512,128]{1,0:T(8,128)(2,1)S(1)} %hidden.1.refs_2_), channel_id=1, source_target_pairs={{0,2},{1,3},{2,0},{3,1},{4,6},{5,7},{6,4},{7,5},{8,10},{9,11},{10,... | collective-permute-start | bytes 393224 | tf_op jit(solution)/shard_map/ppermute | solution.py:26
  9.0 4.0 %copy-start = (bf16[512,128]{1,0:T(8,128)(2,1)S(1)}, bf16[512,128]{1,0:T(8,128)(2,1)}, u32[]{:S(2)}) copy-start(bf16[512,128]{1,0:T(8,128)(2,1)} %param.6) | copy-start | bytes 393220
  12.3 5.0 %collective-permute-start.5 = (bf16[512,128]{1,0:T(8,128)(2,1)S(1)}, bf16[512,128]{1,0:T(8,128)(2,1)S(1)}, u32[]{:S(2)}, u32[]{:S(2)}) collective-permute-start(bf16[512,128]{1,0:T(8,128)(2,1)S(1)} %collective-permute-done.refs_6_), channel_id=1, source_target_pairs={{0,2},{1,3},{2,0},{3,1},{4,6},{5,7},{6,4},{7,5},{8,10},{9,11},{10,... | collective-permute-start | bytes 393224 | tf_op jit(solution)/shard_map/ppermute | solution.py:26
  13.0 9.6 %collective-permute-start.8 = (bf16[1024,128]{1,0:T(8,128)(2,1)S(1)}, bf16[1024,128]{1,0:T(8,128)(2,1)S(1)}, u32[]{:S(2)}, u32[]{:S(2)}) collective-permute-start(bf16[1024,128]{1,0:T(8,128)(2,1)S(1)} %pad_maximum_fusion.1), channel_id=1, source_target_pairs={{0,16},{1,9},{2,18},{3,11},{4,20},{5,13},{6,22},{7,15},{8,24},{9,1... | collective-permute-start | bytes 786440 | tf_op jit(solution)/shard_map/ppermute | solution.py:32
  14.6 2.7 %collective-permute-start.4 = (bf16[512,128]{1,0:T(8,128)(2,1)S(1)}, bf16[512,128]{1,0:T(8,128)(2,1)S(1)}, u32[]{:S(2)}, u32[]{:S(2)}) collective-permute-start(bf16[512,128]{1,0:T(8,128)(2,1)S(1)} %collective-permute-done.refs_6_), channel_id=1, source_target_pairs={{0,1},{1,0},{2,3},{3,2},{4,5},{5,4},{6,7},{7,6},{8,9},{9,8},{10,11... | collective-permute-start | bytes 393224 | tf_op jit(solution)/shard_map/ppermute | solution.py:26
  14.6 2.7 %collective-permute-start.1 = (bf16[512,128]{1,0:T(8,128)(2,1)S(1)}, bf16[512,128]{1,0:T(8,128)(2,1)S(1)}, u32[]{:S(2)}, u32[]{:S(2)}) collective-permute-start(bf16[512,128]{1,0:T(8,128)(2,1)S(1)} %hidden.1.refs_2_), channel_id=1, source_target_pairs={{0,1},{1,0},{2,3},{3,2},{4,5},{5,4},{6,7},{7,6},{8,9},{9,8},{10,11... | collective-permute-start | bytes 393224 | tf_op jit(solution)/shard_map/ppermute | solution.py:26
  15.1 2.2 %collective-permute-start.3 = (bf16[512,128]{1,0:T(8,128)(2,1)S(1)}, bf16[512,128]{1,0:T(8,128)(2,1)S(1)}, u32[]{:S(2)}, u32[]{:S(2)}) collective-permute-start(bf16[512,128]{1,0:T(8,128)(2,1)S(1)} %collective-permute-done.2.refs_4_), channel_id=1, source_target_pairs={{0,1},{1,0},{2,3},{3,2},{4,5},{5,4},{6,7},{7,6},{8,9},{9,8},{10,11... | collective-permute-start | bytes 393224 | tf_op jit(solution)/shard_map/ppermute | solution.py:26
  17.3 1.3 %collective-permute-start.6 = (bf16[512,128]{1,0:T(8,128)(2,1)S(1)}, bf16[512,128]{1,0:T(8,128)(2,1)S(1)}, u32[]{:S(2)}, u32[]{:S(2)}) collective-permute-start(bf16[512,128]{1,0:T(8,128)(2,1)S(1)} %collective-permute-done.5.refs_8_), channel_id=1, source_target_pairs={{0,1},{1,0},{2,3},{3,2},{4,5},{5,4},{6,7},{7,6},{8,9},{9,8},{10,11... | collective-permute-start | bytes 393224 | tf_op jit(solution)/shard_map/ppermute | solution.py:26
  19.1 7.3 %collective-permute-start.10 = (bf16[512,128]{1,0:T(8,128)(2,1)S(1)}, bf16[512,128]{1,0:T(8,128)(2,1)S(1)}, u32[]{:S(2)}, u32[]{:S(2)}) collective-permute-start(bf16[512,128]{1,0:T(8,128)(2,1)S(1)} %get-tuple-element.36), channel_id=1, source_target_pairs={{0,24},{8,16},{16,8},{24,0},{1,25},{9,17},{17,9},{25,1},{2,26},{10... | collective-permute-start | bytes 393224 | tf_op jit(solution)/shard_map/ppermute | solution.py:26
  21.9 6.9 %collective-permute-start.11 = (bf16[512,128]{1,0:T(8,128)(2,1)S(1)}, bf16[512,128]{1,0:T(8,128)(2,1)S(1)}, u32[]{:S(2)}, u32[]{:S(2)}) collective-permute-start(bf16[512,128]{1,0:T(8,128)(2,1)S(1)} %get-tuple-element.37), channel_id=1, source_target_pairs={{0,8},{8,0},{16,24},{24,16},{1,9},{9,1},{17,25},{25,17},{2,10},{10... | collective-permute-start | bytes 393224 | tf_op jit(solution)/shard_map/ppermute | solution.py:26
  22.2 6.6 %collective-permute-start.9 = (bf16[512,128]{1,0:T(8,128)(2,1)S(1)}, bf16[512,128]{1,0:T(8,128)(2,1)S(1)}, u32[]{:S(2)}, u32[]{:S(2)}) collective-permute-start(bf16[512,128]{1,0:T(8,128)(2,1)S(1)} %get-tuple-element.35), channel_id=1, source_target_pairs={{0,16},{8,24},{16,0},{24,8},{1,17},{9,25},{17,1},{25,9},{2,18},{10... | collective-permute-start | bytes 393224 | tf_op jit(solution)/shard_map/ppermute | solution.py:26

commit v7 on v6

--- a/solution.py
+++ b/solution.py
@@ -120,18 +120,17 @@
         total[places[3 * tiles + p]] += jnp.dot(adj[t], panel[places[t]], preferred_element_type=jnp.float32)
 
 
-def rest_kernel(per, places, adj, total, last, *refs):
-    *outs, blocks, extra = refs
+def rest_kernel(per, places, adj, start, last, *refs):
+    total, *outs, blocks = refs
     tiles = adj.shape[0]
     for i in range(per):
         blocks[i] = last[i * BLOCK : (i + 1) * BLOCK, :]
     blocks[per] = jnp.zeros_like(blocks[per])
-    extra[...] = jnp.zeros_like(extra)
 
     def body(g, carry):
         for i in range(GROUP):
             p = g * GROUP + i
-            extra[places[3 * tiles + p]] += jnp.dot(
+            total[places[3 * tiles + p]] += jnp.dot(
                 adj[places[2 * tiles + p]], blocks[places[4 * tiles + p]], preferred_element_type=jnp.float32
             )
         return carry
@@ -139,8 +138,7 @@
     lax.fori_loop(places[5 * tiles], tiles // GROUP, body, 0)
     for s, out in enumerate(outs):
         for i in range(per):
-            found = total[s * per + i] + extra[s * per + i]
-            out[i * BLOCK : (i + 1) * BLOCK, :] = found.astype(out.dtype)
+            out[i * BLOCK : (i + 1) * BLOCK, :] = total[s * per + i].astype(out.dtype)
 
 
 def scores_kernel(per, places, panel, last, keep, features, out, rows, cols, stage, sems):
@@ -247,12 +245,14 @@
         compiler_params=params,
         name="sums",
     )(places, *map(in_vmem, (adj, *slots)))
-    own, *parts = pl.pallas_call(
+    _, own, *parts = pl.pallas_call(
         functools.partial(rest_kernel, per),
         in_specs=[scalars] + [whole] * 3,
-        out_specs=[whole] * n_row,
-        out_shape=[VMEM((nodes, fin), jnp.float32)] + [VMEM((nodes, fin), jnp.bfloat16)] * (n_row - 1),
-        scratch_shapes=[VMEM((per + 1, BLOCK, fin), jnp.bfloat16), VMEM(total_shape, jnp.float32)],
+        out_specs=[whole] * (1 + n_row),
+        out_shape=[VMEM(total_shape, jnp.float32), VMEM((nodes, fin), jnp.float32)]
+        + [VMEM((nodes, fin), jnp.bfloat16)] * (n_row - 1),
+        scratch_shapes=[VMEM((per + 1, BLOCK, fin), jnp.bfloat16)],
+        input_output_aliases={2: 0},
         cost_estimate=pl.CostEstimate(flops=0, bytes_accessed=4096, transcendentals=0),
         compiler_params=params,
         name="rest",

time: 29.6 us -> 29.5 us (level)
  no operation moved by 1% of the time
where the time goes in v7:
time: 29.5 us; the launch traced here: 29.4 us
  starting transfers between devices  13.5 us (46%)
  Pallas kernels  7.42 us (25%)
  waiting for transfers between devices  7.02 us (24%)
  other arithmetic  0.77 us (3%)
  between operations  0.7 us (2%)
    ppermute x10, starting transfers between devices, swap(): return lax.ppermute(x, axis, [(i, i ^ mask) for i in range(size)])  10.4 us
    ppermute x10, waiting for transfers between devices, swap(): return lax.ppermute(x, axis, [(i, i ^ mask) for i in range(size)])  7.01 us
    pallas_call x1, Pallas kernels, local(): pl.pallas_call(prep_kernel, in_specs=[far, far, far], out_specs=[whole, w...  3.09 us
    ppermute x2, starting transfers between devices, swap_rows(): return lax.ppermute(x, ('row', 'col'), pairs)  3.07 us
    pallas_call x1, Pallas kernels, local(): pl.pallas_call(functools.partial(scores_kernel, per), in_specs=[scalars]...  1.92 us
    pallas_call x1, Pallas kernels, local(): pl.pallas_call(hidden_kernel, in_specs=[far, far], out_specs=whole, out_s...  1.19 us
    pallas_call x1, Pallas kernels, local(): pl.pallas_call(functools.partial(sums_kernel, per), in_specs=[scalars] +...  0.92 us
    convert_element_type x1, other arithmetic, local(): return (edge_grad, own.astype(jnp.bfloat16))  0.72 us
  transfers between devices with their start and end apart: 12, of which 5 were waited for; matrix products, arithmetic and copies ran while one was open for 0% of the time, Pallas kernels for 21%

profile of v7, /device:TPU:0, one launch (start us, length us, event | category | flops | bytes accessed | tf_op | source)
XLA Modules:
  0.0 29.4 jit_solution(11901541303830983704)
XLA Ops:
  0.6 1.2 %hidden.1.refs_2_ = bf16[512,128]{1,0:T(8,128)(2,1)S(1)} custom-call(bf16[512,256]{1,0:T(8,128)(2,1)} %grads.1, bf16[128,256]{1,0:T(8,128)(2,1)} %weight.1), custom_call_target="tpu_custom_call" | custom-call | tf_op jit(solution)/shard_map/hidden/pallas_call | solution.py:175
  1.8 4.1 %collective-permute-start = (bf16[512,128]{1,0:T(8,128)(2,1)S(1)}, bf16[512,128]{1,0:T(8,128)(2,1)S(1)}, u32[]{:S(2)}, u32[]{:S(2)}) collective-permute-start(bf16[512,128]{1,0:T(8,128)(2,1)S(1)} %hidden.1.refs_2_), channel_id=1, source_target_pairs={{0,4},{1,5},{2,6},{3,7},{4,0},{5,1},{6,2},{7,3},{8,12},{9,13},{10,... | collective-permute-start | bytes 393224 | tf_op jit(solution)/shard_map/ppermute | solution.py:26
  5.9 1.5 %collective-permute-start.7 = (bf16[512,128]{1,0:T(8,128)(2,1)}, bf16[512,128]{1,0:T(8,128)(2,1)S(1)}, u32[]{:S(2)}, u32[]{:S(2)}) collective-permute-start(bf16[512,128]{1,0:T(8,128)(2,1)} %param.6), channel_id=1, source_target_pairs={{0,8},{1,17},{2,10},{3,19},{4,12},{5,21},{6,14},{7,23},{8,0},{9,25... | collective-permute-start | bytes 393224 | tf_op jit(solution)/shard_map/ppermute | solution.py:32
  7.4 1.6 %collective-permute-start.2 = (bf16[512,128]{1,0:T(8,128)(2,1)S(1)}, bf16[512,128]{1,0:T(8,128)(2,1)S(1)}, u32[]{:S(2)}, u32[]{:S(2)}) collective-permute-start(bf16[512,128]{1,0:T(8,128)(2,1)S(1)} %hidden.1.refs_2_), channel_id=1, source_target_pairs={{0,2},{1,3},{2,0},{3,1},{4,6},{5,7},{6,4},{7,5},{8,10},{9,11},{10,... | collective-permute-start | bytes 393224 | tf_op jit(solution)/shard_map/ppermute | solution.py:26
  9.0 0.0 copy-start
  9.0 3.1 %prep.1 = (bf16[64,128,128]{2,1,0:T(8,128)(2,1)S(1)}, bf16[64,128,128]{2,1,0:T(8,128)(2,1)S(1)}, s32[1,3,1,64]{3,2,1,0:T(1,128)S(4)}) custom-call(s32[1,3,1,64]{3,2,1,0:T(1,128)} %bitcast.1, s32[1,1,64,128,128]{4,3,2,1,0:T(8,128)} %mask.1, bf16[1,1,64,128,128]{4,3,2,1,0:T(8,128)(2,1)} %weights.1), custom_call_target="tpu_custom_call" | custom-call | bytes 4096 | tf_op jit(solution)/shard_map/prep/pallas_call | solution.py:199
  12.1 0.2 collective-permute-done.refs_6_
  12.3 0.7 %collective-permute-start.5 = (bf16[512,128]{1,0:T(8,128)(2,1)S(1)}, bf16[512,128]{1,0:T(8,128)(2,1)S(1)}, u32[]{:S(2)}, u32[]{:S(2)}) collective-permute-start(bf16[512,128]{1,0:T(8,128)(2,1)S(1)} %collective-permute-done.refs_6_), channel_id=1, source_target_pairs={{0,2},{1,3},{2,0},{3,1},{4,6},{5,7},{6,4},{7,5},{8,10},{9,11},{10,... | collective-permute-start | bytes 393224 | tf_op jit(solution)/shard_map/ppermute | solution.py:26
  13.0 0.0 collective-permute-done.7
  13.0 0.0 copy-done
  13.0 1.6 %collective-permute-start.8 = (bf16[1024,128]{1,0:T(8,128)(2,1)S(1)}, bf16[1024,128]{1,0:T(8,128)(2,1)S(1)}, u32[]{:S(2)}, u32[]{:S(2)}) collective-permute-start(bf16[1024,128]{1,0:T(8,128)(2,1)S(1)} %pad_maximum_fusion.1), channel_id=1, source_target_pairs={{0,16},{1,9},{2,18},{3,11},{4,20},{5,13},{6,22},{7,15},{8,24},{9,1... | collective-permute-start | bytes 786440 | tf_op jit(solution)/shard_map/ppermute | solution.py:32
  14.6 0.0 collective-permute-start.4
  14.6 0.5 %collective-permute-start.1 = (bf16[512,128]{1,0:T(8,128)(2,1)S(1)}, bf16[512,128]{1,0:T(8,128)(2,1)S(1)}, u32[]{:S(2)}, u32[]{:S(2)}) collective-permute-start(bf16[512,128]{1,0:T(8,128)(2,1)S(1)} %hidden.1.refs_2_), channel_id=1, source_target_pairs={{0,1},{1,0},{2,3},{3,2},{4,5},{5,4},{6,7},{7,6},{8,9},{9,8},{10,11... | collective-permute-start | bytes 393224 | tf_op jit(solution)/shard_map/ppermute | solution.py:26
  15.1 0.0 collective-permute-done.2.refs_4_
  15.1 0.0 collective-permute-start.3
  15.1 2.2 %collective-permute-done.5.refs_8_ = bf16[512,128]{1,0:T(8,128)(2,1)S(1)} collective-permute-done((bf16[512,128]{1,0:T(8,128)(2,1)S(1)}, bf16[512,128]{1,0:T(8,128)(2,1)S(1)}, u32[]{:S(2)}, u32[]{:S(2)}) %collective-permute-start.5) | collective-permute-done | bytes 131104 | tf_op jit(solution)/shard_map/ppermute | solution.py:26
  17.3 0.0 collective-permute-start.6
  17.3 0.0 collective-permute-done.4.refs_7_
  17.3 0.0 collective-permute-done.1.refs_3_
  17.3 0.0 collective-permute-done.3.refs_5_
  17.3 0.9 %sums.1 = (bf16[32,128,128]{2,1,0:T(8,128)(2,1)S(1)}, f32[16,128,128]{2,1,0:T(8,128)S(1)}) custom-call(s32[321]{0:T(512)S(4)} %places.1.refs_0_, bf16[64,128,128]{2,1,0:T(8,128)(2,1)S(1)} %get-tuple-element.24.refs_1_.adj, bf16[512,128]{1,0:T(8,128)(2,1)S(1)} %hidden.1.refs_2_, bf16[512,128]{1,0:T(8,128)(2,1)S(1)} %collective-permute-done.1.refs_3_, ...), custom_call_target="tpu_custom_call" | custom-call | flops 268435456 | bytes 1048576 | tf_op jit(solution)/shard_map/sums/pallas_call | solution.py:239
  18.3 0.4 %collective-permute-done.6.last = bf16[512,128]{1,0:T(8,128)(2,1)S(1)} collective-permute-done((bf16[512,128]{1,0:T(8,128)(2,1)S(1)}, bf16[512,128]{1,0:T(8,128)(2,1)S(1)}, u32[]{:S(2)}, u32[]{:S(2)}) %collective-permute-start.6) | collective-permute-done | bytes 131104 | tf_op jit(solution)/shard_map/ppermute | solution.py:26
  18.7 0.3 %rest.1 = (f32[16,128,128]{2,1,0:T(8,128)S(1)}, f32[512,128]{1,0:T(8,128)S(1)}, bf16[512,128]{1,0:T(8,128)(2,1)S(1)}, bf16[512,128]{1,0:T(8,128)(2,1)S(1)}, bf16[512,128]{1,0:T(8,128)(2,1)S(1)}) custom-call(s32[321]{0:T(512)S(4)} %places.1.refs_0_, bf16[64,128,128]{2,1,0:T(8,128)(2,1)S(1)} %get-tuple-element.24.refs_1_.adj, ...), custom_call_target="tpu_custom_call", output_to_operand_aliasing={{0}: (2, {})} | custom-call | bytes 4096 | tf_op jit(solution)/shard_map/rest/pallas_call | solution.py:248
  19.0 2.8 %collective-permute-start.10 = (bf16[512,128]{1,0:T(8,128)(2,1)S(1)}, bf16[512,128]{1,0:T(8,128)(2,1)S(1)}, u32[]{:S(2)}, u32[]{:S(2)}) collective-permute-start(bf16[512,128]{1,0:T(8,128)(2,1)S(1)} %get-tuple-element.36), channel_id=1, source_target_pairs={{0,24},{8,16},{16,8},{24,0},{1,25},{9,17},{17,9},{25,1},{2,26},{10... | collective-permute-start | bytes 393224 | tf_op jit(solution)/shard_map/ppermute | solution.py:26
  21.8 0.3 %collective-permute-start.11 = (bf16[512,128]{1,0:T(8,128)(2,1)S(1)}, bf16[512,128]{1,0:T(8,128)(2,1)S(1)}, u32[]{:S(2)}, u32[]{:S(2)}) collective-permute-start(bf16[512,128]{1,0:T(8,128)(2,1)S(1)} %get-tuple-element.37), channel_id=1, source_target_pairs={{0,8},{8,0},{16,24},{24,16},{1,9},{9,1},{17,25},{25,17},{2,10},{10... | collective-permute-start | bytes 393224 | tf_op jit(solution)/shard_map/ppermute | solution.py:26
  22.1 0.4 %collective-permute-start.9 = (bf16[512,128]{1,0:T(8,128)(2,1)S(1)}, bf16[512,128]{1,0:T(8,128)(2,1)S(1)}, u32[]{:S(2)}, u32[]{:S(2)}) collective-permute-start(bf16[512,128]{1,0:T(8,128)(2,1)S(1)} %get-tuple-element.35), channel_id=1, source_target_pairs={{0,16},{8,24},{16,0},{24,8},{1,17},{9,25},{17,1},{25,9},{2,18},{10... | collective-permute-start | bytes 393224 | tf_op jit(solution)/shard_map/ppermute | solution.py:26
  22.5 0.0 collective-permute-done.8
  22.6 1.9 %scores.1 = bf16[1,1,64,128,128]{4,3,2,1,0:T(8,128)(2,1)} custom-call(s32[321]{0:T(512)S(4)} %places.1.refs_0_, bf16[32,128,128]{2,1,0:T(8,128)(2,1)S(1)} %get-tuple-element.27.panel, bf16[512,128]{1,0:T(8,128)(2,1)S(1)} %collective-permute-done.6.last, bf16[64,128,128]{2,1,0:T(8,128)(2,1)S(1)} %get-tuple-element.30.keep, ...), custom_call_target="tpu_custom_call" | custom-call | flops 268435456 | bytes 4194304 | tf_op jit(solution)/shard_map/scores/pallas_call | solution.py:265
  24.5 1.8 %collective-permute-done.10 = bf16[512,128]{1,0:T(8,128)(2,1)S(1)} collective-permute-done((bf16[512,128]{1,0:T(8,128)(2,1)S(1)}, bf16[512,128]{1,0:T(8,128)(2,1)S(1)}, u32[]{:S(2)}, u32[]{:S(2)}) %collective-permute-start.10) | collective-permute-done | bytes 131104 | tf_op jit(solution)/shard_map/ppermute | solution.py:26
  26.3 2.4 %collective-permute-done.11 = bf16[512,128]{1,0:T(8,128)(2,1)S(1)} collective-permute-done((bf16[512,128]{1,0:T(8,128)(2,1)S(1)}, bf16[512,128]{1,0:T(8,128)(2,1)S(1)}, u32[]{:S(2)}, u32[]{:S(2)}) %collective-permute-start.11) | collective-permute-done | bytes 131104 | tf_op jit(solution)/shard_map/ppermute | solution.py:26
  28.7 0.0 collective-permute-done.9
  28.7 0.7 %add_convert_fusion = bf16[512,128]{1,0:T(8,128)(2,1)} fusion(bf16[512,128]{1,0:T(8,128)(2,1)S(1)} %collective-permute-done.11, bf16[512,128]{1,0:T(8,128)(2,1)S(1)} %collective-permute-done.10, f32[512,128]{1,0:T(8,128)S(1)} %get-tuple-element.34, bf16[512,128]{1,0:T(8,128)(2,1)S(1)} %collective-permute-done.9), kind=kLoop, calls=%fused_computation.2 | loop fusion | flops 458752 | bytes 786432 | tf_op jit(solution)/shard_map/convert_element_type | solution.py:283
  (3 shorter events, 0.1 us)
Async XLA Ops:
  1.8 10.5 %collective-permute-start = (bf16[512,128]{1,0:T(8,128)(2,1)S(1)}, bf16[512,128]{1,0:T(8,128)(2,1)S(1)}, u32[]{:S(2)}, u32[]{:S(2)}) collective-permute-start(bf16[512,128]{1,0:T(8,128)(2,1)S(1)} %hidden.1.refs_2_), channel_id=1, source_target_pairs={{0,4},{1,5},{2,6},{3,7},{4,0},{5,1},{6,2},{7,3},{8,12},{9,13},{10,... | collective-permute-start | bytes 393224 | tf_op jit(solution)/shard_map/ppermute | solution.py:26
  5.9 7.1 %collective-permute-start.7 = (bf16[512,128]{1,0:T(8,128)(2,1)}, bf16[512,128]{1,0:T(8,128)(2,1)S(1)}, u32[]{:S(2)}, u32[]{:S(2)}) collective-permute-start(bf16[512,128]{1,0:T(8,128)(2,1)} %param.6), channel_id=1, source_target_pairs={{0,8},{1,17},{2,10},{3,19},{4,12},{5,21},{6,14},{7,23},{8,0},{9,25... | collective-permute-start | bytes 393224 | tf_op jit(solution)/shard_map/ppermute | solution.py:32
  7.4 7.7 %collective-permute-start.2 = (bf16[512,128]{1,0:T(8,128)(2,1)S(1)}, bf16[512,128]{1,0:T(8,128)(2,1)S(1)}, u32[]{:S(2)}, u32[]{:S(2)}) collective-permute-start(bf16[512,128]{1,0:T(8,128)(2,1)S(1)} %hidden.1.refs_2_), channel_id=1, source_target_pairs={{0,2},{1,3},{2,0},{3,1},{4,6},{5,7},{6,4},{7,5},{8,10},{9,11},{10,... | collective-permute-start | bytes 393224 | tf_op jit(solution)/shard_map/ppermute | solution.py:26
  9.0 4.0 %copy-start = (bf16[512,128]{1,0:T(8,128)(2,1)S(1)}, bf16[512,128]{1,0:T(8,128)(2,1)}, u32[]{:S(2)}) copy-start(bf16[512,128]{1,0:T(8,128)(2,1)} %param.6) | copy-start | bytes 393220
  12.3 5.0 %collective-permute-start.5 = (bf16[512,128]{1,0:T(8,128)(2,1)S(1)}, bf16[512,128]{1,0:T(8,128)(2,1)S(1)}, u32[]{:S(2)}, u32[]{:S(2)}) collective-permute-start(bf16[512,128]{1,0:T(8,128)(2,1)S(1)} %collective-permute-done.refs_6_), channel_id=1, source_target_pairs={{0,2},{1,3},{2,0},{3,1},{4,6},{5,7},{6,4},{7,5},{8,10},{9,11},{10,... | collective-permute-start | bytes 393224 | tf_op jit(solution)/shard_map/ppermute | solution.py:26
  13.0 9.5 %collective-permute-start.8 = (bf16[1024,128]{1,0:T(8,128)(2,1)S(1)}, bf16[1024,128]{1,0:T(8,128)(2,1)S(1)}, u32[]{:S(2)}, u32[]{:S(2)}) collective-permute-start(bf16[1024,128]{1,0:T(8,128)(2,1)S(1)} %pad_maximum_fusion.1), channel_id=1, source_target_pairs={{0,16},{1,9},{2,18},{3,11},{4,20},{5,13},{6,22},{7,15},{8,24},{9,1... | collective-permute-start | bytes 786440 | tf_op jit(solution)/shard_map/ppermute | solution.py:32
  14.6 2.7 %collective-permute-start.4 = (bf16[512,128]{1,0:T(8,128)(2,1)S(1)}, bf16[512,128]{1,0:T(8,128)(2,1)S(1)}, u32[]{:S(2)}, u32[]{:S(2)}) collective-permute-start(bf16[512,128]{1,0:T(8,128)(2,1)S(1)} %collective-permute-done.refs_6_), channel_id=1, source_target_pairs={{0,1},{1,0},{2,3},{3,2},{4,5},{5,4},{6,7},{7,6},{8,9},{9,8},{10,11... | collective-permute-start | bytes 393224 | tf_op jit(solution)/shard_map/ppermute | solution.py:26
  14.6 2.7 %collective-permute-start.1 = (bf16[512,128]{1,0:T(8,128)(2,1)S(1)}, bf16[512,128]{1,0:T(8,128)(2,1)S(1)}, u32[]{:S(2)}, u32[]{:S(2)}) collective-permute-start(bf16[512,128]{1,0:T(8,128)(2,1)S(1)} %hidden.1.refs_2_), channel_id=1, source_target_pairs={{0,1},{1,0},{2,3},{3,2},{4,5},{5,4},{6,7},{7,6},{8,9},{9,8},{10,11... | collective-permute-start | bytes 393224 | tf_op jit(solution)/shard_map/ppermute | solution.py:26
  15.1 2.2 %collective-permute-start.3 = (bf16[512,128]{1,0:T(8,128)(2,1)S(1)}, bf16[512,128]{1,0:T(8,128)(2,1)S(1)}, u32[]{:S(2)}, u32[]{:S(2)}) collective-permute-start(bf16[512,128]{1,0:T(8,128)(2,1)S(1)} %collective-permute-done.2.refs_4_), channel_id=1, source_target_pairs={{0,1},{1,0},{2,3},{3,2},{4,5},{5,4},{6,7},{7,6},{8,9},{9,8},{10,11... | collective-permute-start | bytes 393224 | tf_op jit(solution)/shard_map/ppermute | solution.py:26
  17.3 1.3 %collective-permute-start.6 = (bf16[512,128]{1,0:T(8,128)(2,1)S(1)}, bf16[512,128]{1,0:T(8,128)(2,1)S(1)}, u32[]{:S(2)}, u32[]{:S(2)}) collective-permute-start(bf16[512,128]{1,0:T(8,128)(2,1)S(1)} %collective-permute-done.5.refs_8_), channel_id=1, source_target_pairs={{0,1},{1,0},{2,3},{3,2},{4,5},{5,4},{6,7},{7,6},{8,9},{9,8},{10,11... | collective-permute-start | bytes 393224 | tf_op jit(solution)/shard_map/ppermute | solution.py:26
  19.0 7.3 %collective-permute-start.10 = (bf16[512,128]{1,0:T(8,128)(2,1)S(1)}, bf16[512,128]{1,0:T(8,128)(2,1)S(1)}, u32[]{:S(2)}, u32[]{:S(2)}) collective-permute-start(bf16[512,128]{1,0:T(8,128)(2,1)S(1)} %get-tuple-element.36), channel_id=1, source_target_pairs={{0,24},{8,16},{16,8},{24,0},{1,25},{9,17},{17,9},{25,1},{2,26},{10... | collective-permute-start | bytes 393224 | tf_op jit(solution)/shard_map/ppermute | solution.py:26
  21.8 6.9 %collective-permute-start.11 = (bf16[512,128]{1,0:T(8,128)(2,1)S(1)}, bf16[512,128]{1,0:T(8,128)(2,1)S(1)}, u32[]{:S(2)}, u32[]{:S(2)}) collective-permute-start(bf16[512,128]{1,0:T(8,128)(2,1)S(1)} %get-tuple-element.37), channel_id=1, source_target_pairs={{0,8},{8,0},{16,24},{24,16},{1,9},{9,1},{17,25},{25,17},{2,10},{10... | collective-permute-start | bytes 393224 | tf_op jit(solution)/shard_map/ppermute | solution.py:26
  22.1 6.6 %collective-permute-start.9 = (bf16[512,128]{1,0:T(8,128)(2,1)S(1)}, bf16[512,128]{1,0:T(8,128)(2,1)S(1)}, u32[]{:S(2)}, u32[]{:S(2)}) collective-permute-start(bf16[512,128]{1,0:T(8,128)(2,1)S(1)} %get-tuple-element.35), channel_id=1, source_target_pairs={{0,16},{8,24},{16,0},{24,8},{1,17},{9,25},{17,1},{25,9},{2,18},{10... | collective-permute-start | bytes 393224 | tf_op jit(solution)/shard_map/ppermute | solution.py:26

commit v8 on v7

--- a/solution.py
+++ b/solution.py
@@ -120,7 +120,7 @@
         total[places[3 * tiles + p]] += jnp.dot(adj[t], panel[places[t]], preferred_element_type=jnp.float32)
 
 
-def rest_kernel(per, places, adj, start, last, *refs):
+def rest_kernel(per, pairs, places, adj, start, last, *refs):
     total, *outs, blocks = refs
     tiles = adj.shape[0]
     for i in range(per):
@@ -136,9 +136,11 @@
         return carry
 
     lax.fori_loop(places[5 * tiles], tiles // GROUP, body, 0)
-    for s, out in enumerate(outs):
+    core = lax.axis_index("col") % 2
+    for (even, odd), out in zip(pairs, outs, strict=True):
+        chunk = (even + core * (odd - even)) * per
         for i in range(per):
-            out[i * BLOCK : (i + 1) * BLOCK, :] = total[s * per + i].astype(out.dtype)
+            out[i * BLOCK : (i + 1) * BLOCK, :] = total[chunk + i].astype(out.dtype)
 
 
 def scores_kernel(per, places, panel, last, keep, features, out, rows, cols, stage, sems):
@@ -245,8 +247,13 @@
         compiler_params=params,
         name="sums",
     )(places, *map(in_vmem, (adj, *slots)))
+    if n_row == 4:
+        pairs = [(3, 3), (1, 2), (2, 1)]
+    else:
+        pairs = [(s, s) for s in sorted(range(1, n_row), key=lambda s: -s.bit_count())]
+    pairs = pairs[-1:] + pairs[:-1]
     _, own, *parts = pl.pallas_call(
-        functools.partial(rest_kernel, per),
+        functools.partial(rest_kernel, per, [(0, 0)] + pairs),
         in_specs=[scalars] + [whole] * 3,
         out_specs=[whole] * (1 + n_row),
         out_shape=[VMEM(total_shape, jnp.float32), VMEM((nodes, fin), jnp.float32)]
@@ -258,9 +265,7 @@
         name="rest",
     )(places, *map(in_vmem, (adj, total, last)))
 
-    order = sorted(range(1, n_row), key=lambda s: -s.bit_count())
-    order = order[-1:] + order[:-1]
-    got = [swap(parts[s - 1], "row", n_row, s) for s in order]
+    got = [swap_rows(x, n_row, n_col, *pair) for x, pair in zip(parts, pairs, strict=True)]
 
     edge_grad = pl.pallas_call(
         functools.partial(scores_kernel, per),

time: 29.5 us -> 29.4 us (level)
  waiting for transfers between devices: 7.02 us -> 6.63 us
    ppermute x10 -> x7, waiting for transfers between devices: 7.01 us -> 2.83 us  [swap(): return lax.ppermute(x, axis, [(i, i ^ mask) for i in range(size)])]
    ppermute x2 -> x5, waiting for transfers between devices: 0.01 us -> 3.8 us  [swap_rows(): return lax.ppermute(x, ('row', 'col'), pairs)]
    ppermute x10 -> x7, starting transfers between devices: 10.4 us -> 6.87 us  [swap(): return lax.ppermute(x, axis, [(i, i ^ mask) for i in range(size)])]
    ppermute x2 -> x5, starting transfers between devices: 3.07 us -> 6.63 us  [swap_rows(): return lax.ppermute(x, ('row', 'col'), pairs)]
  transfers between devices with their start and end apart: 12 -> 12, of which waited for: 5 -> 6; matrix products, arithmetic and copies ran while one was open for 0% -> 0% of each run, Pallas kernels for 21% -> 22%
where the time goes in v8:
time: 29.4 us; the launch traced here: 29.2 us
  starting transfers between devices  13.5 us (46%)
  Pallas kernels  7.65 us (26%)
  waiting for transfers between devices  6.63 us (23%)
  other arithmetic  0.77 us (3%)
  between operations  0.7 us (2%)
    ppermute x7, starting transfers between devices, swap(): return lax.ppermute(x, axis, [(i, i ^ mask) for i in range(size)])  6.87 us
    ppermute x5, starting transfers between devices, swap_rows(): return lax.ppermute(x, ('row', 'col'), pairs)  6.63 us
    ppermute x5, waiting for transfers between devices, swap_rows(): return lax.ppermute(x, ('row', 'col'), pairs)  3.8 us
    pallas_call x1, Pallas kernels, local(): pl.pallas_call(prep_kernel, in_specs=[far, far, far], out_specs=[whole, w...  3.09 us
    ppermute x7, waiting for transfers between devices, swap(): return lax.ppermute(x, axis, [(i, i ^ mask) for i in range(size)])  2.83 us
    pallas_call x1, Pallas kernels, local(): pl.pallas_call(functools.partial(scores_kernel, per), in_specs=[scalars]...  1.92 us
    pallas_call x1, Pallas kernels, local(): pl.pallas_call(hidden_kernel, in_specs=[far, far], out_specs=whole, out_s...  1.19 us
    pallas_call x1, Pallas kernels, local(): pl.pallas_call(functools.partial(sums_kernel, per), in_specs=[scalars] +...  0.92 us
  transfers between devices with their start and end apart: 12, of which 6 were waited for; matrix products, arithmetic and copies ran while one was open for 0% of the time, Pallas kernels for 22%

profile of v8, /device:TPU:0, one launch (start us, length us, event | category | flops | bytes accessed | tf_op | source)
XLA Modules:
  0.0 29.2 jit_solution(11683263168633715762)
XLA Ops:
  0.6 1.2 %hidden.1.refs_2_ = bf16[512,128]{1,0:T(8,128)(2,1)S(1)} custom-call(bf16[512,256]{1,0:T(8,128)(2,1)} %grads.1, bf16[128,256]{1,0:T(8,128)(2,1)} %weight.1), custom_call_target="tpu_custom_call" | custom-call | tf_op jit(solution)/shard_map/hidden/pallas_call | solution.py:177
  1.8 4.1 %collective-permute-start = (bf16[512,128]{1,0:T(8,128)(2,1)S(1)}, bf16[512,128]{1,0:T(8,128)(2,1)S(1)}, u32[]{:S(2)}, u32[]{:S(2)}) collective-permute-start(bf16[512,128]{1,0:T(8,128)(2,1)S(1)} %hidden.1.refs_2_), channel_id=1, source_target_pairs={{0,4},{1,5},{2,6},{3,7},{4,0},{5,1},{6,2},{7,3},{8,12},{9,13},{10,... | collective-permute-start | bytes 393224 | tf_op jit(solution)/shard_map/ppermute | solution.py:26
  5.9 1.5 %collective-permute-start.7 = (bf16[512,128]{1,0:T(8,128)(2,1)}, bf16[512,128]{1,0:T(8,128)(2,1)S(1)}, u32[]{:S(2)}, u32[]{:S(2)}) collective-permute-start(bf16[512,128]{1,0:T(8,128)(2,1)} %param.6), channel_id=1, source_target_pairs={{0,8},{1,17},{2,10},{3,19},{4,12},{5,21},{6,14},{7,23},{8,0},{9,25... | collective-permute-start | bytes 393224 | tf_op jit(solution)/shard_map/ppermute | solution.py:32
  7.4 1.6 %collective-permute-start.2 = (bf16[512,128]{1,0:T(8,128)(2,1)S(1)}, bf16[512,128]{1,0:T(8,128)(2,1)S(1)}, u32[]{:S(2)}, u32[]{:S(2)}) collective-permute-start(bf16[512,128]{1,0:T(8,128)(2,1)S(1)} %hidden.1.refs_2_), channel_id=1, source_target_pairs={{0,2},{1,3},{2,0},{3,1},{4,6},{5,7},{6,4},{7,5},{8,10},{9,11},{10,... | collective-permute-start | bytes 393224 | tf_op jit(solution)/shard_map/ppermute | solution.py:26
  9.0 0.0 copy-start
  9.0 3.1 %prep.1 = (bf16[64,128,128]{2,1,0:T(8,128)(2,1)S(1)}, bf16[64,128,128]{2,1,0:T(8,128)(2,1)S(1)}, s32[1,3,1,64]{3,2,1,0:T(1,128)S(4)}) custom-call(s32[1,3,1,64]{3,2,1,0:T(1,128)} %bitcast.1, s32[1,1,64,128,128]{4,3,2,1,0:T(8,128)} %mask.1, bf16[1,1,64,128,128]{4,3,2,1,0:T(8,128)(2,1)} %weights.1), custom_call_target="tpu_custom_call" | custom-call | bytes 4096 | tf_op jit(solution)/shard_map/prep/pallas_call | solution.py:201
  12.1 0.2 collective-permute-done.refs_6_
  12.3 0.7 %collective-permute-start.5 = (bf16[512,128]{1,0:T(8,128)(2,1)S(1)}, bf16[512,128]{1,0:T(8,128)(2,1)S(1)}, u32[]{:S(2)}, u32[]{:S(2)}) collective-permute-start(bf16[512,128]{1,0:T(8,128)(2,1)S(1)} %collective-permute-done.refs_6_), channel_id=1, source_target_pairs={{0,2},{1,3},{2,0},{3,1},{4,6},{5,7},{6,4},{7,5},{8,10},{9,11},{10,... | collective-permute-start | bytes 393224 | tf_op jit(solution)/shard_map/ppermute | solution.py:26
  13.0 0.0 collective-permute-done.7
  13.0 0.0 copy-done
  13.0 1.6 %collective-permute-start.8 = (bf16[1024,128]{1,0:T(8,128)(2,1)S(1)}, bf16[1024,128]{1,0:T(8,128)(2,1)S(1)}, u32[]{:S(2)}, u32[]{:S(2)}) collective-permute-start(bf16[1024,128]{1,0:T(8,128)(2,1)S(1)} %pad_maximum_fusion.1), channel_id=1, source_target_pairs={{0,16},{1,9},{2,18},{3,11},{4,20},{5,13},{6,22},{7,15},{8,24},{9,1... | collective-permute-start | bytes 786440 | tf_op jit(solution)/shard_map/ppermute | solution.py:32
  14.6 0.0 collective-permute-start.4
  14.6 0.5 %collective-permute-start.1 = (bf16[512,128]{1,0:T(8,128)(2,1)S(1)}, bf16[512,128]{1,0:T(8,128)(2,1)S(1)}, u32[]{:S(2)}, u32[]{:S(2)}) collective-permute-start(bf16[512,128]{1,0:T(8,128)(2,1)S(1)} %hidden.1.refs_2_), channel_id=1, source_target_pairs={{0,1},{1,0},{2,3},{3,2},{4,5},{5,4},{6,7},{7,6},{8,9},{9,8},{10,11... | collective-permute-start | bytes 393224 | tf_op jit(solution)/shard_map/ppermute | solution.py:26
  15.1 0.0 collective-permute-done.2.refs_4_
  15.1 0.0 collective-permute-start.3
  15.1 2.2 %collective-permute-done.5.refs_8_ = bf16[512,128]{1,0:T(8,128)(2,1)S(1)} collective-permute-done((bf16[512,128]{1,0:T(8,128)(2,1)S(1)}, bf16[512,128]{1,0:T(8,128)(2,1)S(1)}, u32[]{:S(2)}, u32[]{:S(2)}) %collective-permute-start.5) | collective-permute-done | bytes 131104 | tf_op jit(solution)/shard_map/ppermute | solution.py:26
  17.3 0.0 collective-permute-start.6
  17.3 0.0 collective-permute-done.4.refs_7_
  17.3 0.0 collective-permute-done.1.refs_3_
  17.3 0.0 collective-permute-done.3.refs_5_
  17.3 0.9 %sums.1 = (bf16[32,128,128]{2,1,0:T(8,128)(2,1)S(1)}, f32[16,128,128]{2,1,0:T(8,128)S(1)}) custom-call(s32[321]{0:T(512)S(4)} %places.1.refs_0_, bf16[64,128,128]{2,1,0:T(8,128)(2,1)S(1)} %get-tuple-element.24.refs_1_.adj, bf16[512,128]{1,0:T(8,128)(2,1)S(1)} %hidden.1.refs_2_, bf16[512,128]{1,0:T(8,128)(2,1)S(1)} %collective-permute-done.1.refs_3_, ...), custom_call_target="tpu_custom_call" | custom-call | flops 268435456 | bytes 1048576 | tf_op jit(solution)/shard_map/sums/pallas_call | solution.py:241
  18.3 0.4 %collective-permute-done.6.last = bf16[512,128]{1,0:T(8,128)(2,1)S(1)} collective-permute-done((bf16[512,128]{1,0:T(8,128)(2,1)S(1)}, bf16[512,128]{1,0:T(8,128)(2,1)S(1)}, u32[]{:S(2)}, u32[]{:S(2)}) %collective-permute-start.6) | collective-permute-done | bytes 131104 | tf_op jit(solution)/shard_map/ppermute | solution.py:26
  18.7 0.5 %rest.1 = (f32[16,128,128]{2,1,0:T(8,128)S(1)}, f32[512,128]{1,0:T(8,128)S(1)}, bf16[512,128]{1,0:T(8,128)(2,1)S(1)}, bf16[512,128]{1,0:T(8,128)(2,1)S(1)}, bf16[512,128]{1,0:T(8,128)(2,1)S(1)}) custom-call(s32[321]{0:T(512)S(4)} %places.1.refs_0_, bf16[64,128,128]{2,1,0:T(8,128)(2,1)S(1)} %get-tuple-element.24.refs_1_.adj, ...), custom_call_target="tpu_custom_call", output_to_operand_aliasing={{0}: (2, {})} | custom-call | bytes 4096 | tf_op jit(solution)/shard_map/rest/pallas_call | solution.py:255
  19.2 2.3 %collective-permute-start.10 = (bf16[512,128]{1,0:T(8,128)(2,1)S(1)}, bf16[512,128]{1,0:T(8,128)(2,1)S(1)}, u32[]{:S(2)}, u32[]{:S(2)}) collective-permute-start(bf16[512,128]{1,0:T(8,128)(2,1)S(1)} %get-tuple-element.36), channel_id=1, source_target_pairs={{0,24},{1,25},{2,26},{3,27},{4,28},{5,29},{6,30},{7,31},{8,16},{9,... | collective-permute-start | bytes 393224 | tf_op jit(solution)/shard_map/ppermute | solution.py:32
  21.5 0.5 %collective-permute-start.11 = (bf16[512,128]{1,0:T(8,128)(2,1)S(1)}, bf16[512,128]{1,0:T(8,128)(2,1)S(1)}, u32[]{:S(2)}, u32[]{:S(2)}) collective-permute-start(bf16[512,128]{1,0:T(8,128)(2,1)S(1)} %get-tuple-element.37), channel_id=1, source_target_pairs={{0,8},{1,17},{2,10},{3,19},{4,12},{5,21},{6,14},{7,23},{8,0},{9,25... | collective-permute-start | bytes 393224 | tf_op jit(solution)/shard_map/ppermute | solution.py:32
  22.1 0.7 %collective-permute-start.9 = (bf16[512,128]{1,0:T(8,128)(2,1)S(1)}, bf16[512,128]{1,0:T(8,128)(2,1)S(1)}, u32[]{:S(2)}, u32[]{:S(2)}) collective-permute-start(bf16[512,128]{1,0:T(8,128)(2,1)S(1)} %get-tuple-element.35), channel_id=1, source_target_pairs={{0,16},{1,9},{2,18},{3,11},{4,20},{5,13},{6,22},{7,15},{8,24},{9,1... | collective-permute-start | bytes 393224 | tf_op jit(solution)/shard_map/ppermute | solution.py:32
  22.8 0.0 collective-permute-done.8
  22.8 1.9 %scores.1 = bf16[1,1,64,128,128]{4,3,2,1,0:T(8,128)(2,1)} custom-call(s32[321]{0:T(512)S(4)} %places.1.refs_0_, bf16[32,128,128]{2,1,0:T(8,128)(2,1)S(1)} %get-tuple-element.27.panel, bf16[512,128]{1,0:T(8,128)(2,1)S(1)} %collective-permute-done.6.last, bf16[64,128,128]{2,1,0:T(8,128)(2,1)S(1)} %get-tuple-element.30.keep, ...), custom_call_target="tpu_custom_call" | custom-call | flops 268435456 | bytes 4194304 | tf_op jit(solution)/shard_map/scores/pallas_call | solution.py:270
  24.7 1.2 %collective-permute-done.10 = bf16[512,128]{1,0:T(8,128)(2,1)S(1)} collective-permute-done((bf16[512,128]{1,0:T(8,128)(2,1)S(1)}, bf16[512,128]{1,0:T(8,128)(2,1)S(1)}, u32[]{:S(2)}, u32[]{:S(2)}) %collective-permute-start.10) | collective-permute-done | bytes 131104 | tf_op jit(solution)/shard_map/ppermute | solution.py:32
  26.0 2.5 %collective-permute-done.11 = bf16[512,128]{1,0:T(8,128)(2,1)S(1)} collective-permute-done((bf16[512,128]{1,0:T(8,128)(2,1)S(1)}, bf16[512,128]{1,0:T(8,128)(2,1)S(1)}, u32[]{:S(2)}, u32[]{:S(2)}) %collective-permute-start.11) | collective-permute-done | bytes 131104 | tf_op jit(solution)/shard_map/ppermute | solution.py:32
  28.4 0.1 collective-permute-done.9
  28.5 0.7 %add_convert_fusion = bf16[512,128]{1,0:T(8,128)(2,1)} fusion(bf16[512,128]{1,0:T(8,128)(2,1)S(1)} %collective-permute-done.11, bf16[512,128]{1,0:T(8,128)(2,1)S(1)} %collective-permute-done.10, f32[512,128]{1,0:T(8,128)S(1)} %get-tuple-element.34, bf16[512,128]{1,0:T(8,128)(2,1)S(1)} %collective-permute-done.9), kind=kLoop, calls=%fused_computation.2 | loop fusion | flops 458752 | bytes 786432 | tf_op jit(solution)/shard_map/convert_element_type | solution.py:288
  (3 shorter events, 0.1 us)
Async XLA Ops:
  1.8 10.5 %collective-permute-start = (bf16[512,128]{1,0:T(8,128)(2,1)S(1)}, bf16[512,128]{1,0:T(8,128)(2,1)S(1)}, u32[]{:S(2)}, u32[]{:S(2)}) collective-permute-start(bf16[512,128]{1,0:T(8,128)(2,1)S(1)} %hidden.1.refs_2_), channel_id=1, source_target_pairs={{0,4},{1,5},{2,6},{3,7},{4,0},{5,1},{6,2},{7,3},{8,12},{9,13},{10,... | collective-permute-start | bytes 393224 | tf_op jit(solution)/shard_map/ppermute | solution.py:26
  5.9 7.1 %collective-permute-start.7 = (bf16[512,128]{1,0:T(8,128)(2,1)}, bf16[512,128]{1,0:T(8,128)(2,1)S(1)}, u32[]{:S(2)}, u32[]{:S(2)}) collective-permute-start(bf16[512,128]{1,0:T(8,128)(2,1)} %param.6), channel_id=1, source_target_pairs={{0,8},{1,17},{2,10},{3,19},{4,12},{5,21},{6,14},{7,23},{8,0},{9,25... | collective-permute-start | bytes 393224 | tf_op jit(solution)/shard_map/ppermute | solution.py:32
  7.4 7.7 %collective-permute-start.2 = (bf16[512,128]{1,0:T(8,128)(2,1)S(1)}, bf16[512,128]{1,0:T(8,128)(2,1)S(1)}, u32[]{:S(2)}, u32[]{:S(2)}) collective-permute-start(bf16[512,128]{1,0:T(8,128)(2,1)S(1)} %hidden.1.refs_2_), channel_id=1, source_target_pairs={{0,2},{1,3},{2,0},{3,1},{4,6},{5,7},{6,4},{7,5},{8,10},{9,11},{10,... | collective-permute-start | bytes 393224 | tf_op jit(solution)/shard_map/ppermute | solution.py:26
  9.0 4.0 %copy-start = (bf16[512,128]{1,0:T(8,128)(2,1)S(1)}, bf16[512,128]{1,0:T(8,128)(2,1)}, u32[]{:S(2)}) copy-start(bf16[512,128]{1,0:T(8,128)(2,1)} %param.6) | copy-start | bytes 393220
  12.3 5.0 %collective-permute-start.5 = (bf16[512,128]{1,0:T(8,128)(2,1)S(1)}, bf16[512,128]{1,0:T(8,128)(2,1)S(1)}, u32[]{:S(2)}, u32[]{:S(2)}) collective-permute-start(bf16[512,128]{1,0:T(8,128)(2,1)S(1)} %collective-permute-done.refs_6_), channel_id=1, source_target_pairs={{0,2},{1,3},{2,0},{3,1},{4,6},{5,7},{6,4},{7,5},{8,10},{9,11},{10,... | collective-permute-start | bytes 393224 | tf_op jit(solution)/shard_map/ppermute | solution.py:26
  13.0 9.7 %collective-permute-start.8 = (bf16[1024,128]{1,0:T(8,128)(2,1)S(1)}, bf16[1024,128]{1,0:T(8,128)(2,1)S(1)}, u32[]{:S(2)}, u32[]{:S(2)}) collective-permute-start(bf16[1024,128]{1,0:T(8,128)(2,1)S(1)} %pad_maximum_fusion.1), channel_id=1, source_target_pairs={{0,16},{1,9},{2,18},{3,11},{4,20},{5,13},{6,22},{7,15},{8,24},{9,1... | collective-permute-start | bytes 786440 | tf_op jit(solution)/shard_map/ppermute | solution.py:32
  14.6 2.7 %collective-permute-start.4 = (bf16[512,128]{1,0:T(8,128)(2,1)S(1)}, bf16[512,128]{1,0:T(8,128)(2,1)S(1)}, u32[]{:S(2)}, u32[]{:S(2)}) collective-permute-start(bf16[512,128]{1,0:T(8,128)(2,1)S(1)} %collective-permute-done.refs_6_), channel_id=1, source_target_pairs={{0,1},{1,0},{2,3},{3,2},{4,5},{5,4},{6,7},{7,6},{8,9},{9,8},{10,11... | collective-permute-start | bytes 393224 | tf_op jit(solution)/shard_map/ppermute | solution.py:26
  14.6 2.7 %collective-permute-start.1 = (bf16[512,128]{1,0:T(8,128)(2,1)S(1)}, bf16[512,128]{1,0:T(8,128)(2,1)S(1)}, u32[]{:S(2)}, u32[]{:S(2)}) collective-permute-start(bf16[512,128]{1,0:T(8,128)(2,1)S(1)} %hidden.1.refs_2_), channel_id=1, source_target_pairs={{0,1},{1,0},{2,3},{3,2},{4,5},{5,4},{6,7},{7,6},{8,9},{9,8},{10,11... | collective-permute-start | bytes 393224 | tf_op jit(solution)/shard_map/ppermute | solution.py:26
  15.1 2.2 %collective-permute-start.3 = (bf16[512,128]{1,0:T(8,128)(2,1)S(1)}, bf16[512,128]{1,0:T(8,128)(2,1)S(1)}, u32[]{:S(2)}, u32[]{:S(2)}) collective-permute-start(bf16[512,128]{1,0:T(8,128)(2,1)S(1)} %collective-permute-done.2.refs_4_), channel_id=1, source_target_pairs={{0,1},{1,0},{2,3},{3,2},{4,5},{5,4},{6,7},{7,6},{8,9},{9,8},{10,11... | collective-permute-start | bytes 393224 | tf_op jit(solution)/shard_map/ppermute | solution.py:26
  17.3 1.3 %collective-permute-start.6 = (bf16[512,128]{1,0:T(8,128)(2,1)S(1)}, bf16[512,128]{1,0:T(8,128)(2,1)S(1)}, u32[]{:S(2)}, u32[]{:S(2)}) collective-permute-start(bf16[512,128]{1,0:T(8,128)(2,1)S(1)} %collective-permute-done.5.refs_8_), channel_id=1, source_target_pairs={{0,1},{1,0},{2,3},{3,2},{4,5},{5,4},{6,7},{7,6},{8,9},{9,8},{10,11... | collective-permute-start | bytes 393224 | tf_op jit(solution)/shard_map/ppermute | solution.py:26
  19.2 6.8 %collective-permute-start.10 = (bf16[512,128]{1,0:T(8,128)(2,1)S(1)}, bf16[512,128]{1,0:T(8,128)(2,1)S(1)}, u32[]{:S(2)}, u32[]{:S(2)}) collective-permute-start(bf16[512,128]{1,0:T(8,128)(2,1)S(1)} %get-tuple-element.36), channel_id=1, source_target_pairs={{0,24},{1,25},{2,26},{3,27},{4,28},{5,29},{6,30},{7,31},{8,16},{9,... | collective-permute-start | bytes 393224 | tf_op jit(solution)/shard_map/ppermute | solution.py:32
  21.5 6.9 %collective-permute-start.11 = (bf16[512,128]{1,0:T(8,128)(2,1)S(1)}, bf16[512,128]{1,0:T(8,128)(2,1)S(1)}, u32[]{:S(2)}, u32[]{:S(2)}) collective-permute-start(bf16[512,128]{1,0:T(8,128)(2,1)S(1)} %get-tuple-element.37), channel_id=1, source_target_pairs={{0,8},{1,17},{2,10},{3,19},{4,12},{5,21},{6,14},{7,23},{8,0},{9,25... | collective-permute-start | bytes 393224 | tf_op jit(solution)/shard_map/ppermute | solution.py:32
  22.1 6.5 %collective-permute-start.9 = (bf16[512,128]{1,0:T(8,128)(2,1)S(1)}, bf16[512,128]{1,0:T(8,128)(2,1)S(1)}, u32[]{:S(2)}, u32[]{:S(2)}) collective-permute-start(bf16[512,128]{1,0:T(8,128)(2,1)S(1)} %get-tuple-element.35), channel_id=1, source_target_pairs={{0,16},{1,9},{2,18},{3,11},{4,20},{5,13},{6,22},{7,15},{8,24},{9,1... | collective-permute-start | bytes 393224 | tf_op jit(solution)/shard_map/ppermute | solution.py:32

commit v9 on v8

--- a/solution.py
+++ b/solution.py
@@ -252,11 +252,11 @@
     else:
         pairs = [(s, s) for s in sorted(range(1, n_row), key=lambda s: -s.bit_count())]
     pairs = pairs[-1:] + pairs[:-1]
-    _, own, *parts = pl.pallas_call(
-        functools.partial(rest_kernel, per, [(0, 0)] + pairs),
+    total, *parts = pl.pallas_call(
+        functools.partial(rest_kernel, per, pairs),
         in_specs=[scalars] + [whole] * 3,
-        out_specs=[whole] * (1 + n_row),
-        out_shape=[VMEM(total_shape, jnp.float32), VMEM((nodes, fin), jnp.float32)]
+        out_specs=[whole] * n_row,
+        out_shape=[VMEM(total_shape, jnp.float32)]
         + [VMEM((nodes, fin), jnp.bfloat16)] * (n_row - 1),
         scratch_shapes=[VMEM((per + 1, BLOCK, fin), jnp.bfloat16)],
         input_output_aliases={2: 0},
@@ -283,6 +283,7 @@
         name="scores",
     )(places, *map(in_vmem, (panel, last, keep, cols)))
 
+    own = total[:per].reshape(nodes, fin)
     for part in got:
         own = own + part.astype(jnp.float32)
     return edge_grad, own.astype(jnp.bfloat16)

time: 29.4 us -> 29.4 us (level)
  transfers between devices with their start and end apart: 12 -> 12, of which waited for: 6 -> 5; matrix products, arithmetic and copies ran while one was open for 0% -> 0% of each run, Pallas kernels for 22% -> 22%
where the time goes in v9:
time: 29.4 us; the launch traced here: 29.1 us
  starting transfers between devices  13.5 us (46%)
  Pallas kernels  7.64 us (26%)
  waiting for transfers between devices  6.51 us (22%)
  other arithmetic  0.77 us (3%)
  between operations  0.71 us (2%)
    ppermute x7, starting transfers between devices, swap(): return lax.ppermute(x, axis, [(i, i ^ mask) for i in range(size)])  6.87 us
    ppermute x5, starting transfers between devices, swap_rows(): return lax.ppermute(x, ('row', 'col'), pairs)  6.63 us
    ppermute x5, waiting for transfers between devices, swap_rows(): return lax.ppermute(x, ('row', 'col'), pairs)  3.69 us
    pallas_call x1, Pallas kernels, local(): pl.pallas_call(prep_kernel, in_specs=[far, far, far], out_specs=[whole, w...  3.09 us
    ppermute x7, waiting for transfers between devices, swap(): return lax.ppermute(x, axis, [(i, i ^ mask) for i in range(size)])  2.83 us
    pallas_call x1, Pallas kernels, local(): pl.pallas_call(functools.partial(scores_kernel, per), in_specs=[scalars]...  1.93 us
    pallas_call x1, Pallas kernels, local(): pl.pallas_call(hidden_kernel, in_specs=[far, far], out_specs=whole, out_s...  1.19 us
    pallas_call x1, Pallas kernels, local(): pl.pallas_call(functools.partial(sums_kernel, per), in_specs=[scalars] +...  0.92 us
  transfers between devices with their start and end apart: 12, of which 5 were waited for; matrix products, arithmetic and copies ran while one was open for 0% of the time, Pallas kernels for 22%

profile of v9, /device:TPU:0, one launch (start us, length us, event | category | flops | bytes accessed | tf_op | source)
XLA Modules:
  0.0 29.1 jit_solution(18112492244113699313)
XLA Ops:
  0.6 1.2 %hidden.1.refs_2_ = bf16[512,128]{1,0:T(8,128)(2,1)S(1)} custom-call(bf16[512,256]{1,0:T(8,128)(2,1)} %grads.1, bf16[128,256]{1,0:T(8,128)(2,1)} %weight.1), custom_call_target="tpu_custom_call" | custom-call | tf_op jit(solution)/shard_map/hidden/pallas_call | solution.py:177
  1.8 4.1 %collective-permute-start = (bf16[512,128]{1,0:T(8,128)(2,1)S(1)}, bf16[512,128]{1,0:T(8,128)(2,1)S(1)}, u32[]{:S(2)}, u32[]{:S(2)}) collective-permute-start(bf16[512,128]{1,0:T(8,128)(2,1)S(1)} %hidden.1.refs_2_), channel_id=1, source_target_pairs={{0,4},{1,5},{2,6},{3,7},{4,0},{5,1},{6,2},{7,3},{8,12},{9,13},{10,... | collective-permute-start | bytes 393224 | tf_op jit(solution)/shard_map/ppermute | solution.py:26
  5.9 1.5 %collective-permute-start.7 = (bf16[512,128]{1,0:T(8,128)(2,1)}, bf16[512,128]{1,0:T(8,128)(2,1)S(1)}, u32[]{:S(2)}, u32[]{:S(2)}) collective-permute-start(bf16[512,128]{1,0:T(8,128)(2,1)} %param.6), channel_id=1, source_target_pairs={{0,8},{1,17},{2,10},{3,19},{4,12},{5,21},{6,14},{7,23},{8,0},{9,25... | collective-permute-start | bytes 393224 | tf_op jit(solution)/shard_map/ppermute | solution.py:32
  7.4 1.6 %collective-permute-start.2 = (bf16[512,128]{1,0:T(8,128)(2,1)S(1)}, bf16[512,128]{1,0:T(8,128)(2,1)S(1)}, u32[]{:S(2)}, u32[]{:S(2)}) collective-permute-start(bf16[512,128]{1,0:T(8,128)(2,1)S(1)} %hidden.1.refs_2_), channel_id=1, source_target_pairs={{0,2},{1,3},{2,0},{3,1},{4,6},{5,7},{6,4},{7,5},{8,10},{9,11},{10,... | collective-permute-start | bytes 393224 | tf_op jit(solution)/shard_map/ppermute | solution.py:26
  9.0 0.0 copy-start
  9.0 3.1 %prep.1 = (bf16[64,128,128]{2,1,0:T(8,128)(2,1)S(1)}, bf16[64,128,128]{2,1,0:T(8,128)(2,1)S(1)}, s32[1,3,1,64]{3,2,1,0:T(1,128)S(4)}) custom-call(s32[1,3,1,64]{3,2,1,0:T(1,128)} %bitcast.9, s32[1,1,64,128,128]{4,3,2,1,0:T(8,128)} %mask.1, bf16[1,1,64,128,128]{4,3,2,1,0:T(8,128)(2,1)} %weights.1), custom_call_target="tpu_custom_call" | custom-call | bytes 4096 | tf_op jit(solution)/shard_map/prep/pallas_call | solution.py:201
  12.1 0.2 collective-permute-done.refs_6_
  12.3 0.7 %collective-permute-start.5 = (bf16[512,128]{1,0:T(8,128)(2,1)S(1)}, bf16[512,128]{1,0:T(8,128)(2,1)S(1)}, u32[]{:S(2)}, u32[]{:S(2)}) collective-permute-start(bf16[512,128]{1,0:T(8,128)(2,1)S(1)} %collective-permute-done.refs_6_), channel_id=1, source_target_pairs={{0,2},{1,3},{2,0},{3,1},{4,6},{5,7},{6,4},{7,5},{8,10},{9,11},{10,... | collective-permute-start | bytes 393224 | tf_op jit(solution)/shard_map/ppermute | solution.py:26
  13.0 0.0 collective-permute-done.7
  13.0 0.0 copy-done
  13.0 1.6 %collective-permute-start.8 = (bf16[1024,128]{1,0:T(8,128)(2,1)S(1)}, bf16[1024,128]{1,0:T(8,128)(2,1)S(1)}, u32[]{:S(2)}, u32[]{:S(2)}) collective-permute-start(bf16[1024,128]{1,0:T(8,128)(2,1)S(1)} %pad_maximum_fusion.1), channel_id=1, source_target_pairs={{0,16},{1,9},{2,18},{3,11},{4,20},{5,13},{6,22},{7,15},{8,24},{9,1... | collective-permute-start | bytes 786440 | tf_op jit(solution)/shard_map/ppermute | solution.py:32
  14.6 0.0 collective-permute-start.4
  14.6 0.5 %collective-permute-start.1 = (bf16[512,128]{1,0:T(8,128)(2,1)S(1)}, bf16[512,128]{1,0:T(8,128)(2,1)S(1)}, u32[]{:S(2)}, u32[]{:S(2)}) collective-permute-start(bf16[512,128]{1,0:T(8,128)(2,1)S(1)} %hidden.1.refs_2_), channel_id=1, source_target_pairs={{0,1},{1,0},{2,3},{3,2},{4,5},{5,4},{6,7},{7,6},{8,9},{9,8},{10,11... | collective-permute-start | bytes 393224 | tf_op jit(solution)/shard_map/ppermute | solution.py:26
  15.1 0.0 collective-permute-done.2.refs_4_
  15.1 0.0 collective-permute-start.3
  15.1 2.2 %collective-permute-done.5.refs_8_ = bf16[512,128]{1,0:T(8,128)(2,1)S(1)} collective-permute-done((bf16[512,128]{1,0:T(8,128)(2,1)S(1)}, bf16[512,128]{1,0:T(8,128)(2,1)S(1)}, u32[]{:S(2)}, u32[]{:S(2)}) %collective-permute-start.5) | collective-permute-done | bytes 131104 | tf_op jit(solution)/shard_map/ppermute | solution.py:26
  17.3 0.0 collective-permute-start.6
  17.3 0.0 collective-permute-done.4.refs_7_
  17.3 0.0 collective-permute-done.1.refs_3_
  17.3 0.0 collective-permute-done.3.refs_5_
  17.3 0.9 %sums.1 = (bf16[32,128,128]{2,1,0:T(8,128)(2,1)S(1)}, f32[16,128,128]{2,1,0:T(8,128)S(1)}) custom-call(s32[321]{0:T(512)S(4)} %places.1.refs_0_, bf16[64,128,128]{2,1,0:T(8,128)(2,1)S(1)} %get-tuple-element.24.refs_1_.adj, bf16[512,128]{1,0:T(8,128)(2,1)S(1)} %hidden.1.refs_2_, bf16[512,128]{1,0:T(8,128)(2,1)S(1)} %collective-permute-done.1.refs_3_, ...), custom_call_target="tpu_custom_call" | custom-call | flops 268435456 | bytes 1048576 | tf_op jit(solution)/shard_map/sums/pallas_call | solution.py:241
  18.3 0.4 %collective-permute-done.6.last = bf16[512,128]{1,0:T(8,128)(2,1)S(1)} collective-permute-done((bf16[512,128]{1,0:T(8,128)(2,1)S(1)}, bf16[512,128]{1,0:T(8,128)(2,1)S(1)}, u32[]{:S(2)}, u32[]{:S(2)}) %collective-permute-start.6) | collective-permute-done | bytes 131104 | tf_op jit(solution)/shard_map/ppermute | solution.py:26
  18.7 0.5 %rest.1 = (f32[16,128,128]{2,1,0:T(8,128)S(1)}, bf16[512,128]{1,0:T(8,128)(2,1)S(1)}, bf16[512,128]{1,0:T(8,128)(2,1)S(1)}, bf16[512,128]{1,0:T(8,128)(2,1)S(1)}) custom-call(s32[321]{0:T(512)S(4)} %places.1.refs_0_, bf16[64,128,128]{2,1,0:T(8,128)(2,1)S(1)} %get-tuple-element.24.refs_1_.adj, ...), custom_call_target="tpu_custom_call", output_to_operand_aliasing={{0}: (2, {})} | custom-call | bytes 4096 | tf_op jit(solution)/shard_map/rest/pallas_call | solution.py:255
  19.2 2.6 %collective-permute-start.10 = (bf16[512,128]{1,0:T(8,128)(2,1)S(1)}, bf16[512,128]{1,0:T(8,128)(2,1)S(1)}, u32[]{:S(2)}, u32[]{:S(2)}) collective-permute-start(bf16[512,128]{1,0:T(8,128)(2,1)S(1)} %get-tuple-element.36), channel_id=1, source_target_pairs={{0,24},{1,25},{2,26},{3,27},{4,28},{5,29},{6,30},{7,31},{8,16},{9,... | collective-permute-start | bytes 393224 | tf_op jit(solution)/shard_map/ppermute | solution.py:32
  21.7 0.3 %collective-permute-start.11 = (bf16[512,128]{1,0:T(8,128)(2,1)S(1)}, bf16[512,128]{1,0:T(8,128)(2,1)S(1)}, u32[]{:S(2)}, u32[]{:S(2)}) collective-permute-start(bf16[512,128]{1,0:T(8,128)(2,1)S(1)} %get-tuple-element.37), channel_id=1, source_target_pairs={{0,8},{1,17},{2,10},{3,19},{4,12},{5,21},{6,14},{7,23},{8,0},{9,25... | collective-permute-start | bytes 393224 | tf_op jit(solution)/shard_map/ppermute | solution.py:32
  22.1 0.7 %collective-permute-start.9 = (bf16[512,128]{1,0:T(8,128)(2,1)S(1)}, bf16[512,128]{1,0:T(8,128)(2,1)S(1)}, u32[]{:S(2)}, u32[]{:S(2)}) collective-permute-start(bf16[512,128]{1,0:T(8,128)(2,1)S(1)} %get-tuple-element.35), channel_id=1, source_target_pairs={{0,16},{1,9},{2,18},{3,11},{4,20},{5,13},{6,22},{7,15},{8,24},{9,1... | collective-permute-start | bytes 393224 | tf_op jit(solution)/shard_map/ppermute | solution.py:32
  22.7 0.0 collective-permute-done.8
  22.8 1.9 %scores.1 = bf16[1,1,64,128,128]{4,3,2,1,0:T(8,128)(2,1)} custom-call(s32[321]{0:T(512)S(4)} %places.1.refs_0_, bf16[32,128,128]{2,1,0:T(8,128)(2,1)S(1)} %get-tuple-element.27.panel, bf16[512,128]{1,0:T(8,128)(2,1)S(1)} %collective-permute-done.6.last, bf16[64,128,128]{2,1,0:T(8,128)(2,1)S(1)} %get-tuple-element.30.keep, ...), custom_call_target="tpu_custom_call" | custom-call | flops 268435456 | bytes 4194304 | tf_op jit(solution)/shard_map/scores/pallas_call | solution.py:270
  24.7 1.0 %collective-permute-done.10 = bf16[512,128]{1,0:T(8,128)(2,1)S(1)} collective-permute-done((bf16[512,128]{1,0:T(8,128)(2,1)S(1)}, bf16[512,128]{1,0:T(8,128)(2,1)S(1)}, u32[]{:S(2)}, u32[]{:S(2)}) %collective-permute-start.10) | collective-permute-done | bytes 131104 | tf_op jit(solution)/shard_map/ppermute | solution.py:32
  25.7 2.7 %collective-permute-done.11 = bf16[512,128]{1,0:T(8,128)(2,1)S(1)} collective-permute-done((bf16[512,128]{1,0:T(8,128)(2,1)S(1)}, bf16[512,128]{1,0:T(8,128)(2,1)S(1)}, u32[]{:S(2)}, u32[]{:S(2)}) %collective-permute-start.11) | collective-permute-done | bytes 131104 | tf_op jit(solution)/shard_map/ppermute | solution.py:32
  28.4 0.0 collective-permute-done.9
  28.4 0.7 %fusion.2 = bf16[512,128]{1,0:T(8,128)(2,1)} fusion(f32[4,128,128]{2,1,0:T(8,128)S(1)} %slice.3, bf16[512,128]{1,0:T(8,128)(2,1)S(1)} %collective-permute-done.11, bf16[512,128]{1,0:T(8,128)(2,1)S(1)} %collective-permute-done.10, bf16[512,128]{1,0:T(8,128)(2,1)S(1)} %collective-permute-done.9), kind=kLoop, calls=%fused_computation.5 | loop fusion | flops 458752 | bytes 786432 | tf_op jit(solution)/shard_map/convert_element_type | solution.py:289
  (4 shorter events, 0.1 us)
Async XLA Ops:
  1.8 10.5 %collective-permute-start = (bf16[512,128]{1,0:T(8,128)(2,1)S(1)}, bf16[512,128]{1,0:T(8,128)(2,1)S(1)}, u32[]{:S(2)}, u32[]{:S(2)}) collective-permute-start(bf16[512,128]{1,0:T(8,128)(2,1)S(1)} %hidden.1.refs_2_), channel_id=1, source_target_pairs={{0,4},{1,5},{2,6},{3,7},{4,0},{5,1},{6,2},{7,3},{8,12},{9,13},{10,... | collective-permute-start | bytes 393224 | tf_op jit(solution)/shard_map/ppermute | solution.py:26
  5.9 7.1 %collective-permute-start.7 = (bf16[512,128]{1,0:T(8,128)(2,1)}, bf16[512,128]{1,0:T(8,128)(2,1)S(1)}, u32[]{:S(2)}, u32[]{:S(2)}) collective-permute-start(bf16[512,128]{1,0:T(8,128)(2,1)} %param.6), channel_id=1, source_target_pairs={{0,8},{1,17},{2,10},{3,19},{4,12},{5,21},{6,14},{7,23},{8,0},{9,25... | collective-permute-start | bytes 393224 | tf_op jit(solution)/shard_map/ppermute | solution.py:32
  7.4 7.7 %collective-permute-start.2 = (bf16[512,128]{1,0:T(8,128)(2,1)S(1)}, bf16[512,128]{1,0:T(8,128)(2,1)S(1)}, u32[]{:S(2)}, u32[]{:S(2)}) collective-permute-start(bf16[512,128]{1,0:T(8,128)(2,1)S(1)} %hidden.1.refs_2_), channel_id=1, source_target_pairs={{0,2},{1,3},{2,0},{3,1},{4,6},{5,7},{6,4},{7,5},{8,10},{9,11},{10,... | collective-permute-start | bytes 393224 | tf_op jit(solution)/shard_map/ppermute | solution.py:26
  9.0 4.0 %copy-start = (bf16[512,128]{1,0:T(8,128)(2,1)S(1)}, bf16[512,128]{1,0:T(8,128)(2,1)}, u32[]{:S(2)}) copy-start(bf16[512,128]{1,0:T(8,128)(2,1)} %param.6) | copy-start | bytes 393220
  12.3 5.0 %collective-permute-start.5 = (bf16[512,128]{1,0:T(8,128)(2,1)S(1)}, bf16[512,128]{1,0:T(8,128)(2,1)S(1)}, u32[]{:S(2)}, u32[]{:S(2)}) collective-permute-start(bf16[512,128]{1,0:T(8,128)(2,1)S(1)} %collective-permute-done.refs_6_), channel_id=1, source_target_pairs={{0,2},{1,3},{2,0},{3,1},{4,6},{5,7},{6,4},{7,5},{8,10},{9,11},{10,... | collective-permute-start | bytes 393224 | tf_op jit(solution)/shard_map/ppermute | solution.py:26
  13.0 9.7 %collective-permute-start.8 = (bf16[1024,128]{1,0:T(8,128)(2,1)S(1)}, bf16[1024,128]{1,0:T(8,128)(2,1)S(1)}, u32[]{:S(2)}, u32[]{:S(2)}) collective-permute-start(bf16[1024,128]{1,0:T(8,128)(2,1)S(1)} %pad_maximum_fusion.1), channel_id=1, source_target_pairs={{0,16},{1,9},{2,18},{3,11},{4,20},{5,13},{6,22},{7,15},{8,24},{9,1... | collective-permute-start | bytes 786440 | tf_op jit(solution)/shard_map/ppermute | solution.py:32
  14.6 2.7 %collective-permute-start.4 = (bf16[512,128]{1,0:T(8,128)(2,1)S(1)}, bf16[512,128]{1,0:T(8,128)(2,1)S(1)}, u32[]{:S(2)}, u32[]{:S(2)}) collective-permute-start(bf16[512,128]{1,0:T(8,128)(2,1)S(1)} %collective-permute-done.refs_6_), channel_id=1, source_target_pairs={{0,1},{1,0},{2,3},{3,2},{4,5},{5,4},{6,7},{7,6},{8,9},{9,8},{10,11... | collective-permute-start | bytes 393224 | tf_op jit(solution)/shard_map/ppermute | solution.py:26
  14.6 2.7 %collective-permute-start.1 = (bf16[512,128]{1,0:T(8,128)(2,1)S(1)}, bf16[512,128]{1,0:T(8,128)(2,1)S(1)}, u32[]{:S(2)}, u32[]{:S(2)}) collective-permute-start(bf16[512,128]{1,0:T(8,128)(2,1)S(1)} %hidden.1.refs_2_), channel_id=1, source_target_pairs={{0,1},{1,0},{2,3},{3,2},{4,5},{5,4},{6,7},{7,6},{8,9},{9,8},{10,11... | collective-permute-start | bytes 393224 | tf_op jit(solution)/shard_map/ppermute | solution.py:26
  15.1 2.2 %collective-permute-start.3 = (bf16[512,128]{1,0:T(8,128)(2,1)S(1)}, bf16[512,128]{1,0:T(8,128)(2,1)S(1)}, u32[]{:S(2)}, u32[]{:S(2)}) collective-permute-start(bf16[512,128]{1,0:T(8,128)(2,1)S(1)} %collective-permute-done.2.refs_4_), channel_id=1, source_target_pairs={{0,1},{1,0},{2,3},{3,2},{4,5},{5,4},{6,7},{7,6},{8,9},{9,8},{10,11... | collective-permute-start | bytes 393224 | tf_op jit(solution)/shard_map/ppermute | solution.py:26
  17.3 1.3 %collective-permute-start.6 = (bf16[512,128]{1,0:T(8,128)(2,1)S(1)}, bf16[512,128]{1,0:T(8,128)(2,1)S(1)}, u32[]{:S(2)}, u32[]{:S(2)}) collective-permute-start(bf16[512,128]{1,0:T(8,128)(2,1)S(1)} %collective-permute-done.5.refs_8_), channel_id=1, source_target_pairs={{0,1},{1,0},{2,3},{3,2},{4,5},{5,4},{6,7},{7,6},{8,9},{9,8},{10,11... | collective-permute-start | bytes 393224 | tf_op jit(solution)/shard_map/ppermute | solution.py:26
  19.2 6.5 %collective-permute-start.10 = (bf16[512,128]{1,0:T(8,128)(2,1)S(1)}, bf16[512,128]{1,0:T(8,128)(2,1)S(1)}, u32[]{:S(2)}, u32[]{:S(2)}) collective-permute-start(bf16[512,128]{1,0:T(8,128)(2,1)S(1)} %get-tuple-element.36), channel_id=1, source_target_pairs={{0,24},{1,25},{2,26},{3,27},{4,28},{5,29},{6,30},{7,31},{8,16},{9,... | collective-permute-start | bytes 393224 | tf_op jit(solution)/shard_map/ppermute | solution.py:32
  21.7 6.7 %collective-permute-start.11 = (bf16[512,128]{1,0:T(8,128)(2,1)S(1)}, bf16[512,128]{1,0:T(8,128)(2,1)S(1)}, u32[]{:S(2)}, u32[]{:S(2)}) collective-permute-start(bf16[512,128]{1,0:T(8,128)(2,1)S(1)} %get-tuple-element.37), channel_id=1, source_target_pairs={{0,8},{1,17},{2,10},{3,19},{4,12},{5,21},{6,14},{7,23},{8,0},{9,25... | collective-permute-start | bytes 393224 | tf_op jit(solution)/shard_map/ppermute | solution.py:32
  22.1 6.4 %collective-permute-start.9 = (bf16[512,128]{1,0:T(8,128)(2,1)S(1)}, bf16[512,128]{1,0:T(8,128)(2,1)S(1)}, u32[]{:S(2)}, u32[]{:S(2)}) collective-permute-start(bf16[512,128]{1,0:T(8,128)(2,1)S(1)} %get-tuple-element.35), channel_id=1, source_target_pairs={{0,16},{1,9},{2,18},{3,11},{4,20},{5,13},{6,22},{7,15},{8,24},{9,1... | collective-permute-start | bytes 393224 | tf_op jit(solution)/shard_map/ppermute | solution.py:32
